TPU v7x, 512 devices: a whole 4x4x16 slice. The times are simulated.
512 devices in a mesh: dp: 4 (over y), ctx: 64 (over x, z), mp: 2 (over core).
Axes of the slice: x: 4, y: 4, z: 16, core: 2. Of those that a mesh axis runs over, the one named last changes fastest.
Arguments:
- features: bfloat16 [4, 8192, 3, 4096], P('dp', 'ctx', None, 'mp'), may hold values from -6 to 6
- conv_weight: float32 [7, 3, 4096], P(None, None, 'mp'), may hold values from -2 to 2
- log_rate: float32 [8, 32], P(None, 'mp'), as said below
- residues: float32 [8, 4096], P(None, 'mp'), may hold values from -4 to 4
- skip_weight: float32 [4096], P('mp'), may hold values from 0.5 to 1.5
- norm_gain: float32 [4096], P('mp'), may hold values from 0.5 to 1.5
- cotangent: bfloat16 [4, 8192, 4096], P('dp', 'ctx', 'mp'), may hold values from -6 to 6
Outputs:
- block_out: bfloat16 [4, 8192, 4096], P('dp', 'ctx', 'mp')
- feature_grad: bfloat16 [4, 8192, 3, 4096], P('dp', 'ctx', None, 'mp')
- conv_grad: float32 [7, 3, 4096], P(None, None, 'mp')
- rate_grad: float32 [8, 32], P(None, 'mp')
- residue_grad: float32 [8, 4096], P(None, 'mp')
- skip_grad: float32 [4096], P('mp')
- gain_grad: float32 [4096], P('mp')
Inputs may be any that keep to these rules, and one draw needn't show every extreme that they name: log_rate lies between ln(1 / 1048576) and ln(1 / 16).
All inputs are finite; a program needn't handle non-finite values.
Results may differ from a plain program's by a relative error of at most 0.0011.
Values may be sent and summed in bfloat16 or wider, within the bound.
No kernel may reach another device: no remote copies, remote signals or barrier semaphores. Data moves between devices by JAX's collectives and lax.ppermute only.
A program may use at most 128 MiB of HBM per device.

v0:
```python
import jax
import jax.numpy as jnp
from jax import lax
from jax.sharding import PartitionSpec as P

D = 4096


EPSILON = 1e-06
HIGHEST = lax.Precision.HIGHEST


def passed_along(value, axis, steps):
    count = lax.axis_size(axis)
    leading, last = (max(0, -steps), min(count, count - steps))
    return lax.ppermute(value, axis, [(source, source + steps) for source in range(leading, last)])


def carried_in(part, axis, combine, identity, reverse):
    count = lax.axis_size(axis)
    place = lax.axis_index(axis)
    ahead = count - 1 - place if reverse else place
    gathered = jax.tree.map(lambda a: lax.all_gather(a, axis), part)
    state = jax.tree.map(lambda a, e: jnp.zeros_like(a) + jnp.asarray(e, a.dtype), part, identity)

    def one(lap, state):
        source = count - 1 - lap if reverse else lap
        return combine(
            state, jax.tree.map(lambda a: lax.dynamic_index_in_dim(a, source, 0, False), gathered)
        )

    return lax.fori_loop(0, ahead, one, state)


def decay_matrix(rate_row, length):
    places = jnp.arange(length, dtype=jnp.float32)
    lagged = places[:, None] - places[None, :]
    clipped = jnp.maximum(lagged, 0.0)
    matrix = jnp.where(lagged >= 0, jnp.exp(-rate_row[:, None, None] * clipped), 0.0)
    return (matrix, clipped)


def compose_back(earlier, later):
    return (earlier[0] * later[0], earlier[1] * later[0][..., None] + later[1])


def local(features, conv_weight, log_rate, residues, skip_weight, norm_gain, cotangent):
    local_feats = features[0]
    length = local_feats.shape[0]
    channels = local_feats.shape[2]
    pole_count = log_rate.shape[0]
    groups_here = log_rate.shape[1]
    group_size = channels // groups_here
    halo_rows = conv_weight.shape[0] - 1
    previous = passed_along(local_feats[length - halo_rows :], "ctx", 1)
    extended = jnp.concatenate([previous, local_feats], axis=0)
    filtered = conv_weight[0] * extended[halo_rows : halo_rows + length]
    for offset in range(1, halo_rows + 1):
        filtered = (
            filtered
            + conv_weight[offset] * extended[halo_rows - offset : halo_rows - offset + length]
        )
    query_rows = filtered[:, 0]
    key_rows = filtered[:, 1]
    value_rows = filtered[:, 2]
    product = key_rows * value_rows
    rate_rows = jnp.exp(log_rate).T
    grouped = product.reshape(length, groups_here, group_size).transpose(1, 0, 2)
    places = jnp.arange(length, dtype=jnp.float32)
    tail_lag = length - 1.0 - places
    block_decay = jnp.exp(-rate_rows * length)

    def forward_plain(pieces):
        rate_row, product_block = pieces
        matrix, clipped = decay_matrix(rate_row, length)
        return jnp.einsum("pts,sc->ptc", matrix, product_block, precision=HIGHEST)

    local_states = lax.map(forward_plain, (rate_rows, grouped))
    end_rows = local_states[:, :, length - 1, :]
    carried = carried_in(
        (block_decay, end_rows),
        "ctx",
        compose_back,
        (jnp.ones_like(block_decay), jnp.zeros_like(end_rows)),
        False,
    )
    state_in = carried[1]
    head_decay = jnp.exp(-rate_rows[:, :, None] * (places + 1.0))
    states = local_states + head_decay[..., None] * state_in[:, :, None, :]
    weights = residues.reshape(pole_count, groups_here, group_size).transpose(1, 0, 2)
    modal_part = jnp.einsum("gptc,gpc->tgc", states, weights, precision=HIGHEST).reshape(
        length, channels
    )
    branch = modal_part + skip_weight * product
    gated_rows = query_rows * branch
    seed_grad = cotangent[0].astype(jnp.float32)
    scaled_grad = norm_gain * seed_grad
    square_sum = lax.psum(jnp.sum(gated_rows * gated_rows, axis=1), "mp")
    inv_rms = lax.rsqrt(square_sum / D + EPSILON)[:, None]
    normed = gated_rows * inv_rms
    block_out = (norm_gain * normed).astype(jnp.bfloat16)
    slope_sum = lax.psum(jnp.sum(scaled_grad * gated_rows, axis=1), "mp")
    gain_local = jnp.sum(seed_grad * normed, axis=0)
    dgated = scaled_grad * inv_rms - gated_rows * (
        slope_sum[:, None] * inv_rms * inv_rms * inv_rms / D
    )
    dquery = dgated * branch
    dbranch = dgated * query_rows
    skip_local = jnp.sum(dbranch * product, axis=0)
    dgrouped = dbranch.reshape(length, groups_here, group_size).transpose(1, 0, 2)
    back_in = jnp.einsum("gpt,gtc->gpc", head_decay, dgrouped, precision=HIGHEST)
    returned = carried_in(
        (block_decay, back_in),
        "ctx",
        compose_back,
        (jnp.ones_like(block_decay), jnp.zeros_like(back_in)),
        True,
    )
    later_in = returned[1]

    def backward_adjoint(pieces):
        (
            rate_row,
            product_block,
            grad_block,
            state_block,
            weight_row,
            later_row,
            start_row,
            slope_row,
        ) = pieces
        matrix, clipped = decay_matrix(rate_row, length)
        residue_part = jnp.sum(grad_block[None] * state_block, axis=1)
        tail_row = jnp.exp(-rate_row[:, None] * tail_lag)
        adjoint = (
            jnp.einsum("pts,tc->psc", matrix, grad_block, precision=HIGHEST)
            + tail_row[..., None] * later_row[:, None, :]
        )
        inner = (
            jnp.sum(adjoint[:, 1:, :] * state_block[:, : length - 1, :], axis=1)
            + adjoint[:, 0, :] * start_row
        )
        rate_part = -jnp.exp(-rate_row) * jnp.sum(weight_row * inner, axis=1)
        return (residue_part, rate_part, jnp.sum(weight_row[:, None, :] * adjoint, axis=0))

    residue_parts, rate_parts, dproduct_groups = lax.map(
        backward_adjoint,
        (rate_rows, grouped, dgrouped, states, weights, later_in, state_in, state_in),
    )
    residue_local = residue_parts.transpose(1, 0, 2).reshape(pole_count, channels)
    rate_local = rate_parts.T * jnp.exp(log_rate)
    dproduct = dproduct_groups.transpose(1, 0, 2).reshape(length, channels) + dbranch * skip_weight
    dfiltered = jnp.stack([dquery, dproduct * value_rows, dproduct * key_rows], axis=1)
    zeros_rim = jnp.zeros((halo_rows, 3, channels), jnp.float32)
    padded_grad = jnp.concatenate([zeros_rim, dfiltered, zeros_rim], axis=0)
    dextended = conv_weight[0] * padded_grad[0 : length + halo_rows]
    for offset in range(1, halo_rows + 1):
        dextended = (
            dextended + conv_weight[offset] * padded_grad[offset : offset + length + halo_rows]
        )
    conv_local = jnp.stack(
        [
            jnp.sum(dfiltered * extended[halo_rows - offset : halo_rows - offset + length], axis=0)
            for offset in range(halo_rows + 1)
        ],
        axis=0,
    )
    incoming = passed_along(dextended[:halo_rows], "ctx", -1)
    dlocal = dextended[halo_rows:] + jnp.concatenate(
        [jnp.zeros((length - halo_rows, 3, channels), jnp.float32), incoming], axis=0
    )
    feature_grad = dlocal.astype(jnp.bfloat16)[None]
    totals = lax.psum(
        (conv_local, rate_local, residue_local, skip_local, gain_local), ("dp", "ctx")
    )
    return (block_out[None], feature_grad, totals[0], totals[1], totals[2], totals[3], totals[4])


def solution(mesh):
    in_specs = (
        P("dp", "ctx", None, "mp"),
        P(None, None, "mp"),
        P(None, "mp"),
        P(None, "mp"),
        P("mp"),
        P("mp"),
        P("dp", "ctx", "mp"),
    )
    out_specs = (
        P("dp", "ctx", "mp"),
        P("dp", "ctx", None, "mp"),
        P(None, None, "mp"),
        P(None, "mp"),
        P(None, "mp"),
        P("mp"),
        P("mp"),
    )
    return jax.shard_map(local, mesh=mesh, in_specs=in_specs, out_specs=out_specs, check_vma=False)
```

profile of v0, /device:TPU:0, one launch (start us, length us, event | category | flops | bytes accessed | tf_op | source)
XLA Modules:
  0.0 2139.7 jit_solution(14530745588208930304)
XLA Ops:
  9.4 2.1 fusion.91
  12.5 7.9 fusion.48
  23.7 1.3 copy.102
  25.0 38.0 %while.51 = (s32[]{:T(128)}, f32[16,8,128,128]{3,2,1,0:T(8,128)}, f32[16,8]{1,0:T(8,128)S(1)}, f32[16,128,128]{2,1,0:T(8,128)}, s32[]{:T(128)}) while((s32[]{:T(128)}, f32[16,8,128,128]{3,2,1,0:T(8,128)}, f32[16,8]{1,0:T(8,128)S(1)}, f32[16,128,128]{2,1,0:T(8,128)}, s32[]{:T(128)}) %tuple.143), condition=%wide.region_1.2_spmd, body=%wide.region_0.1_spmd.sunk | while | flops 201654288 | bytes 754849 | solution.py:78
  25.1 2.3 fusion.110
  27.5 2.3 fusion.110
  29.9 2.3 fusion.110
  32.3 2.3 fusion.110
  34.6 2.3 fusion.110
  37.0 2.3 fusion.110
  39.4 2.3 fusion.110
  41.7 2.3 fusion.110
  44.1 2.3 fusion.110
  46.5 2.3 fusion.110
  48.9 2.3 fusion.110
  51.3 2.3 fusion.110
  53.6 2.3 fusion.110
  56.0 2.3 fusion.110
  58.3 2.3 fusion.110
  60.7 2.3 fusion.110
  63.0 9.9 copy.50
  76.2 91.5 %all-gather.3 = f32[64,16,8]{1,2,0:T(8,128)} all-gather(f32[1,16,8]{1,2,0:T(8,128)S(1)} %get-tuple-element.392), channel_id=2, replica_groups=mesh['dp'=4,'ctx'=64,'mp'=2] {'ctx'}, dimensions={0}, use_global_device_ids=true | all-gather | bytes 33280 | tf_op jit(solution)/shard_map/all_gather | solution.py:23
  169.1 53.8 %all-gather.7.cloned.1.call-done = f32[1024,8,1,128]{3,1,2,0:T(8,128)} async-done(((f32[16,8,1,128]{3,1,2,0:T(8,128)}), f32[1024,8,1,128]{3,1,2,0:T(8,128)}) %all-gather.7.cloned.1.call-update) | async-done | bytes 4194320 | tf_op jit(solution)/shard_map/all_gather | solution.py:23
  223.0 8.3 multiply_reduce_fusion.2
  231.3 1.3 fusion.67
  232.6 2.5 all-reduce.5
  235.1 3.2 fusion.85
  239.3 1.6 fusion.87
  241.1 2.9 copy.51
  243.9 2.4 reshape.384
  246.3 2.4 reshape.382
  248.7 2.9 fusion.72
  252.8 232.8 %all-gather.9.cloned.1.call-done = f32[1024,8,128]{2,1,0:T(8,128)} async-done(((f32[16,8,128]{2,1,0:T(8,128)}), f32[1024,8,128]{2,1,0:T(8,128)}) %all-gather.9.cloned.1.call-update) | async-done | bytes 4194320 | tf_op jit(solution)/shard_map/all_gather | solution.py:23
  485.6 107.9 %while.53 = (s32[]{:T(128)}, f32[16,8,128]{2,1,0:T(8,128)S(1)}, s32[]{:T(128)}, f32[64,16,8]{1,2,0:T(8,128)}, f32[64,16,8,128]{3,2,1,0:T(8,128)}, /*index=5*/s32[]{:T(128)}, s32[]{:T(128)}, s32[]{:T(128)}, s32[]{:T(128)}) while((s32[]{:T(128)}, f32[16,8,128]{2,1,0:T(8,128)S(1)}, s32[]{:T(128)}, f32[64,16,8]{1,2,0:T(8,128)}, ...), condition=%wide.region_9.10_spmd, body=%wide.region_8.9_spmd.sunk | while | flops 32774 | bytes 199315 | solution.py:32
  594.1 146.1 %while.54 = (s32[]{:T(128)}, f32[16,8,128]{2,1,0:T(8,128)}, f32[16,8]{1,0:T(8,128)}, f32[16,128,128]{2,1,0:T(8,128)}, f32[16,128,128]{2,1,0:T(8,128)}, /*index=5...) while((s32[]{:T(128)}, f32[16,8,128]{2,1,0:T(8,128)}, ...), condition=%wide.region_15.16_spmd.clone, body=%wide.region_10.15_spmd.clone.sunk | while | flops 202687648 | bytes 3312593 | solution.py:146
  595.6 1.5 multiply_reduce_fusion.7
  604.8 1.5 multiply_reduce_fusion.7
  610.5 1.3 dynamic_update_slice.29
  613.9 1.5 multiply_reduce_fusion.7
  623.1 1.5 multiply_reduce_fusion.7
  628.7 1.3 dynamic_update_slice.29
  632.2 1.5 multiply_reduce_fusion.7
  641.3 1.5 multiply_reduce_fusion.7
  650.4 1.5 multiply_reduce_fusion.7
  659.6 1.5 multiply_reduce_fusion.7
  668.7 1.5 multiply_reduce_fusion.7
  677.8 1.5 multiply_reduce_fusion.7
  686.9 1.5 multiply_reduce_fusion.7
  696.1 1.5 multiply_reduce_fusion.7
  705.2 1.5 multiply_reduce_fusion.7
  714.3 1.5 multiply_reduce_fusion.7
  723.5 1.5 multiply_reduce_fusion.7
  732.6 1.5 multiply_reduce_fusion.7
  740.2 1.4 copy.60
  741.6 2.8 copy.59
  744.4 2.4 reshape.385
  746.8 2.9 slice_multiply_fusion.6
  751.2 3.4 fusion.54
  755.3 2.8 fusion.38
  758.1 1.7 copy-done.5
  762.0 1364.5 %all-reduce.3 = (f32[8,16]{1,0:T(8,128)}, f32[2048]{0:T(1024)}, f32[2048]{0:T(1024)}) all-reduce(f32[8,16]{1,0:T(8,128)S(1)} %bitcast_multiply_fusion.4, f32[2048]{0:T(1024)} %get-tuple-element.308, f32[2048]{0:T(1024)S(1)} %copy-done.24), channel_id=1, replica_groups=mesh['dp'=4,'ctx'=64,'mp'=2] {'dp','ctx'}, use_global_device_ids=true, to_apply=%region_24.25 | all-reduce | flops 4224 | bytes 33792 | tf_op jit(solution)/shard_map/psum | solution.py:173
  2126.5 3.5 fusion.57
  2130.0 1.7 copy.61
  2131.7 1.5 copy.150
  (590 shorter events, 244.1 us)
Async XLA Ops:
  7.2 215.7 %all-gather.7.cloned.1.call-start = ((), (), s32[]{:S(2)}) async-start(), calls=%async_computation | async-start | bytes 4259840 | tf_op jit(solution)/shard_map/all_gather | solution.py:23
  8.1 4.3 collective-permute-start
  11.6 9.9 copy-start.12
  12.4 9.1 copy-start.14
  21.5 1.0 copy-start
  22.7 1.0 copy-start.6
  63.0 10.0 copy-start.26
  63.0 10.7 copy-start.23
  73.6 411.9 %all-gather.9.cloned.1.call-start = ((), (), s32[]{:S(2)}) async-start(), calls=%async_computation.1 | async-start | bytes 4259840 | tf_op jit(solution)/shard_map/all_gather | solution.py:23
  73.8 149.1 %copy-start.21 = (f32[16,8]{1,0:T(8,128)}, f32[16,8]{1,0:T(8,128)S(1)}, u32[]{:S(2)}) copy-start(f32[16,8]{1,0:T(8,128)S(1)} %copy.49) | copy-start | bytes 1540
  73.8 94.1 %copy-start.9 = (f32[16,8,16,128]{3,1,2,0:T(8,128)S(1)}, f32[16,8,16,128]{3,1,2,0:T(8,128)}, u32[]{:S(2)}) copy-start(f32[16,8,16,128]{3,1,2,0:T(8,128)} %get-tuple-element.382) | copy-start | bytes 3145732
  167.8 55.1 %copy-start.31 = (f32[128]{0:T(128)}, f32[128]{0:T(128)S(1)}, u32[]{:S(2)}) copy-start(f32[128]{0:T(128)S(1)} %iota_add_fusion) | copy-start | bytes 1540
  222.9 8.3 copy-start.1
  222.9 8.3 copy-start.7
  222.9 8.3 copy-start.16
  222.9 8.3 copy-start.18
  231.2 1.4 copy-start.3
  231.2 3.9 copy-start.19
  232.6 6.7 copy-start.22
  232.6 6.7 copy-start.32
  235.1 13.6 copy-start.29
  235.1 16.5 copy-start.27
  238.3 1.1 copy-start.8
  241.0 1888.9 %all-reduce.8.cloned.1.call-start = ((), (), s32[]{:S(2)}) async-start(), calls=%async_computation.2 | async-start | bytes 589824 | tf_op jit(solution)/shard_map/psum | solution.py:173
  248.7 2.9 copy-start.2
  248.7 2.9 copy-start.10
  740.2 6.6 copy-start.17
  740.2 6.6 copy-start.20
  740.2 6.6 copy-start.28
  740.2 6.6 copy-start.30
  749.8 1.4 copy-start.4
  754.6 0.8 copy-start.13
  754.6 0.8 copy-start.15
  755.3 6.6 copy-start.25
  755.3 6.7 copy-start.24
  758.1 1.7 copy-start.5
  759.8 1366.6 %collective-permute-start.1 = (f32[6,3,2048]{2,0,1:T(8,128)S(1)}, f32[6,3,2048]{2,0,1:T(8,128)S(1)}, u32[]{:S(2)}, u32[]{:S(2)}) collective-permute-start(f32[6,3,2048]{2,0,1:T(8,128)S(1)} %slice.156), channel_id=1, source_target_pairs={{2,0},{4,2},{6,4},{8,6},{10,8},{12,10},{14,12},{16,14},{18,16},{20... | collective-permute-start | bytes 442376 | tf_op jit(solution)/shard_map/ppermute | solution.py:16
  761.3 0.7 copy-start.11
Sparse Core Ops, SparseCore 0:
  73.8 149.0 all-gather.6
  241.1 244.3 all-gather.8
  762.1 380.4 all-reduce.7
where the time goes:
time: 2150 us; the launch traced here: 2140 us
  blocking collectives  1460 us (68%)
  waiting for transfers between devices  287 us (13%)
  local copies, waits for them, and re-layouts  156 us (7%)
  other arithmetic  156 us (7%)
  matrix products  62.4 us (3%)
    psum x1, blocking collectives, local(): lax.psum((conv_local, rate_local, residue_local, skip_local, gain_local),...  1360 us
    all_gather x2, waiting for transfers between devices, carried_in(): gathered = jax.tree.map(lambda a: lax.all_gather(a, axis), part)  287 us
    all_gather x1, blocking collectives, carried_in(): gathered = jax.tree.map(lambda a: lax.all_gather(a, axis), part)  91.5 us
    add x63, other arithmetic, compose_back(): return (earlier[0] * later[0], earlier[1] * later[0][..., None] + later[1])  58.2 us
    mul x126, local copies, waits for them, and re-layouts, compose_back(): return (earlier[0] * later[0], earlier[1] * later[0][..., None] + later[1])  47.7 us
  transfers between devices with their start and end apart: 5, of which 2 were waited for; matrix products, arithmetic and copies ran while one was open for 1% of the time, Pallas kernels for 0%

commit v1 on v0

v1 whole, which is shorter than its diff:
```python
import functools
import jax
import jax.numpy as jnp
from jax import lax
from jax.experimental import pallas as pl
from jax.experimental.pallas import tpu as pltpu
from jax.sharding import PartitionSpec as P

D = 4096
EPSILON = 1e-06
HIGHEST = lax.Precision.HIGHEST
F32 = jnp.float32
BF16 = jnp.bfloat16
L = 128
GS = 128
POLES = 8
TAPS = 7
PAD = 8
GB = 2
ROWS = 32


def params(mib):
    return pltpu.CompilerParams(vmem_limit_bytes=mib * 1024 * 1024)


def iota(shape, dim):
    return lax.broadcasted_iota(jnp.int32, shape, dim)


def ones_tri(lower):
    row = iota((L, 2 * L), 0)
    col = iota((L, 2 * L), 1) % L
    keep = col <= row if lower else col >= row
    return jnp.where(keep, 1.0, 0.0).astype(BF16)


def split(x):
    high = x.astype(BF16)
    low = (x - high.astype(F32)).astype(BF16)
    return jnp.concatenate([high, low], axis=0)


def tri_dot(tri, xs):
    return jnp.dot(tri, jnp.concatenate([split(x) for x in xs], axis=1), preferred_element_type=F32)


def contract_rows(a, b):
    return lax.dot_general(a, b, (((0,), (0,)), ((), ())), precision=HIGHEST, preferred_element_type=F32)


def rowsum(x):
    return jnp.sum(x, axis=0, keepdims=True)


def fill_ext(ext, feat, halo, cs):
    for j in range(3):
        ext[j, 0:PAD, :] = halo[j, :, cs].astype(F32)
        ext[j, PAD : PAD + L, :] = feat[j, :, cs].astype(F32)


def forward_kernel(rate, feat, halo, taps, weight, skip, q_o, k_o, v_o, bl_o, s_o, e_o, ext):
    first = pl.program_id(0) * GB
    tri = ones_tri(True)
    place = iota((L, GS), 0).astype(F32)
    for gi in range(GB):
        cs = slice(gi * GS, (gi + 1) * GS)
        fill_ext(ext, feat, halo, cs)
        rows = []
        for j in range(3):
            acc = taps[j, 0:1, cs] * ext[j, PAD : PAD + L, :]
            for k in range(1, TAPS):
                acc = acc + taps[j, k : k + 1, cs] * ext[j, pl.ds(PAD - k, L), :]
            rows.append(acc)
        q, key, value = rows
        q_o[:, cs] = q
        k_o[:, cs] = key
        v_o[:, cs] = value
        prod = key * value
        modal = skip[0:1, cs] * prod
        for p in range(0, POLES, 2):
            rates = [rate[p + i, first + gi] for i in range(2)]
            both = tri_dot(tri, [jnp.exp(place * r) * prod for r in rates])
            for i, r in enumerate(rates):
                state = jnp.exp(place * (-r)) * both[:, i * GS : (i + 1) * GS]
                s_o[p + i, :, cs] = state
                e_o[gi, p + i : p + i + 1, :] = state[L - 1 : L, :]
                modal = modal + weight[p + i : p + i + 1, cs] * state
        bl_o[:, cs] = modal


def scan_kernel(back, rate, where, rows, out):
    me = where[0]
    group = me // 4
    pole = 2 * (me % 4)
    low, high = rate[pole, group], rate[pole + 1, group]
    row, col = iota((L, L), 0), iota((L, L), 1)
    lag = col // 2 - row // 2 - 1 if back else row // 2 - col // 2 - 1
    keep = (lag >= 0) & (row % 2 == col % 2)
    own = jnp.where(row % 2 == 0, low, high)
    decay = jnp.where(keep, jnp.exp(-(own * L) * jnp.maximum(lag, 0).astype(F32)), 0.0)
    out[...] = jnp.dot(decay, rows[...], precision=HIGHEST, preferred_element_type=F32)


def branch_kernel(q, bl, cot, gain, state_in, head, weight, br_o, stats_o, acc):
    step = pl.program_id(0)

    @pl.when(step == 0)
    def _():
        acc[...] = jnp.zeros_like(acc)

    for gi in range(GB):
        cs = slice(gi * GS, (gi + 1) * GS)
        branch = bl[:, cs] + contract_rows(head[gi], weight[:, cs] * state_in[gi])
        br_o[:, cs] = branch
        gated = q[:, cs] * branch
        acc[0] += gated * gated
        acc[1] += (gain[0:1, cs] * cot[:, cs].astype(F32)) * gated

    @pl.when(step == pl.num_programs(0) - 1)
    def _():
        row = iota((8, L), 0)
        squares = rowsum(acc[0].T)
        slopes = rowsum(acc[1].T)
        stats_o[...] = jnp.where(row == 0, squares, jnp.where(row == 1, slopes, 0.0))


def down(row):
    return jnp.broadcast_to(row, (L, L)).T


def gate_kernel(stats, q, br, cot, gain, k, v, head, out_o, g_o, dq_o, back_o, gain_o, skip_o):
    inv_row = lax.rsqrt(stats[0:1, :] / D + EPSILON)
    inv = down(inv_row)
    pull = down(stats[1:2, :] * inv_row * inv_row * inv_row / D)
    for gi in range(GB):
        cs = slice(gi * GS, (gi + 1) * GS)
        query = q[:, cs]
        branch = br[:, cs]
        grad = cot[:, cs].astype(F32)
        gated = query * branch
        normed = gated * inv
        out_o[:, cs] = (gain[0:1, cs] * normed).astype(BF16)
        gain_o[0:1, cs] = rowsum(grad * normed)
        dgated = (gain[0:1, cs] * grad) * inv - gated * pull
        dq_o[:, cs] = dgated * branch
        dbranch = dgated * query
        g_o[:, cs] = dbranch
        skip_o[0:1, cs] = rowsum(dbranch * (k[:, cs] * v[:, cs]))
        back_o[gi] = jnp.dot(head[gi], dbranch, precision=HIGHEST, preferred_element_type=F32)


def adjoint_kernel(
    rate, g, dq, k, v, states, weight, skip, state_in, back, heads, tails, feat, halo,
    dpl_o, res_o, loc_o, mix_o, cq_o, ext,
):
    first = pl.program_id(0) * GB
    tri = ones_tri(False)
    place = iota((L, GS), 0).astype(F32)
    centre = place - (L - 1) / 2
    for gi in range(GB):
        cs = slice(gi * GS, (gi + 1) * GS)
        dbranch = g[:, cs]
        prod = k[:, cs] * v[:, cs]
        total = skip[0:1, cs] * dbranch
        far_grad = centre * dbranch
        far_prod = centre * prod
        own_in = state_in[gi]
        residue = own_in * back[gi]
        heavy = jnp.dot(heads[gi], dbranch, precision=HIGHEST, preferred_element_type=F32)
        deep = jnp.dot(tails[gi], prod, precision=HIGHEST, preferred_element_type=F32)
        for p in range(0, POLES, 2):
            rates = [rate[p + i, first + gi] for i in range(2)]
            both = tri_dot(tri, [jnp.exp(place * (-r)) * dbranch for r in rates])
            for i, r in enumerate(rates):
                at = slice(p + i, p + i + 1)
                adjoint = jnp.exp(place * r) * both[:, i * GS : (i + 1) * GS]
                total = total + weight[at, cs] * adjoint
                res_o[at, cs] = residue[at, :] + rowsum(prod * adjoint)
                loc_o[at, cs] = rowsum(far_grad * states[p + i, :, cs] - far_prod * adjoint)
        dpl_o[:, cs] = total
        lane_rate = jnp.zeros((POLES, GS), F32)
        for p in range(POLES):
            lane_rate = jnp.where(iota((POLES, GS), 0) == p, rate[p, first + gi], lane_rate)
        once = jnp.exp(-lane_rate)
        loc_o[:, cs] += once * own_in * heavy
        mix_o[:, cs] = once * (deep + L * jnp.exp(-(L - 1) * lane_rate) * own_in)
        fill_ext_one(ext, feat, halo, cs)
        dquery = dq[:, cs]
        for t in range(TAPS):
            cq_o[t : t + 1, cs] = rowsum(dquery * ext[pl.ds(PAD - t, L), :])


def fill_ext_one(ext, feat, halo, cs):
    ext[0:PAD, :] = halo[0, :, cs].astype(F32)
    ext[PAD : PAD + L, :] = feat[0, :, cs].astype(F32)


def finish_kernel(
    rate, later, dpl, dq, k, v, tails, weight, loc, mix, cq, res, skip, gain, feat, halo, rim, taps,
    grad_o, pack_o, ext, dext,
):
    first = pl.program_id(0) * GB
    lane = iota((POLES, GS), 1)
    sub = iota((POLES, GS), 0)
    ahead = (iota((PAD, GS), 0) + 1).astype(F32)
    for gi in range(GB):
        cs = slice(gi * GS, (gi + 1) * GS)
        coming = later[gi]
        dprod = dpl[:, cs] + contract_rows(tails[gi], weight[:, cs] * coming)
        key, value = k[:, cs], v[:, cs]
        dext[0, 0:L, :] = dq[:, cs]
        dext[1, 0:L, :] = dprod * value
        dext[2, 0:L, :] = dprod * key
        beyond = weight[:, cs] * (coming - rim[4, :, cs])
        next_prod = rim[1, :, cs]
        for p in range(POLES):
            next_prod = next_prod + jnp.exp(ahead * rate[p, first + gi]) * beyond[p : p + 1, :]
        dext[0, L : L + PAD, :] = rim[0, :, cs]
        dext[1, L : L + PAD, :] = next_prod * rim[3, :, cs]
        dext[2, L : L + PAD, :] = next_prod * rim[2, :, cs]
        fill_ext(ext, feat, halo, cs)
        pack_o[gi, 0:TAPS, :] = cq[0:TAPS, cs]
        for j in range(3):
            acc = taps[j, 0:1, cs] * dext[j, 0:L, :]
            for t in range(1, TAPS):
                acc = acc + taps[j, t : t + 1, cs] * dext[j, pl.ds(t, L), :]
            grad_o[j, :, cs] = acc.astype(BF16)
            if j:
                own = dext[j, 0:L, :]
                for t in range(TAPS):
                    at = TAPS * j + t
                    pack_o[gi, at : at + 1, :] = rowsum(own * ext[j, pl.ds(PAD - t, L), :])
        pack_o[gi, 21:29, :] = res[:, cs]
        pack_o[gi, 29:30, :] = skip[0:1, cs]
        pack_o[gi, 30:31, :] = gain[0:1, cs]
        inner = jnp.sum(weight[:, cs] * (loc[:, cs] + coming * mix[:, cs]), axis=1, keepdims=True)
        lane_rate = jnp.zeros((POLES, GS), F32)
        for p in range(POLES):
            lane_rate = jnp.where(sub == p, rate[p, first + gi], lane_rate)
        pack_o[gi, 31:32, :] = rowsum(jnp.where(lane == sub, -lane_rate * inner, 0.0))


def add_kernel(parts, out):
    out[...] = jnp.sum(parts[...], axis=0)


def unpack_kernel(pack, conv_o, rate_o, res_o, skip_o, gain_o):
    groups = pack.shape[0]
    for gi in range(groups):
        cs = slice(gi * GS, (gi + 1) * GS)
        for j in range(3):
            conv_o[j, :, cs] = pack[gi, TAPS * j : TAPS * j + TAPS, :]
        res_o[:, cs] = pack[gi, 21:29, :]
        skip_o[0:1, cs] = pack[gi, 29:30, :]
        gain_o[0:1, cs] = pack[gi, 30:31, :]
        rate_o[gi : gi + 1, :] = pack[gi, 31:32, :]


def smem():
    return pl.BlockSpec(memory_space=pltpu.SMEM)


def cols(*lead):
    return pl.BlockSpec((*lead, GB * GS), lambda i: (0,) * len(lead) + (i,))


def groups_of(rows):
    return pl.BlockSpec((GB, rows, GS), lambda i: (i, 0, 0))


def shape(*dims, dtype=F32):
    return jax.ShapeDtypeStruct(dims, dtype)


def local(features, conv_weight, log_rate, residues, skip_weight, norm_gain, cotangent):
    feat = features[0].transpose(1, 0, 2)
    taps = conv_weight.transpose(1, 0, 2)
    cot = cotangent[0]
    channels = feat.shape[2]
    groups = log_rate.shape[1]
    count = lax.axis_size("ctx")
    steps = groups // GB
    skip = skip_weight[None]
    gain = norm_gain[None]
    where = lax.axis_index("ctx").astype(jnp.int32)[None]

    halo = lax.ppermute(feat[:, L - PAD :], "ctx", [(i, i + 1) for i in range(count - 1)])
    rate = jnp.exp(log_rate)
    by_group = rate.T[:, :, None]
    places = jnp.arange(L, dtype=F32)
    head = jnp.exp(-by_group * (places + 1.0))
    heads = (places + 1.0) * jnp.exp(-by_group * places)
    tail = jnp.exp(-by_group * (L - 1.0 - places))
    tails = (L - 1.0 - places) * jnp.exp(-by_group * (L - 2.0 - places))

    query, key, value, base, states, ends = pl.pallas_call(
        forward_kernel,
        grid=(steps,),
        in_specs=[smem(), cols(3, L), cols(3, PAD), cols(3, TAPS), cols(POLES), cols(1)],
        out_specs=[cols(L)] * 4 + [cols(POLES, L), groups_of(POLES)],
        out_shape=[shape(L, channels)] * 4 + [shape(POLES, L, channels), shape(groups, POLES, GS)],
        scratch_shapes=[pltpu.VMEM((3, PAD + L, GS), F32)],
        compiler_params=params(24),
        name="forward_local",
    )(rate, feat, halo, taps, residues, skip)

    def carried(rows, back):
        sent = lax.all_to_all(rows.reshape(count, 2, GS), "ctx", 0, 0)
        summed = pl.pallas_call(
            functools.partial(scan_kernel, back),
            in_specs=[smem(), smem(), pl.BlockSpec((L, GS), lambda: (0, 0))],
            out_specs=pl.BlockSpec((L, GS), lambda: (0, 0)),
            out_shape=shape(L, GS),
            name="carry_back" if back else "carry_on",
        )(rate, where, sent.reshape(L, GS))
        given = lax.all_to_all(summed.reshape(count, 2, GS), "ctx", 0, 0)
        return given.reshape(groups, POLES, GS)

    state_in = carried(ends, False)

    branch, stats = pl.pallas_call(
        branch_kernel,
        grid=(steps,),
        in_specs=[cols(L), cols(L), cols(L), cols(1), groups_of(POLES), groups_of(POLES), cols(POLES)],
        out_specs=[cols(L), pl.BlockSpec((8, L), lambda i: (0, 0))],
        out_shape=[shape(L, channels), shape(8, L)],
        scratch_shapes=[pltpu.VMEM((2, L, GS), F32)],
        compiler_params=params(24),
        name="branch",
    )(query, base, cot, gain, state_in, head, residues)
    stats = lax.psum(stats, "mp")

    block_out, dbranch, dquery, back_in, gain_part, skip_part = pl.pallas_call(
        gate_kernel,
        grid=(steps,),
        in_specs=[pl.BlockSpec((8, L), lambda i: (0, 0))]
        + [cols(L)] * 3
        + [cols(1), cols(L), cols(L), groups_of(POLES)],
        out_specs=[cols(L)] * 3 + [groups_of(POLES), cols(1), cols(1)],
        out_shape=[shape(L, channels, dtype=BF16), shape(L, channels), shape(L, channels)]
        + [shape(groups, POLES, GS), shape(1, channels), shape(1, channels)],
        compiler_params=params(24),
        name="gate",
    )(stats, query, branch, cot, gain, key, value, head)

    dlocal, res_part, loc_part, mix_part, cq_part = pl.pallas_call(
        adjoint_kernel,
        grid=(steps,),
        in_specs=[smem()]
        + [cols(L)] * 4
        + [cols(POLES, L), cols(POLES), cols(1)]
        + [groups_of(POLES)] * 4
        + [cols(3, L), cols(3, PAD)],
        out_specs=[cols(L), cols(POLES), cols(POLES), cols(POLES), cols(TAPS)],
        out_shape=[shape(L, channels)] + [shape(POLES, channels)] * 3 + [shape(TAPS, channels)],
        scratch_shapes=[pltpu.VMEM((PAD + L, GS), F32)],
        compiler_params=params(24),
        cost_estimate=pl.CostEstimate(flops=6_000_000_000, bytes_accessed=16_000_000, transcendentals=4_000_000),
        name="adjoint_local",
    )(rate, dbranch, dquery, key, value, states, residues, skip, state_in, back_in, heads, tails, feat, halo)

    edge = jnp.stack(
        [dquery[:PAD], dlocal[:PAD], key[:PAD], value[:PAD], back_in.transpose(1, 0, 2).reshape(POLES, channels)]
    )
    rim = lax.ppermute(edge, "ctx", [(i + 1, i) for i in range(count - 1)])
    later = carried(back_in, True)

    feature_grad, pack = pl.pallas_call(
        finish_kernel,
        grid=(steps,),
        in_specs=[smem(), groups_of(POLES)]
        + [cols(L)] * 4
        + [groups_of(POLES)]
        + [cols(POLES)] * 3
        + [cols(TAPS), cols(POLES), cols(1), cols(1)]
        + [cols(3, L), cols(3, PAD), cols(5, PAD), cols(3, TAPS)],
        out_specs=[cols(3, L), groups_of(ROWS)],
        out_shape=[shape(3, L, channels, dtype=BF16), shape(groups, ROWS, GS)],
        scratch_shapes=[pltpu.VMEM((3, PAD + L, GS), F32), pltpu.VMEM((3, PAD + L, GS), F32)],
        compiler_params=params(24),
        name="finish",
    )(rate, later, dlocal, dquery, key, value, tail, residues, loc_part, mix_part, cq_part, res_part, skip_part, gain_part, feat, halo, rim, taps)

    share = groups * ROWS // count
    parts = lax.all_to_all(pack.reshape(count, share, GS), "ctx", 0, 0)
    mine = pl.pallas_call(add_kernel, out_shape=shape(share, GS), name="add_parts")(parts)
    mine = lax.psum(mine, "dp")
    totals = lax.all_to_all(jnp.broadcast_to(mine[None], (count, share, GS)), "ctx", 0, 0)
    conv, rate_grad, res, skip_grad, gain_grad = pl.pallas_call(
        unpack_kernel,
        out_shape=[shape(3, TAPS, channels), shape(groups, GS), shape(POLES, channels)] + [shape(1, channels)] * 2,
        name="unpack",
    )(totals.reshape(groups, ROWS, GS))
    return (
        block_out[None],
        feature_grad.transpose(1, 0, 2)[None],
        conv.transpose(1, 0, 2),
        rate_grad[:, :POLES].T,
        res,
        skip_grad[0],
        gain_grad[0],
    )


def solution(mesh):
    in_specs = (
        P("dp", "ctx", None, "mp"),
        P(None, None, "mp"),
        P(None, "mp"),
        P(None, "mp"),
        P("mp"),
        P("mp"),
        P("dp", "ctx", "mp"),
    )
    out_specs = (
        P("dp", "ctx", "mp"),
        P("dp", "ctx", None, "mp"),
        P(None, None, "mp"),
        P(None, "mp"),
        P(None, "mp"),
        P("mp"),
        P("mp"),
    )
    return jax.shard_map(local, mesh=mesh, in_specs=in_specs, out_specs=out_specs, check_vma=False)
```

time: 2150 us -> 246 us (0.11)
  the two profiles are of different devices: /device:TPU:0 before, /device:TPU:6 now
where the time goes in v1:
time: 246 us; the launch traced here: 244 us
  blocking collectives  62.7 us (25%)
  waiting for transfers between devices  47.9 us (19%)
  starting transfers between devices  47 us (19%)
  local copies, waits for them, and re-layouts  43.4 us (18%)
  Pallas kernels  40.8 us (17%)
    unnamed x95, local copies, waits for them, and re-layouts  41.1 us
    all_to_all x1, blocking collectives, local(): parts = lax.all_to_all(pack.reshape(count, share, GS), 'ctx', 0, 0)  25.6 us
    all_to_all x2, waiting for transfers between devices, carried(): given = lax.all_to_all(summed.reshape(count, 2, GS), 'ctx', 0, 0)  25 us
    all_to_all x1, blocking collectives, local(): lax.all_to_all(jnp.broadcast_to(mine[None], (count, share, GS)), 'ctx', 0...  23.8 us
    all_to_all x2, starting transfers between devices, carried(): sent = lax.all_to_all(rows.reshape(count, 2, GS), 'ctx', 0, 0)  19.2 us
    all_to_all x2, starting transfers between devices, carried(): given = lax.all_to_all(summed.reshape(count, 2, GS), 'ctx', 0, 0)  19.1 us
    all_to_all x2, waiting for transfers between devices, carried(): sent = lax.all_to_all(rows.reshape(count, 2, GS), 'ctx', 0, 0)  12.9 us
    psum x1, blocking collectives, local(): mine = lax.psum(mine, 'dp')  10.9 us
  transfers between devices with their start and end apart: 6, of which 4 were waited for; matrix products, arithmetic and copies ran while one was open for 2% of the time, Pallas kernels for 5%

profile of v1, /device:TPU:6, one launch (start us, length us, event | category | flops | bytes accessed | tf_op | source)
XLA Modules:
  0.0 244.1 jit_solution(12370070798101757422)
XLA Ops:
  0.7 0.9 slice.24
  1.6 3.8 %collective-permute-start = (bf16[3,8,2048]{2,1,0:T(8,128)(2,1)S(1)}, bf16[3,8,2048]{2,1,0:T(8,128)(2,1)S(1)}, u32[]{:S(2)}, u32[]{:S(2)}) collective-permute-start(bf16[3,8,2048]{2,1,0:T(8,128)(2,1)S(1)} %slice.24), channel_id=1, source_target_pairs={{0,2},{2,4},{4,6},{6,8},{8,10},{10,12},{12,14},{14,16},{16,18},{18... | collective-permute-start | bytes 294920 | tf_op jit(solution)/shard_map/ppermute | solution.py:288
  5.4 0.7 negate_bitcast_fusion
  6.1 9.9 %collective-permute-done.halo = bf16[3,8,2048]{2,1,0:T(8,128)(2,1)S(1)} collective-permute-done((bf16[3,8,2048]{2,1,0:T(8,128)(2,1)S(1)}, bf16[3,8,2048]{2,1,0:T(8,128)(2,1)S(1)}, u32[]{:S(2)}, u32[]{:S(2)}) %collective-permute-start) | collective-permute-done | bytes 98336 | tf_op jit(solution)/shard_map/ppermute | solution.py:288
  16.0 1.4 copy-done
  17.4 0.9 copy-done.18
  18.4 0.8 copy-done.20
  19.2 0.7 copy-done.38
  19.9 9.0 %forward_local.1 = (f32[128,2048]{1,0:T(8,128)S(1)}, f32[128,2048]{1,0:T(8,128)S(1)}, f32[128,2048]{1,0:T(8,128)S(1)}, f32[128,2048]{1,0:T(8,128)S(1)}, f32[8,12...) custom-call(f32[8,16]{1,0:T(8,128)S(1)} %get-tuple-element.73.rate, bf16[3,128,2048]{2,1,0:T(8,128)(2,1)S(1)} %bitcast.42, ...), custom_call_target="tpu_custom_call" | custom-call | tf_op jit(solution)/shard_map/forward_local/pallas_call | solution.py:297
  28.9 1.0 copy-done.2
  29.8 1.0 copy-done.14
  30.8 3.3 %copy-done.40 = f32[8,128,2048]{2,1,0:T(8,128)} copy-done((f32[8,128,2048]{2,1,0:T(8,128)}, f32[8,128,2048]{2,1,0:T(8,128)S(1)}, u32[]{:S(2)}) %copy-start.40) | copy-done | bytes 8388632
  34.1 12.1 %all-to-all-start = ((f32[64,2,128]{2,1,0:T(2,128)}), f32[64,2,128]{2,1,0:T(2,128)S(1)}, u32[]{:S(2)}, u32[]{:S(2)}) async-start(f32[64,2,128]{2,1,0:T(2,128)} %bitcast.8), calls=%async_computation | async-start | bytes 131072 | tf_op jit(solution)/shard_map/all_to_all | solution.py:309
  46.2 12.9 %all-to-all-done = f32[64,2,128]{2,1,0:T(2,128)S(1)} async-done(((f32[64,2,128]{2,1,0:T(2,128)}), f32[64,2,128]{2,1,0:T(2,128)S(1)}, u32[]{:S(2)}, u32[]{:S(2)}) %all-to-all-start) | async-done | bytes 65568 | tf_op jit(solution)/shard_map/all_to_all | solution.py:309
  59.1 0.6 copy-done.44
  59.8 1.7 carry_on.1
  61.5 6.3 %all-to-all-start.1 = ((f32[64,2,128]{2,1,0:T(2,128)}), f32[64,2,128]{2,1,0:T(2,128)S(1)}, u32[]{:S(2)}, u32[]{:S(2)}) async-start(f32[64,2,128]{2,1,0:T(2,128)} %bitcast.60), calls=%async_computation.1 | async-start | bytes 131072 | tf_op jit(solution)/shard_map/all_to_all | solution.py:317
  67.9 0.8 multiply_exponential_fusion
  68.7 12.1 %all-to-all-done.1 = f32[64,2,128]{2,1,0:T(2,128)S(1)} async-done(((f32[64,2,128]{2,1,0:T(2,128)}), f32[64,2,128]{2,1,0:T(2,128)S(1)}, u32[]{:S(2)}, u32[]{:S(2)}) %all-to-all-start.1) | async-done | bytes 65568 | tf_op jit(solution)/shard_map/all_to_all | solution.py:317
  80.8 1.2 copy-done.15
  82.0 3.3 %branch.1 = (f32[128,2048]{1,0:T(8,128)S(1)}, f32[8,128]{1,0:T(8,128)S(1)}) custom-call(f32[128,2048]{1,0:T(8,128)S(1)} %get-tuple-element.33.q, f32[128,2048]{1,0:T(8,128)S(1)} %copy-done.15, bf16[128,2048]{1,0:T(8,128)(2,1)S(1)} %bitcast.45, f32[1,2048]{1,0:T(1,128)S(1)} %bitcast.54, f32[16,8,128]{2,1,0:T(8,128)S(1)} %bitcast.50, ...), custom_call_target="tpu_custom_call" | custom-call | tf_op jit(solution)/shard_map/branch/pallas_call | solution.py:322
  85.4 1.0 copy-done.16
  86.3 2.4 %psum.14.stats = f32[8,128]{1,0:T(8,128)S(1)} all-reduce(f32[8,128]{1,0:T(8,128)S(1)} %get-tuple-element.36), channel_id=1, replica_groups=mesh['dp'=4,'ctx'=64,'mp'=2] {'mp'}, use_global_device_ids=true, to_apply=%region_0.0 | all-reduce | flops 1024 | bytes 8192 | tf_op jit(solution)/shard_map/psum | solution.py:332
  88.8 1.2 copy-done.3
  90.0 1.2 copy-done.7
  91.2 1.2 copy-done.17
  92.5 4.0 %gate.1 = (bf16[128,2048]{1,0:T(8,128)(2,1)}, f32[128,2048]{1,0:T(8,128)S(1)}, f32[128,2048]{1,0:T(8,128)S(1)}, f32[16,8,128]{2,1,0:T(8,128)S(1)}, f32[1,2048]{1,0:T(1,128)S(1)}, /*index=5*/f32[1,2048]{1,0:T(1,128)S(1)}) custom-call(f32[8,128]{1,0:T(8,128)S(1)} %psum.14.stats, f32[128,2048]{1,0:T(8,128)S(1)} %copy-done.7, f32[128,2048]{1,0:T(8,128)S(1)} %copy-done.17, ...), custom_call_target="tpu_custom_call" | custom-call | tf_op jit(solution)/shard_map/gate/pallas_call | solution.py:334
  96.4 1.0 copy-done.9
  97.4 0.6 copy-done.22
  98.0 1.0 copy-done.42
  99.0 7.2 %all-to-all-start.2 = ((f32[64,2,128]{2,1,0:T(2,128)}), f32[64,2,128]{2,1,0:T(2,128)}, u32[]{:S(2)}, u32[]{:S(2)}) async-start(f32[64,2,128]{2,1,0:T(2,128)} %bitcast.53), calls=%async_computation.2 | async-start | bytes 131072 | tf_op jit(solution)/shard_map/all_to_all | solution.py:309
  106.2 1.5 bitcast_dynamic-update-slice_fusion.4
  107.7 1.2 copy-done.4
  108.9 1.2 copy-done.10
  110.1 0.8 copy-done.23
  110.9 0.8 copy-done.35
  111.8 0.8 copy-done.36
  112.6 3.4 %copy-done.41 = f32[8,128,2048]{2,1,0:T(8,128)S(1)} copy-done((f32[8,128,2048]{2,1,0:T(8,128)S(1)}, f32[8,128,2048]{2,1,0:T(8,128)}, u32[]{:S(2)}) %copy-start.41) | copy-done | bytes 8388632
  116.0 1.2 copy-done.43
  117.2 9.4 %adjoint_local.1 = (f32[128,2048]{1,0:T(8,128)S(1)}, f32[8,2048]{1,0:T(8,128)S(1)}, f32[8,2048]{1,0:T(8,128)S(1)}, f32[8,2048]{1,0:T(8,128)S(1)}, f32[7,2048]{1,0:T(8,128)S(1)}) custom-call(f32[8,16]{1,0:T(8,128)S(1)} %copy-done.25, f32[128,2048]{1,0:T(8,128)S(1)} %copy-done.43, f32[128,2048]{1,0:T(8,128)S(1)} %copy-done.10, ...), custom_call_target="tpu_custom_call" | custom-call | flops 6000000000 | bytes 16000000 | tf_op jit(solution)/shard_map/adjoint_local/pallas_call | solution.py:347
  126.6 0.6 copy-done.31
  127.9 0.7 bitcast_dynamic-update-slice_fusion.3
  128.6 1.0 copy-done.12
  130.2 0.6 bitcast_dynamic-update-slice_fusion.1
  130.8 0.6 bitcast_dynamic-update-slice_fusion
  131.4 4.9 %collective-permute-start.1 = (f32[5,8,2048]{2,1,0:T(8,128)}, f32[5,8,2048]{2,1,0:T(8,128)S(1)}, u32[]{:S(2)}, u32[]{:S(2)}) collective-permute-start(f32[5,8,2048]{2,1,0:T(8,128)} %bitcast_dynamic-update-slice_fusion), channel_id=1, source_target_pairs={{2,0},{4,2},{6,4},{8,6},{10,8},{12,10},{14,12},{16,14},{18,16},{20... | collective-permute-start | bytes 983048 | tf_op jit(solution)/shard_map/ppermute | solution.py:366
  136.3 1.7 carry_back.1
  138.0 12.7 %all-to-all-start.3 = ((f32[64,2,128]{2,1,0:T(2,128)}), f32[64,2,128]{2,1,0:T(2,128)S(1)}, u32[]{:S(2)}, u32[]{:S(2)}) async-start(f32[64,2,128]{2,1,0:T(2,128)} %bitcast.61), calls=%async_computation.3 | async-start | bytes 131072 | tf_op jit(solution)/shard_map/all_to_all | solution.py:317
  150.8 12.9 %all-to-all-done.3 = f32[64,2,128]{2,1,0:T(2,128)S(1)} async-done(((f32[64,2,128]{2,1,0:T(2,128)}), f32[64,2,128]{2,1,0:T(2,128)S(1)}, u32[]{:S(2)}, u32[]{:S(2)}) %all-to-all-start.3) | async-done | bytes 65568 | tf_op jit(solution)/shard_map/all_to_all | solution.py:317
  163.7 1.2 copy-done.5
  164.9 1.2 copy-done.11
  166.1 1.2 copy-done.13
  167.4 0.8 copy-done.28
  168.2 0.8 copy-done.30
  169.0 0.8 copy-done.32
  169.9 0.8 copy-done.34
  170.7 8.4 %finish.1 = (bf16[3,128,2048]{2,1,0:T(8,128)(2,1)}, f32[16,32,128]{2,1,0:T(8,128)S(1)}) custom-call(f32[8,16]{1,0:T(8,128)S(1)} %copy-done.26, f32[16,8,128]{2,1,0:T(8,128)S(1)} %bitcast.49, f32[128,2048]{1,0:T(8,128)S(1)} %copy-done.13, f32[128,2048]{1,0:T(8,128)S(1)} %copy-done.11, f32[128,2048]{1,0:T(8,128)S(1)} %get-tuple-element.38.k, ...), custom_call_target="tpu_custom_call" | custom-call | tf_op jit(solution)/shard_map/finish/pallas_call | solution.py:369
  179.1 25.6 %all_to_all.30.parts = f32[64,8,128]{2,1,0:T(8,128)} all-to-all(f32[64,8,128]{2,1,0:T(8,128)S(1)} %bitcast.52), channel_id=1, replica_groups=mesh['dp'=4,'ctx'=64,'mp'=2] {'ctx'}, dimensions={0} | all-to-all | bytes 524288 | tf_op jit(solution)/shard_map/all_to_all | solution.py:386
  204.7 1.6 add_parts.1
  206.4 10.9 %psum.15 = f32[8,128]{1,0:T(8,128)S(1)} all-reduce(f32[8,128]{1,0:T(8,128)} %add_parts.1), channel_id=1, replica_groups=mesh['dp'=4,'ctx'=64,'mp'=2] {'dp'}, use_global_device_ids=true, to_apply=%region_1.0 | all-reduce | flops 1024 | bytes 8192 | tf_op jit(solution)/shard_map/psum | solution.py:388
  217.2 23.8 %all_to_all.31 = f32[64,8,128]{2,1,0:T(8,128)} all-to-all(f32[64,8,128]{2,1,0:T(8,128)S(1)} %broadcast_in_dim.33), channel_id=1, replica_groups=mesh['dp'=4,'ctx'=64,'mp'=2] {'ctx'}, dimensions={0} | all-to-all | bytes 524288 | tf_op jit(solution)/shard_map/all_to_all | solution.py:389
  241.0 1.7 unpack.1
  242.7 0.7 slice_bitcast_fusion
  243.4 0.7 copy.15
  (65 shorter events, 1.5 us)
Async XLA Ops:
  0.6 80.1 %copy-start.21 = (f32[8,2048]{1,0:T(8,128)S(1)}, f32[8,2048]{1,0:T(8,128)}, u32[]{:S(2)}) copy-start(f32[8,2048]{1,0:T(8,128)} %weight.7) | copy-start | bytes 196612
  0.6 80.1 %copy-start.37 = (f32[2048]{0:T(1024)S(1)}, f32[2048]{0:T(1024)}, u32[]{:S(2)}) copy-start(f32[2048]{0:T(1024)} %param.12) | copy-start | bytes 24580
  1.6 14.4 %collective-permute-start = (bf16[3,8,2048]{2,1,0:T(8,128)(2,1)S(1)}, bf16[3,8,2048]{2,1,0:T(8,128)(2,1)S(1)}, u32[]{:S(2)}, u32[]{:S(2)}) collective-permute-start(bf16[3,8,2048]{2,1,0:T(8,128)(2,1)S(1)} %slice.24), channel_id=1, source_target_pairs={{0,2},{2,4},{4,6},{6,8},{8,10},{10,12},{12,14},{14,16},{16,18},{18... | collective-permute-start | bytes 294920 | tf_op jit(solution)/shard_map/ppermute | solution.py:288
  6.1 53.0 %copy-start.24 = (f32[8,16]{1,0:T(8,128)}, f32[8,16]{1,0:T(8,128)S(1)}, u32[]{:S(2)}) copy-start(f32[8,16]{1,0:T(8,128)S(1)} %get-tuple-element.73.rate) | copy-start | bytes 1540
  16.0 1.4 copy-start
  17.4 0.9 copy-start.18
  18.4 0.8 copy-start.20
  19.2 0.7 copy-start.38
  19.9 60.9 %copy-start.8 = (bf16[1,128,2048]{2,1,0:T(8,128)(2,1)S(1)}, bf16[1,128,2048]{2,1,0:T(8,128)(2,1)}, u32[]{:S(2)}) copy-start(bf16[1,128,2048]{2,1,0:T(8,128)(2,1)} %param.13) | copy-start | bytes 1572868
  28.9 1.0 copy-start.2
  29.8 1.0 copy-start.14
  30.8 3.3 %copy-start.40 = (f32[8,128,2048]{2,1,0:T(8,128)}, f32[8,128,2048]{2,1,0:T(8,128)S(1)}, u32[]{:S(2)}) copy-start(f32[8,128,2048]{2,1,0:T(8,128)S(1)} %get-tuple-element.44.states) | copy-start | bytes 25165828
  34.1 51.2 %copy-start.6 = (f32[128,2048]{1,0:T(8,128)}, f32[128,2048]{1,0:T(8,128)S(1)}, u32[]{:S(2)}) copy-start(f32[128,2048]{1,0:T(8,128)S(1)} %get-tuple-element.33.q) | copy-start | bytes 3145732
  34.1 25.0 %all-to-all-start = ((f32[64,2,128]{2,1,0:T(2,128)}), f32[64,2,128]{2,1,0:T(2,128)S(1)}, u32[]{:S(2)}, u32[]{:S(2)}) async-start(f32[64,2,128]{2,1,0:T(2,128)} %bitcast.8), calls=%async_computation | async-start | bytes 131072 | tf_op jit(solution)/shard_map/all_to_all | solution.py:309
  59.1 0.6 copy-start.44
  61.5 19.3 %all-to-all-start.1 = ((f32[64,2,128]{2,1,0:T(2,128)}), f32[64,2,128]{2,1,0:T(2,128)S(1)}, u32[]{:S(2)}, u32[]{:S(2)}) async-start(f32[64,2,128]{2,1,0:T(2,128)} %bitcast.60), calls=%async_computation.1 | async-start | bytes 131072 | tf_op jit(solution)/shard_map/all_to_all | solution.py:317
  80.8 1.2 copy-start.15
  85.4 1.0 copy-start.16
  88.8 1.2 copy-start.3
  90.0 1.2 copy-start.7
  91.2 1.2 copy-start.17
  92.4 15.2 %copy-start.1 = (bf16[1,128,3,2048]{3,1,2,0:T(8,128)(2,1)S(1)}, bf16[1,128,3,2048]{3,1,2,0:T(8,128)(2,1)}, u32[]{:S(2)}) copy-start(bf16[1,128,3,2048]{3,1,2,0:T(8,128)(2,1)} %param.7) | copy-start | bytes 4718596
  92.5 15.2 %copy-start.25 = (f32[8,16]{1,0:T(8,128)S(1)}, f32[8,16]{1,0:T(8,128)}, u32[]{:S(2)}) copy-start(f32[8,16]{1,0:T(8,128)} %copy-done.24) | copy-start | bytes 1540
  92.5 15.2 %copy-start.39 = (f32[2048]{0:T(1024)S(1)}, f32[2048]{0:T(1024)}, u32[]{:S(2)}) copy-start(f32[2048]{0:T(1024)} %param.11) | copy-start | bytes 24580
  96.4 1.0 copy-start.9
  97.4 0.6 copy-start.22
  98.0 1.0 copy-start.42
  99.0 37.3 %all-to-all-start.2 = ((f32[64,2,128]{2,1,0:T(2,128)}), f32[64,2,128]{2,1,0:T(2,128)}, u32[]{:S(2)}, u32[]{:S(2)}) async-start(f32[64,2,128]{2,1,0:T(2,128)} %bitcast.53), calls=%async_computation.2 | async-start | bytes 131072 | tf_op jit(solution)/shard_map/all_to_all | solution.py:309
  107.6 1.2 copy-start.4
  108.9 1.2 copy-start.10
  110.1 0.8 copy-start.23
  110.9 0.8 copy-start.35
  111.8 0.8 copy-start.36
  112.6 3.4 %copy-start.41 = (f32[8,128,2048]{2,1,0:T(8,128)S(1)}, f32[8,128,2048]{2,1,0:T(8,128)}, u32[]{:S(2)}) copy-start(f32[8,128,2048]{2,1,0:T(8,128)} %copy-done.40) | copy-start | bytes 25165828
  116.0 1.2 copy-start.43
  117.2 46.5 %copy-start.19 = (f32[7,3,2048]{2,0,1:T(8,128)S(1)}, f32[7,3,2048]{2,0,1:T(8,128)}, u32[]{:S(2)}) copy-start(f32[7,3,2048]{2,0,1:T(8,128)} %param.8) | copy-start | bytes 516100
  117.2 46.5 %copy-start.26 = (f32[8,16]{1,0:T(8,128)S(1)}, f32[8,16]{1,0:T(8,128)}, u32[]{:S(2)}) copy-start(f32[8,16]{1,0:T(8,128)} %copy-done.24) | copy-start | bytes 1540
  126.6 0.6 copy-start.31
  127.3 0.6 copy-start.33
  127.9 2.9 %copy-start.27 = (f32[8,2048]{1,0:T(8,128)}, f32[8,2048]{1,0:T(8,128)S(1)}, u32[]{:S(2)}) copy-start(f32[8,2048]{1,0:T(8,128)S(1)} %get-tuple-element.49.res) | copy-start | bytes 196612
  127.9 2.9 %copy-start.29 = (f32[8,2048]{1,0:T(8,128)}, f32[8,2048]{1,0:T(8,128)S(1)}, u32[]{:S(2)}) copy-start(f32[8,2048]{1,0:T(8,128)S(1)} %get-tuple-element.46.loc) | copy-start | bytes 196612
  128.6 1.0 copy-start.12
  131.4 19.3 %collective-permute-start.1 = (f32[5,8,2048]{2,1,0:T(8,128)}, f32[5,8,2048]{2,1,0:T(8,128)S(1)}, u32[]{:S(2)}, u32[]{:S(2)}) collective-permute-start(f32[5,8,2048]{2,1,0:T(8,128)} %bitcast_dynamic-update-slice_fusion), channel_id=1, source_target_pairs={{2,0},{4,2},{6,4},{8,6},{10,8},{12,10},{14,12},{16,14},{18,16},{20... | collective-permute-start | bytes 983048 | tf_op jit(solution)/shard_map/ppermute | solution.py:366
  138.0 25.7 %all-to-all-start.3 = ((f32[64,2,128]{2,1,0:T(2,128)}), f32[64,2,128]{2,1,0:T(2,128)S(1)}, u32[]{:S(2)}, u32[]{:S(2)}) async-start(f32[64,2,128]{2,1,0:T(2,128)} %bitcast.61), calls=%async_computation.3 | async-start | bytes 131072 | tf_op jit(solution)/shard_map/all_to_all | solution.py:317
  163.7 1.2 copy-start.5
  164.9 1.2 copy-start.11
  166.1 1.2 copy-start.13
  167.4 0.8 copy-start.28
  168.2 0.8 copy-start.30
  169.0 0.8 copy-start.32
  169.9 0.8 copy-start.34

commit v2 on v1

v2 whole, which is shorter than its diff:
```python
import functools
import jax
import jax.numpy as jnp
from jax import lax
from jax.experimental import pallas as pl
from jax.experimental.pallas import tpu as pltpu
from jax.sharding import Mesh
from jax.sharding import PartitionSpec as P

D = 4096
EPSILON = 1e-06
HIGHEST = lax.Precision.HIGHEST
F32 = jnp.float32
BF16 = jnp.bfloat16
L = 128
GS = 128
POLES = 8
TAPS = 7
PAD = 8
GB = 2
ROWS = 32
VMEM_MIB = 53
CTX = ("x", "z")
YX = ("y", "x")


def params(mib):
    return pltpu.CompilerParams(vmem_limit_bytes=mib * 1024 * 1024)


def iota(shape, dim):
    return lax.broadcasted_iota(jnp.int32, shape, dim)


def ones_tri(lower):
    row = iota((L, 2 * L), 0)
    col = iota((L, 2 * L), 1) % L
    keep = col <= row if lower else col >= row
    return jnp.where(keep, 1.0, 0.0).astype(BF16)


def split(x):
    high = x.astype(BF16)
    low = (x - high.astype(F32)).astype(BF16)
    return jnp.concatenate([high, low], axis=0)


def tri_dot(tri, xs):
    return jnp.dot(tri, jnp.concatenate([split(x) for x in xs], axis=1), preferred_element_type=F32)


def rowsum(x):
    return jnp.sum(x, axis=0, keepdims=True)


def fill_ext(ext, feat, halo, cs):
    for j in range(3):
        ext[j, 0:PAD, :] = halo[j, :, cs].astype(F32)
        ext[j, PAD : PAD + L, :] = feat[j, :, cs].astype(F32)


def filtered(j, taps, feat, halo, cs, ext):
    ext[j, 0:PAD, :] = halo[j, :, cs].astype(F32)
    ext[j, PAD : PAD + L, :] = feat[j, :, cs].astype(F32)
    acc = taps[j, 0:1, cs] * ext[j, PAD : PAD + L, :]
    for k in range(1, TAPS):
        acc = acc + taps[j, k : k + 1, cs] * ext[j, pl.ds(PAD - k, L), :]
    return acc


def two_parts(table):
    high = table.astype(BF16).astype(F32)
    both = jnp.concatenate([high, table - high], axis=0)
    return jnp.concatenate([both, both], axis=1).astype(BF16)


def weighted_rows(table, x):
    both = jnp.dot(two_parts(table), split(x), preferred_element_type=F32)
    return both[0:POLES, :] + both[POLES : 2 * POLES, :]


def lane_place():
    return iota((POLES, L), 1).astype(F32)


def spread_poles(lane_rate, sign, rows):
    lane = iota((L, 4 * POLES), 1)
    place = iota((L, 4 * POLES), 0).astype(F32)
    steps = place + 1.0 if sign > 0 else L - 1.0 - place
    table = jnp.exp(-steps * lane_rate[:, 0 : 4 * POLES])
    high = table.astype(BF16).astype(F32)
    left = jnp.where((lane // POLES) % 2 == 0, high, table - high).astype(BF16)
    top = rows.astype(BF16).astype(F32)
    low = rows - top
    right = jnp.concatenate([top, top, low, low], axis=0).astype(BF16)
    return jnp.dot(left, right, preferred_element_type=F32)


def ends_kernel(by_pole, feat, halo, taps, k_o, v_o, e_o, edge_o, ext):
    for gi in range(GB):
        cs = slice(gi * GS, (gi + 1) * GS)
        key = filtered(1, taps, feat, halo, cs, ext)
        value = filtered(2, taps, feat, halo, cs, ext)
        k_o[:, cs] = key
        v_o[:, cs] = value
        edge_o[0, :, cs] = key[0:PAD, :]
        edge_o[1, :, cs] = value[0:PAD, :]
        e_o[gi] = weighted_rows(jnp.exp(-by_pole[gi] * (L - 1.0 - lane_place())), key * value)


def states_kernel(rate, feat, halo, taps, k, v, weight, skip, q_o, bl_o, s_o, ext):
    first = pl.program_id(0) * GB
    tri = ones_tri(True)
    place = iota((L, GS), 0).astype(F32)
    for gi in range(GB):
        cs = slice(gi * GS, (gi + 1) * GS)
        q_o[:, cs] = filtered(0, taps, feat, halo, cs, ext)
        prod = k[:, cs] * v[:, cs]
        modal = skip[0:1, cs] * prod
        for p in range(0, POLES, 2):
            rates = [rate[p + i, first + gi] for i in range(2)]
            both = tri_dot(tri, [jnp.exp(place * r) * prod for r in rates])
            for i, r in enumerate(rates):
                state = jnp.exp(place * (-r)) * both[:, i * GS : (i + 1) * GS]
                s_o[p + i, :, cs] = state
                modal = modal + weight[p + i : p + i + 1, cs] * state
        bl_o[:, cs] = modal


def coefs_kernel(by_pole, k, v, feat, halo, c_o, ext):
    for gi in range(GB):
        cs = slice(gi * GS, (gi + 1) * GS)
        fill_ext(ext, feat, halo, cs)
        table = two_parts(jnp.exp(-by_pole[gi] * (L - 1.0 - lane_place())))
        for j, other in ((1, v[:, cs]), (2, k[:, cs])):
            xs = [split(other * ext[j, pl.ds(PAD - t, L), :]) for t in range(TAPS)]
            both = jnp.dot(table, jnp.concatenate(xs, axis=1), preferred_element_type=F32)
            both = both[0:POLES, :] + both[POLES : 2 * POLES, :]
            for t in range(TAPS):
                at = POLES * (TAPS * (j - 1) + t)
                c_o[gi, at : at + POLES, :] = both[:, t * GS : (t + 1) * GS]


def scan_kernel(back, rate, where, rows, out):
    me = where[0]
    group = me // 4
    pole = 2 * (me % 4)
    low, high = rate[pole, group], rate[pole + 1, group]
    row, col = iota((L, L), 0), iota((L, L), 1)
    lag = col // 2 - row // 2 - 1 if back else row // 2 - col // 2 - 1
    keep = (lag >= 0) & (row % 2 == col % 2)
    own = jnp.where(row % 2 == 0, low, high)
    decay = jnp.where(keep, jnp.exp(-(own * L) * jnp.maximum(lag, 0).astype(F32)), 0.0)
    out[...] = jnp.dot(decay, rows[...], precision=HIGHEST, preferred_element_type=F32)


def branch_kernel(q, bl, cot, gain, state_in, by_lane, weight, br_o, stats_o, acc):
    step = pl.program_id(0)

    @pl.when(step == 0)
    def _():
        acc[...] = jnp.zeros_like(acc)

    for gi in range(GB):
        cs = slice(gi * GS, (gi + 1) * GS)
        branch = bl[:, cs] + spread_poles(by_lane[gi], 1, weight[:, cs] * state_in[gi])
        br_o[:, cs] = branch
        gated = q[:, cs] * branch
        acc[0] += gated * gated
        acc[1] += (gain[0:1, cs] * cot[:, cs].astype(F32)) * gated

    @pl.when(step == pl.num_programs(0) - 1)
    def _():
        row = iota((8, L), 0)
        squares = rowsum(acc[0].T)
        slopes = rowsum(acc[1].T)
        stats_o[...] = jnp.where(row == 0, squares, jnp.where(row == 1, slopes, 0.0))


def down(row):
    return jnp.broadcast_to(row, (L, L)).T


def gate_kernel(stats, q, br, cot, gain, by_pole, g_o, back_o, edge_o):
    inv_row = lax.rsqrt(stats[0:1, :] / D + EPSILON)
    inv = down(inv_row)
    pull = down(stats[1:2, :] * inv_row * inv_row * inv_row / D)
    for gi in range(GB):
        cs = slice(gi * GS, (gi + 1) * GS)
        query, branch = q[:, cs], br[:, cs]
        dgated = (gain[0:1, cs] * cot[:, cs].astype(F32)) * inv - (query * branch) * pull
        dbranch = dgated * query
        g_o[:, cs] = dbranch
        back = weighted_rows(jnp.exp(-by_pole[gi] * (lane_place() + 1.0)), dbranch)
        back_o[gi] = back
        edge_o[0, :, cs] = dgated[0:PAD, :] * branch[0:PAD, :]
        edge_o[1, :, cs] = back


def adjoint_kernel(
    rate, by_pole, g, k, v, states, weight, skip, state_in, back, edge,
    dpl_o, res_o, loc_o, mix_o, edge_o,
):
    first = pl.program_id(0) * GB
    tri = ones_tri(False)
    place = iota((L, GS), 0).astype(F32)
    centre = place - (L - 1) / 2
    lane = lane_place()
    for gi in range(GB):
        cs = slice(gi * GS, (gi + 1) * GS)
        dbranch = g[:, cs]
        prod = k[:, cs] * v[:, cs]
        total = skip[0:1, cs] * dbranch
        far_grad = centre * dbranch
        far_prod = centre * prod
        own_in = state_in[gi]
        own_rate = by_pole[gi]
        once = jnp.exp(-own_rate)
        residue = own_in * back[gi]
        heavy = weighted_rows((lane + 1.0) * jnp.exp(-own_rate * lane), dbranch)
        deep = weighted_rows((L - 1.0 - lane) * jnp.exp(-own_rate * (L - 2.0 - lane)), prod)
        mix_o[gi] = once * (deep + L * jnp.exp(-(L - 1) * own_rate) * own_in)
        loc = once * own_in * heavy
        for p in range(0, POLES, 2):
            rates = [rate[p + i, first + gi] for i in range(2)]
            both = tri_dot(tri, [jnp.exp(place * (-r)) * dbranch for r in rates])
            for i, r in enumerate(rates):
                at = slice(p + i, p + i + 1)
                adjoint = jnp.exp(place * r) * both[:, i * GS : (i + 1) * GS]
                total = total + weight[at, cs] * adjoint
                res_o[gi, at, :] = residue[at, :] + rowsum(prod * adjoint)
                loc_o[gi, at, :] = loc[at, :] + rowsum(far_grad * states[p + i, :, cs] - far_prod * adjoint)
        dpl_o[:, cs] = total
        edge_o[0, :, cs] = edge[0, :, cs]
        edge_o[1, :, cs] = total[0:PAD, :]
        edge_o[2, :, cs] = edge[1, :, cs]


def outs_kernel(
    stats, q, br, cot, gain, k, v, g, dpl, res, feat, halo, out_o, dq_o, pack_o, ext,
):
    inv_row = lax.rsqrt(stats[0:1, :] / D + EPSILON)
    inv = down(inv_row)
    pull = down(stats[1:2, :] * inv_row * inv_row * inv_row / D)
    for gi in range(GB):
        cs = slice(gi * GS, (gi + 1) * GS)
        fill_ext(ext, feat, halo, cs)
        query, branch, key, value = q[:, cs], br[:, cs], k[:, cs], v[:, cs]
        grad = cot[:, cs].astype(F32)
        gated = query * branch
        normed = gated * inv
        out_o[:, cs] = (gain[0:1, cs] * normed).astype(BF16)
        dquery = ((gain[0:1, cs] * grad) * inv - gated * pull) * branch
        dq_o[:, cs] = dquery
        local_prod = dpl[:, cs]
        for j, own in enumerate((dquery, local_prod * value, local_prod * key)):
            for t in range(TAPS):
                at = TAPS * j + t
                pack_o[gi, at : at + 1, :] = rowsum(own * ext[j, pl.ds(PAD - t, L), :])
        pack_o[gi, 21:29, :] = res[gi]
        pack_o[gi, 29:30, :] = rowsum(g[:, cs] * (key * value))
        pack_o[gi, 30:31, :] = rowsum(grad * normed)
        pack_o[gi, 31:32, :] = jnp.zeros((1, GS), F32)


def sums_kernel(later, by_pole, weight, loc, mix, coefs, pack, pack_o):
    lane, sub = iota((POLES, GS), 1), iota((POLES, GS), 0)
    for gi in range(GB):
        cs = slice(gi * GS, (gi + 1) * GS)
        coming = later[gi]
        scaled = weight[:, cs] * coming
        pack_o[gi] = pack[gi]
        for i in range(2 * TAPS):
            at = TAPS + i
            more = rowsum(scaled * coefs[gi, POLES * i : POLES * (i + 1), :])
            pack_o[gi, at : at + 1, :] = pack[gi, at : at + 1, :] + more
        inner = jnp.sum(weight[:, cs] * (loc[gi] + coming * mix[gi]), axis=1, keepdims=True)
        pack_o[gi, 31:32, :] = rowsum(jnp.where(lane == sub, -by_pole[gi] * inner, 0.0))


def finish_kernel(rate, later, by_lane, dpl, dq, k, v, weight, rim, near, taps, grad_o, dext):
    first = pl.program_id(0) * GB
    ahead = (iota((PAD, GS), 0) + 1).astype(F32)
    for gi in range(GB):
        cs = slice(gi * GS, (gi + 1) * GS)
        coming = later[gi]
        dprod = dpl[:, cs] + spread_poles(by_lane[gi], -1, weight[:, cs] * coming)
        dext[0, 0:L, :] = dq[:, cs]
        dext[1, 0:L, :] = dprod * v[:, cs]
        dext[2, 0:L, :] = dprod * k[:, cs]
        beyond = weight[:, cs] * (coming - rim[2, :, cs])
        next_prod = rim[1, :, cs]
        for p in range(POLES):
            next_prod = next_prod + jnp.exp(ahead * rate[p, first + gi]) * beyond[p : p + 1, :]
        dext[0, L : L + PAD, :] = rim[0, :, cs]
        dext[1, L : L + PAD, :] = next_prod * near[1, :, cs]
        dext[2, L : L + PAD, :] = next_prod * near[0, :, cs]
        for j in range(3):
            acc = taps[j, 0:1, cs] * dext[j, 0:L, :]
            for t in range(1, TAPS):
                acc = acc + taps[j, t : t + 1, cs] * dext[j, pl.ds(t, L), :]
            grad_o[j, :, cs] = acc.astype(BF16)


def unpack_kernel(pack, conv_o, rate_o, res_o, skip_o, gain_o):
    groups = pack.shape[0]
    for gi in range(groups):
        cs = slice(gi * GS, (gi + 1) * GS)
        for j in range(3):
            conv_o[j, :, cs] = pack[gi, TAPS * j : TAPS * j + TAPS, :]
        res_o[:, cs] = pack[gi, 21:29, :]
        skip_o[0:1, cs] = pack[gi, 29:30, :]
        gain_o[0:1, cs] = pack[gi, 30:31, :]
        rate_o[gi : gi + 1, :] = pack[gi, 31:32, :]


def smem():
    return pl.BlockSpec(memory_space=pltpu.SMEM)


def cols(*lead):
    return pl.BlockSpec((*lead, GB * GS), lambda i: (0,) * len(lead) + (i,))


def groups_of(rows):
    return pl.BlockSpec((GB, rows, GS), lambda i: (i, 0, 0))


def shape(*dims, dtype=F32):
    return jax.ShapeDtypeStruct(dims, dtype)


def shifted(value, step):
    pairs = [(i, i + step) for i in range(64) if 0 <= i + step < 64]
    return lax.ppermute(value, CTX, pairs)


def local(features, conv_weight, log_rate, residues, skip_weight, norm_gain, cotangent):
    feat = features[0].transpose(1, 0, 2)
    taps = conv_weight.transpose(1, 0, 2)
    cot = cotangent[0]
    channels = feat.shape[2]
    groups = log_rate.shape[1]
    count = lax.axis_size(CTX)
    skip = skip_weight[None]
    gain = norm_gain[None]
    where = lax.axis_index(CTX).astype(jnp.int32)[None]

    def call(kernel, ins, outs, args, scratch=(), flops=0, moved=0, special=0):
        return pl.pallas_call(
            kernel,
            grid=(groups // GB,),
            in_specs=ins,
            out_specs=[o[0] for o in outs],
            out_shape=[o[1] for o in outs],
            scratch_shapes=[pltpu.VMEM(d, F32) for d in scratch],
            compiler_params=params(VMEM_MIB),
            cost_estimate=pl.CostEstimate(flops=flops, bytes_accessed=moved, transcendentals=special),
            name=kernel.__name__,
        )(*args)

    wide = (cols(L), shape(L, channels))
    per_pole = (groups_of(POLES), shape(groups, POLES, GS))
    ext3 = (3, PAD + L, GS)

    halo = shifted(feat[:, L - PAD :], 1)
    rate = jnp.exp(log_rate)
    by_pole = jnp.broadcast_to(rate.T[:, :, None], (groups, POLES, GS))
    by_lane = jnp.tile(rate.T, (1, GS // POLES))[:, None, :]
    poles, lanes = groups_of(POLES), groups_of(1)

    key, value, ends, edge = call(
        ends_kernel,
        [poles, cols(3, L), cols(3, PAD), cols(3, TAPS)],
        [wide, wide, per_pole, (cols(2, PAD), shape(2, PAD, channels))],
        (by_pole, feat, halo, taps),
        [ext3],
    )
    near = shifted(edge, -1)

    def carried(rows, back):
        sent = lax.all_to_all(rows.reshape(count, 2, GS), CTX, 0, 0)
        summed = pl.pallas_call(
            functools.partial(scan_kernel, back),
            in_specs=[smem(), smem(), pl.BlockSpec((L, GS), lambda: (0, 0))],
            out_specs=pl.BlockSpec((L, GS), lambda: (0, 0)),
            out_shape=shape(L, GS),
            compiler_params=params(16),
            name="carry_back" if back else "carry_on",
        )(rate, where, sent.reshape(L, GS))
        given = lax.all_to_all(summed.reshape(count, 2, GS), CTX, 0, 0)
        return given.reshape(groups, POLES, GS)

    state_in = carried(ends, False)

    query, base, states = call(
        states_kernel,
        [smem(), cols(3, L), cols(3, PAD), cols(3, TAPS), cols(L), cols(L), cols(POLES), cols(1)],
        [wide, wide, (cols(POLES, L), shape(POLES, L, channels))],
        (rate, feat, halo, taps, key, value, residues, skip),
        [ext3],
        flops=4_000_000_000,
        moved=14_000_000,
        special=4_000_000,
    )
    coefs = call(
        coefs_kernel,
        [poles, cols(L), cols(L), cols(3, L), cols(3, PAD)],
        [(groups_of(2 * TAPS * POLES), shape(groups, 2 * TAPS * POLES, GS))],
        (by_pole, key, value, feat, halo),
        [ext3],
        flops=4_000_000_000,
        moved=4_000_000,
    )[0]

    branch, stats = call(
        branch_kernel,
        [cols(L), cols(L), cols(L), cols(1), poles, lanes, cols(POLES)],
        [wide, (pl.BlockSpec((8, L), lambda i: (0, 0)), shape(8, L))],
        (query, base, cot, gain, state_in, by_lane, residues),
        [(2, L, GS)],
    )
    stats = lax.psum(stats, "c")
    small = pl.BlockSpec((8, L), lambda i: (0, 0))

    dbranch, back_in, edge = call(
        gate_kernel,
        [small] + [cols(L)] * 3 + [cols(1), poles],
        [wide, per_pole, (cols(2, PAD), shape(2, PAD, channels))],
        (stats, query, branch, cot, gain, by_pole),
    )
    later = carried(back_in, True)

    dlocal, res_part, loc_part, mix_part, edge = call(
        adjoint_kernel,
        [smem(), poles] + [cols(L)] * 3 + [cols(POLES, L), cols(POLES), cols(1), poles, poles, cols(2, PAD)],
        [wide, per_pole, per_pole, per_pole, (cols(3, PAD), shape(3, PAD, channels))],
        (rate, by_pole, dbranch, key, value, states, residues, skip, state_in, back_in, edge),
        flops=6_000_000_000,
        moved=16_000_000,
        special=4_000_000,
    )
    rim = shifted(edge, -1)

    block_out, dquery, pack = call(
        outs_kernel,
        [small] + [cols(L)] * 3 + [cols(1)] + [cols(L)] * 4 + [poles, cols(3, L), cols(3, PAD)],
        [(cols(L), shape(L, channels, dtype=BF16)), wide, (groups_of(ROWS), shape(groups, ROWS, GS))],
        (stats, query, branch, cot, gain, key, value, dbranch, dlocal, res_part, feat, halo),
        [ext3],
        flops=1_000_000_000,
        moved=10_000_000,
    )
    pack = call(
        sums_kernel,
        [poles, poles, cols(POLES), poles, poles, groups_of(2 * TAPS * POLES), groups_of(ROWS)],
        [(groups_of(ROWS), shape(groups, ROWS, GS))],
        (later, by_pole, residues, loc_part, mix_part, coefs, pack),
    )[0]
    feature_grad = call(
        finish_kernel,
        [smem(), poles, lanes] + [cols(L)] * 4 + [cols(POLES), cols(3, PAD), cols(2, PAD), cols(3, TAPS)],
        [(cols(3, L), shape(3, L, channels, dtype=BF16))],
        (rate, later, by_lane, dlocal, dquery, key, value, residues, rim, near, taps),
        [ext3],
        flops=1_000_000_000,
        moved=10_000_000,
    )[0]

    parts = lax.all_to_all(pack, YX, 0, 0)
    mine = lax.psum(jnp.sum(parts, axis=0), "z")
    totals = lax.all_to_all(jnp.broadcast_to(mine[None], (groups, ROWS, GS)), YX, 0, 0)
    conv, rate_grad, res, skip_grad, gain_grad = pl.pallas_call(
        unpack_kernel,
        out_shape=[shape(3, TAPS, channels), shape(groups, GS), shape(POLES, channels)] + [shape(1, channels)] * 2,
        compiler_params=params(16),
        name="unpack",
    )(totals)
    return (
        block_out[None],
        feature_grad.transpose(1, 0, 2)[None],
        conv.transpose(1, 0, 2),
        rate_grad[:, :POLES].T,
        res,
        skip_grad[0],
        gain_grad[0],
    )


def solution(mesh):
    split_mesh = Mesh(mesh.devices.reshape(4, 4, 16, 2), ("y", "x", "z", "c"))
    in_specs = (
        P("y", CTX, None, "c"),
        P(None, None, "c"),
        P(None, "c"),
        P(None, "c"),
        P("c"),
        P("c"),
        P("y", CTX, "c"),
    )
    out_specs = (
        P("y", CTX, "c"),
        P("y", CTX, None, "c"),
        P(None, None, "c"),
        P(None, "c"),
        P(None, "c"),
        P("c"),
        P("c"),
    )
    return jax.shard_map(local, mesh=split_mesh, in_specs=in_specs, out_specs=out_specs, check_vma=False)
```

time: 246 us -> 238 us (0.967)
  local copies, waits for them, and re-layouts: 43.4 us -> 4.22 us
  Pallas kernels: 40.8 us -> 71.2 us
  starting transfers between devices: 47 us -> 65.1 us
  waiting for transfers between devices: 47.9 us -> 36.5 us
  blocking collectives: 62.7 us -> 58.3 us
    all_to_all x2 -> x0, blocking collectives: 49.4 us -> none  [the longest x1 25.6 us: local(): parts = lax.all_to_all(pack.reshape(count, share, GS), 'ctx', 0, 0)]
    psum x2, blocking collectives: 13.3 us -> 58.3 us  [the longest x1 55.9 us: local(): mine = lax.psum(jnp.sum(parts, axis=0), 'z')]
    unnamed x95 -> x13, local copies, waits for them, and re-layouts: 41.1 us -> 1.62 us
    pallas_call x6 -> x9, Pallas kernels: 35.7 us -> 67.6 us  [call(): pl.pallas_call(kernel, grid=(groups // GB,), in_specs=ins, out_specs=[o[0...]
    all_to_all x4 -> x6, waiting for transfers between devices: 37.9 us -> 23.1 us  [the longest x2 18.8 us: carried(): sent = lax.all_to_all(rows.reshape(count, 2, GS), CTX, 0, 0)]
    all_to_all x4 -> x6, starting transfers between devices: 38.3 us -> 53 us  [the longest x2 24.2 us: carried(): sent = lax.all_to_all(rows.reshape(count, 2, GS), CTX, 0, 0)]
    ppermute x2 -> x3, waiting for transfers between devices: 9.93 us -> 13.4 us  [shifted(): return lax.ppermute(value, CTX, pairs)]
    ppermute x2 -> x3, starting transfers between devices: 8.67 us -> 12.1 us  [shifted(): return lax.ppermute(value, CTX, pairs)]
  transfers between devices with their start and end apart: 6 -> 9, of which waited for: 4 -> 6; matrix products, arithmetic and copies ran while one was open for 2% -> 1% of each run, Pallas kernels for 5% -> 18%
where the time goes in v2:
time: 238 us; the launch traced here: 236 us
  Pallas kernels  71.2 us (30%)
  starting transfers between devices  65.1 us (27%)
  blocking collectives  58.3 us (24%)
  waiting for transfers between devices  36.5 us (15%)
  local copies, waits for them, and re-layouts  4.22 us (2%)
    pallas_call x9, Pallas kernels, call(): pl.pallas_call(kernel, grid=(groups // GB,), in_specs=ins, out_specs=[o[0...  67.6 us
    psum x1, blocking collectives, local(): mine = lax.psum(jnp.sum(parts, axis=0), 'z')  55.9 us
    all_to_all x2, starting transfers between devices, carried(): sent = lax.all_to_all(rows.reshape(count, 2, GS), CTX, 0, 0)  24.2 us
    all_to_all x2, waiting for transfers between devices, carried(): sent = lax.all_to_all(rows.reshape(count, 2, GS), CTX, 0, 0)  18.8 us
    all_to_all x2, starting transfers between devices, carried(): given = lax.all_to_all(summed.reshape(count, 2, GS), CTX, 0, 0)  15.6 us
    ppermute x3, waiting for transfers between devices, shifted(): return lax.ppermute(value, CTX, pairs)  13.4 us
    ppermute x3, starting transfers between devices, shifted(): return lax.ppermute(value, CTX, pairs)  12.1 us
    all_to_all x1, starting transfers between devices, local(): parts = lax.all_to_all(pack, YX, 0, 0)  7.34 us
  transfers between devices with their start and end apart: 9, of which 6 were waited for; matrix products, arithmetic and copies ran while one was open for 1% of the time, Pallas kernels for 18%

profile of v2, /device:TPU:6, one launch (start us, length us, event | category | flops | bytes accessed | tf_op | source)
XLA Modules:
  0.0 236.1 jit_solution(3252472396280699204)
XLA Ops:
  0.6 0.0 copy-start.2
  0.6 0.0 copy-start.5
  0.7 0.0 copy-start.3
  0.7 0.9 slice.8
  1.6 3.8 %collective-permute-start = (bf16[3,8,2048]{2,1,0:T(8,128)(2,1)S(1)}, bf16[3,8,2048]{2,1,0:T(8,128)(2,1)S(1)}, u32[]{:S(2)}, u32[]{:S(2)}) collective-permute-start(bf16[3,8,2048]{2,1,0:T(8,128)(2,1)S(1)} %slice.8), channel_id=1, source_target_pairs={{0,2},{2,4},{4,6},{6,8},{8,10},{10,12},{12,14},{14,16},{16,18},{18... | collective-permute-start | bytes 294920 | tf_op jit(solution)/shard_map/ppermute | solution.py:335
  5.4 0.7 exponential_bitcast_fusion
  6.1 0.1 copy.17
  6.2 9.9 %collective-permute-done.halo = bf16[3,8,2048]{2,1,0:T(8,128)(2,1)S(1)} collective-permute-done((bf16[3,8,2048]{2,1,0:T(8,128)(2,1)S(1)}, bf16[3,8,2048]{2,1,0:T(8,128)(2,1)S(1)}, u32[]{:S(2)}, u32[]{:S(2)}) %collective-permute-start) | collective-permute-done | bytes 98336 | tf_op jit(solution)/shard_map/ppermute | solution.py:335
  16.1 0.1 broadcast_in_dim.27.by_pole
  16.1 0.0 copy-start.1
  16.1 0.9 copy-done.1
  17.1 6.3 %ends_kernel.1 = (f32[128,2048]{1,0:T(8,128)}, f32[128,2048]{1,0:T(8,128)}, f32[16,8,128]{2,1,0:T(8,128)}, f32[2,8,2048]{2,1,0:T(8,128)S(1)}) custom-call(f32[16,8,128]{2,1,0:T(8,128)S(1)} %broadcast_in_dim.27.by_pole, bf16[3,128,2048]{2,1,0:T(8,128)(2,1)} %bitcast.47, bf16[3,8,2048]{2,1,0:T(8,128)(2,1)S(1)} %collective-permute-done.halo, ...), custom_call_target="tpu_custom_call" | custom-call | tf_op jit(solution)/shard_map/ends_kernel/pallas_call | solution.py:350
  23.4 12.1 %all-to-all-start = ((f32[64,2,128]{2,1,0:T(2,128)}), f32[64,2,128]{2,1,0:T(2,128)S(1)}, u32[]{:S(2)}, u32[]{:S(2)}) async-start(f32[64,2,128]{2,1,0:T(2,128)} %bitcast.9), calls=%async_computation | async-start | bytes 131072 | tf_op jit(solution)/shard_map/all_to_all | solution.py:382
  35.5 0.1 copy.18.by_lane
  35.5 12.9 %all-to-all-done = f32[64,2,128]{2,1,0:T(2,128)S(1)} async-done(((f32[64,2,128]{2,1,0:T(2,128)}), f32[64,2,128]{2,1,0:T(2,128)S(1)}, u32[]{:S(2)}, u32[]{:S(2)}) %all-to-all-start) | async-done | bytes 65568 | tf_op jit(solution)/shard_map/all_to_all | solution.py:382
  48.4 1.5 carry_on.1
  49.8 6.4 %all-to-all-start.1 = ((f32[64,2,128]{2,1,0:T(2,128)}), f32[64,2,128]{2,1,0:T(2,128)S(1)}, u32[]{:S(2)}, u32[]{:S(2)}) async-start(f32[64,2,128]{2,1,0:T(2,128)} %bitcast.11), calls=%async_computation.1 | async-start | bytes 131072 | tf_op jit(solution)/shard_map/all_to_all | solution.py:391
  56.2 0.0 copy-done.2
  56.2 0.0 copy-done.5
  56.2 0.0 copy-done.3
  56.2 0.0 copy-start
  56.2 0.0 copy-start.4
  56.3 9.9 %states_kernel.1 = (f32[128,2048]{1,0:T(8,128)}, f32[128,2048]{1,0:T(8,128)}, f32[8,128,2048]{2,1,0:T(8,128)}) custom-call(f32[8,16]{1,0:T(8,128)S(1)} %get-tuple-element.72.rate, bf16[3,128,2048]{2,1,0:T(8,128)(2,1)} %bitcast.48, bf16[3,8,2048]{2,1,0:T(8,128)(2,1)S(1)} %collective-permute-done.halo, f32[3,7,2048]{2,1,0:T(8,128)S(1)} %bitcast.33, ...), custom_call_target="tpu_custom_call" | custom-call | flops 4000000000 | bytes 14000000 | tf_op jit(solution)/shard_map/states_kernel/pallas_call | solution.py:350
  66.2 3.0 %all-to-all-done.1 = f32[64,2,128]{2,1,0:T(2,128)S(1)} async-done(((f32[64,2,128]{2,1,0:T(2,128)}), f32[64,2,128]{2,1,0:T(2,128)S(1)}, u32[]{:S(2)}, u32[]{:S(2)}) %all-to-all-start.1) | async-done | bytes 65568 | tf_op jit(solution)/shard_map/all_to_all | solution.py:391
  69.1 0.0 copy-done
  69.1 0.0 copy-done.4
  69.1 6.2 %branch_kernel.1 = (f32[128,2048]{1,0:T(8,128)}, f32[8,128]{1,0:T(8,128)S(1)}) custom-call(f32[128,2048]{1,0:T(8,128)} %get-tuple-element.34.q, f32[128,2048]{1,0:T(8,128)} %get-tuple-element.35.bl, bf16[128,2048]{1,0:T(8,128)(2,1)S(1)} %bitcast.29, f32[1,2048]{1,0:T(1,128)S(1)} %bitcast.41, f32[16,8,128]{2,1,0:T(8,128)S(1)} %bitcast.37, ...), custom_call_target="tpu_custom_call" | custom-call | tf_op jit(solution)/shard_map/branch_kernel/pallas_call | solution.py:350
  75.4 2.4 %psum.14.stats = f32[8,128]{1,0:T(8,128)S(1)} all-reduce(f32[8,128]{1,0:T(8,128)S(1)} %get-tuple-element.37), channel_id=1, replica_groups=mesh['y'=4,'x'=4,'z'=16,'c'=2] {'c'}, use_global_device_ids=true, to_apply=%region_0.0 | all-reduce | flops 1024 | bytes 8192 | tf_op jit(solution)/shard_map/psum | solution.py:423
  77.8 6.1 %gate_kernel.1 = (f32[128,2048]{1,0:T(8,128)}, f32[16,8,128]{2,1,0:T(8,128)}, f32[2,8,2048]{2,1,0:T(8,128)S(1)}) custom-call(f32[8,128]{1,0:T(8,128)S(1)} %psum.14.stats, f32[128,2048]{1,0:T(8,128)} %get-tuple-element.34.q, f32[128,2048]{1,0:T(8,128)} %get-tuple-element.38.br, bf16[128,2048]{1,0:T(8,128)(2,1)S(1)} %bitcast.30, f32[1,2048]{1,0:T(1,128)S(1)} %bitcast.42, ...), custom_call_target="tpu_custom_call" | custom-call | tf_op jit(solution)/shard_map/gate_kernel/pallas_call | solution.py:350
  84.0 12.2 %all-to-all-start.2 = ((f32[64,2,128]{2,1,0:T(2,128)}), f32[64,2,128]{2,1,0:T(2,128)S(1)}, u32[]{:S(2)}, u32[]{:S(2)}) async-start(f32[64,2,128]{2,1,0:T(2,128)} %bitcast.15), calls=%async_computation.2 | async-start | bytes 131072 | tf_op jit(solution)/shard_map/all_to_all | solution.py:382
  96.2 7.4 %coefs_kernel.1.coefs = f32[16,112,128]{2,1,0:T(8,128)} custom-call(f32[16,8,128]{2,1,0:T(8,128)S(1)} %broadcast_in_dim.27.by_pole, f32[128,2048]{1,0:T(8,128)} %get-tuple-element.32.k, f32[128,2048]{1,0:T(8,128)} %get-tuple-element.33.v, bf16[3,128,2048]{2,1,0:T(8,128)(2,1)} %bitcast.49, bf16[3,8,2048]{2,1,0:T(8,128)(2,1)S(1)} %collective-permute-done.halo), custom_call_target="tpu_custom_call" | custom-call | flops 4000000000 | bytes 4000000 | tf_op jit(solution)/shard_map/coefs_kernel/pallas_call | solution.py:350
  103.5 5.9 %all-to-all-done.2 = f32[64,2,128]{2,1,0:T(2,128)S(1)} async-done(((f32[64,2,128]{2,1,0:T(2,128)}), f32[64,2,128]{2,1,0:T(2,128)S(1)}, u32[]{:S(2)}, u32[]{:S(2)}) %all-to-all-start.2) | async-done | bytes 65568 | tf_op jit(solution)/shard_map/all_to_all | solution.py:382
  109.4 1.5 carry_back.1
  110.9 9.2 %all-to-all-start.3 = ((f32[64,2,128]{2,1,0:T(2,128)}), f32[64,2,128]{2,1,0:T(2,128)S(1)}, u32[]{:S(2)}, u32[]{:S(2)}) async-start(f32[64,2,128]{2,1,0:T(2,128)} %bitcast.17), calls=%async_computation.3 | async-start | bytes 131072 | tf_op jit(solution)/shard_map/all_to_all | solution.py:391
  120.1 10.7 %adjoint_kernel.1 = (f32[128,2048]{1,0:T(8,128)}, f32[16,8,128]{2,1,0:T(8,128)S(1)}, f32[16,8,128]{2,1,0:T(8,128)S(1)}, f32[16,8,128]{2,1,0:T(8,128)S(1)}, f32[3,8,2048]{2,1,0:T(8,128)S(1)}) custom-call(f32[8,16]{1,0:T(8,128)S(1)} %get-tuple-element.72.rate, f32[16,8,128]{2,1,0:T(8,128)S(1)} %broadcast_in_dim.27.by_pole, f32[128,2048]{1,0:T(8,128)} %get-tuple-element.39.g, ...), custom_call_target="tpu_custom_call" | custom-call | flops 6000000000 | bytes 16000000 | tf_op jit(solution)/shard_map/adjoint_kernel/pallas_call | solution.py:350
  130.8 8.1 %outs_kernel.1 = (bf16[128,2048]{1,0:T(8,128)(2,1)}, f32[128,2048]{1,0:T(8,128)}, f32[16,32,128]{2,1,0:T(8,128)S(1)}) custom-call(f32[8,128]{1,0:T(8,128)S(1)} %psum.14.stats, f32[128,2048]{1,0:T(8,128)} %get-tuple-element.34.q, f32[128,2048]{1,0:T(8,128)} %get-tuple-element.38.br, bf16[128,2048]{1,0:T(8,128)(2,1)S(1)} %bitcast.31, f32[1,2048]{1,0:T(1,128)S(1)} %bitcast.43, ...), custom_call_target="tpu_custom_call" | custom-call | flops 1000000000 | bytes 10000000 | tf_op jit(solution)/shard_map/outs_kernel/pallas_call | solution.py:350
  138.9 0.0 all-to-all-done.3
  138.9 5.3 %sums_kernel.1 = f32[16,32,128]{2,1,0:T(8,128)} custom-call(f32[16,8,128]{2,1,0:T(8,128)S(1)} %bitcast.35, f32[16,8,128]{2,1,0:T(8,128)S(1)} %broadcast_in_dim.27.by_pole, f32[8,2048]{1,0:T(8,128)S(1)} %copy-done.3, f32[16,8,128]{2,1,0:T(8,128)S(1)} %get-tuple-element.49.loc, f32[16,8,128]{2,1,0:T(8,128)S(1)} %get-tuple-element.50.mix, ...), custom_call_target="tpu_custom_call" | custom-call | tf_op jit(solution)/shard_map/sums_kernel/pallas_call | solution.py:350
  144.2 7.3 %all-to-all-start.4 = ((f32[16,32,128]{2,1,0:T(8,128)}), f32[16,32,128]{2,1,0:T(8,128)S(1)}, u32[]{:S(2)}, u32[]{:S(2)}) async-start(f32[16,32,128]{2,1,0:T(8,128)} %sums_kernel.1), calls=%async_computation.4 | async-start | bytes 524288 | tf_op jit(solution)/shard_map/all_to_all | solution.py:470
  151.5 5.0 %collective-permute-start.1 = (f32[3,8,2048]{2,1,0:T(8,128)S(1)}, f32[3,8,2048]{2,1,0:T(8,128)S(1)}, u32[]{:S(2)}, u32[]{:S(2)}) collective-permute-start(f32[3,8,2048]{2,1,0:T(8,128)S(1)} %get-tuple-element.47), channel_id=1, source_target_pairs={{2,0},{4,2},{6,4},{8,6},{10,8},{12,10},{14,12},{16,14},{18,16},{20... | collective-permute-start | bytes 589832 | tf_op jit(solution)/shard_map/ppermute | solution.py:335
  156.5 1.3 all-to-all-done.4
  157.9 55.9 %psum.15 = f32[32,128]{1,0:T(8,128)S(1)} all-reduce(f32[32,128]{1,0:T(8,128)S(1)} %reduce_sum.9), channel_id=1, replica_groups=mesh['y'=4,'x'=4,'z'=16,'c'=2] {'z'}, use_global_device_ids=true, to_apply=%region_2.0 | all-reduce | flops 4096 | bytes 32768 | tf_op jit(solution)/shard_map/psum | solution.py:471
  213.7 0.7 broadcast_in_dim.33
  214.5 5.8 %all-to-all-start.5 = ((f32[16,32,128]{2,1,0:T(8,128)}), f32[16,32,128]{2,1,0:T(8,128)S(1)}, u32[]{:S(2)}, u32[]{:S(2)}) async-start(f32[16,32,128]{2,1,0:T(8,128)} %broadcast_in_dim.33), calls=%async_computation.5 | async-start | bytes 524288 | tf_op jit(solution)/shard_map/all_to_all | solution.py:472
  220.3 3.3 %collective-permute-start.2 = (f32[2,8,2048]{2,1,0:T(8,128)S(1)}, f32[2,8,2048]{2,1,0:T(8,128)S(1)}, u32[]{:S(2)}, u32[]{:S(2)}) collective-permute-start(f32[2,8,2048]{2,1,0:T(8,128)S(1)} %get-tuple-element.48), channel_id=1, source_target_pairs={{2,0},{4,2},{6,4},{8,6},{10,8},{12,10},{14,12},{16,14},{18,16},{20... | collective-permute-start | bytes 393224 | tf_op jit(solution)/shard_map/ppermute | solution.py:335
  223.6 3.5 %collective-permute-done.2.near = f32[2,8,2048]{2,1,0:T(8,128)S(1)} collective-permute-done((f32[2,8,2048]{2,1,0:T(8,128)S(1)}, f32[2,8,2048]{2,1,0:T(8,128)S(1)}, u32[]{:S(2)}, u32[]{:S(2)}) %collective-permute-start.2) | collective-permute-done | bytes 131104 | tf_op jit(solution)/shard_map/ppermute | solution.py:335
  227.1 0.0 collective-permute-done.1.rim
  227.1 7.6 %finish_kernel.1 = bf16[3,128,2048]{2,1,0:T(8,128)(2,1)} custom-call(f32[8,16]{1,0:T(8,128)S(1)} %get-tuple-element.72.rate, f32[16,8,128]{2,1,0:T(8,128)S(1)} %bitcast.36, f32[16,1,128]{2,1,0:T(1,128)S(1)} %copy.18.by_lane, f32[128,2048]{1,0:T(8,128)} %get-tuple-element.43.dpl, f32[128,2048]{1,0:T(8,128)} %get-tuple-element.46.dq, ...), custom_call_target="tpu_custom_call" | custom-call | flops 1000000000 | bytes 10000000 | tf_op jit(solution)/shard_map/finish_kernel/pallas_call | solution.py:350
  234.7 0.0 all-to-all-done.5.pack
  234.7 0.7 unpack.1
  235.4 0.7 copy.20
  (3 shorter events, 0.0 us)
Async XLA Ops:
  0.6 55.6 %copy-start.2 = (f32[7,3,2048]{2,0,1:T(8,128)S(1)}, f32[7,3,2048]{2,0,1:T(8,128)}, u32[]{:S(2)}) copy-start(f32[7,3,2048]{2,0,1:T(8,128)} %param.8) | copy-start | bytes 516100
  0.6 55.6 %copy-start.5 = (f32[2048]{0:T(1024)S(1)}, f32[2048]{0:T(1024)}, u32[]{:S(2)}) copy-start(f32[2048]{0:T(1024)} %param.11) | copy-start | bytes 24580
  0.7 55.6 %copy-start.3 = (f32[8,2048]{1,0:T(8,128)S(1)}, f32[8,2048]{1,0:T(8,128)}, u32[]{:S(2)}) copy-start(f32[8,2048]{1,0:T(8,128)} %weight.9) | copy-start | bytes 196612
  1.6 14.4 %collective-permute-start = (bf16[3,8,2048]{2,1,0:T(8,128)(2,1)S(1)}, bf16[3,8,2048]{2,1,0:T(8,128)(2,1)S(1)}, u32[]{:S(2)}, u32[]{:S(2)}) collective-permute-start(bf16[3,8,2048]{2,1,0:T(8,128)(2,1)S(1)} %slice.8), channel_id=1, source_target_pairs={{0,2},{2,4},{4,6},{6,8},{8,10},{10,12},{12,14},{14,16},{16,18},{18... | collective-permute-start | bytes 294920 | tf_op jit(solution)/shard_map/ppermute | solution.py:335
  16.1 0.9 copy-start.1
  23.4 25.0 %all-to-all-start = ((f32[64,2,128]{2,1,0:T(2,128)}), f32[64,2,128]{2,1,0:T(2,128)S(1)}, u32[]{:S(2)}, u32[]{:S(2)}) async-start(f32[64,2,128]{2,1,0:T(2,128)} %bitcast.9), calls=%async_computation | async-start | bytes 131072 | tf_op jit(solution)/shard_map/all_to_all | solution.py:382
  49.8 19.3 %all-to-all-start.1 = ((f32[64,2,128]{2,1,0:T(2,128)}), f32[64,2,128]{2,1,0:T(2,128)S(1)}, u32[]{:S(2)}, u32[]{:S(2)}) async-start(f32[64,2,128]{2,1,0:T(2,128)} %bitcast.11), calls=%async_computation.1 | async-start | bytes 131072 | tf_op jit(solution)/shard_map/all_to_all | solution.py:391
  56.2 12.9 %copy-start = (bf16[1,128,2048]{2,1,0:T(8,128)(2,1)S(1)}, bf16[1,128,2048]{2,1,0:T(8,128)(2,1)}, u32[]{:S(2)}) copy-start(bf16[1,128,2048]{2,1,0:T(8,128)(2,1)} %param.13) | copy-start | bytes 1572868
  56.2 12.9 %copy-start.4 = (f32[2048]{0:T(1024)S(1)}, f32[2048]{0:T(1024)}, u32[]{:S(2)}) copy-start(f32[2048]{0:T(1024)} %param.12) | copy-start | bytes 24580
  84.0 25.5 %all-to-all-start.2 = ((f32[64,2,128]{2,1,0:T(2,128)}), f32[64,2,128]{2,1,0:T(2,128)S(1)}, u32[]{:S(2)}, u32[]{:S(2)}) async-start(f32[64,2,128]{2,1,0:T(2,128)} %bitcast.15), calls=%async_computation.2 | async-start | bytes 131072 | tf_op jit(solution)/shard_map/all_to_all | solution.py:382
  110.9 28.0 %all-to-all-start.3 = ((f32[64,2,128]{2,1,0:T(2,128)}), f32[64,2,128]{2,1,0:T(2,128)S(1)}, u32[]{:S(2)}, u32[]{:S(2)}) async-start(f32[64,2,128]{2,1,0:T(2,128)} %bitcast.17), calls=%async_computation.3 | async-start | bytes 131072 | tf_op jit(solution)/shard_map/all_to_all | solution.py:391
  144.2 13.7 %all-to-all-start.4 = ((f32[16,32,128]{2,1,0:T(8,128)}), f32[16,32,128]{2,1,0:T(8,128)S(1)}, u32[]{:S(2)}, u32[]{:S(2)}) async-start(f32[16,32,128]{2,1,0:T(8,128)} %sums_kernel.1), calls=%async_computation.4 | async-start | bytes 524288 | tf_op jit(solution)/shard_map/all_to_all | solution.py:470
  151.5 75.6 %collective-permute-start.1 = (f32[3,8,2048]{2,1,0:T(8,128)S(1)}, f32[3,8,2048]{2,1,0:T(8,128)S(1)}, u32[]{:S(2)}, u32[]{:S(2)}) collective-permute-start(f32[3,8,2048]{2,1,0:T(8,128)S(1)} %get-tuple-element.47), channel_id=1, source_target_pairs={{2,0},{4,2},{6,4},{8,6},{10,8},{12,10},{14,12},{16,14},{18,16},{20... | collective-permute-start | bytes 589832 | tf_op jit(solution)/shard_map/ppermute | solution.py:335
  214.5 20.2 %all-to-all-start.5 = ((f32[16,32,128]{2,1,0:T(8,128)}), f32[16,32,128]{2,1,0:T(8,128)S(1)}, u32[]{:S(2)}, u32[]{:S(2)}) async-start(f32[16,32,128]{2,1,0:T(8,128)} %broadcast_in_dim.33), calls=%async_computation.5 | async-start | bytes 524288 | tf_op jit(solution)/shard_map/all_to_all | solution.py:472
  220.3 6.8 %collective-permute-start.2 = (f32[2,8,2048]{2,1,0:T(8,128)S(1)}, f32[2,8,2048]{2,1,0:T(8,128)S(1)}, u32[]{:S(2)}, u32[]{:S(2)}) collective-permute-start(f32[2,8,2048]{2,1,0:T(8,128)S(1)} %get-tuple-element.48), channel_id=1, source_target_pairs={{2,0},{4,2},{6,4},{8,6},{10,8},{12,10},{14,12},{16,14},{18,16},{20... | collective-permute-start | bytes 393224 | tf_op jit(solution)/shard_map/ppermute | solution.py:335

commit v3 on v2

--- a/solution.py
+++ b/solution.py
@@ -17,11 +17,92 @@
 POLES = 8
 TAPS = 7
 PAD = 8
-GB = 2
+GROUPS_HERE = 16
+PARTS = 4
+HELD = ("smem", "vmem", "order")
+C, G, W, S, V, O = "cols", "groups", "whole", "smem", "vmem", "order"
 ROWS = 32
 VMEM_MIB = 53
 CTX = ("x", "z")
-YX = ("y", "x")
+
+
+def window(ref, kind, part):
+    if kind == "cols":
+        span = ref.shape[-1] // PARTS
+        at = pl.ds(pl.multiple_of(part * span, span), span)
+        return ref.at[(slice(None),) * (len(ref.shape) - 1) + (at,)]
+    if kind == "groups":
+        span = ref.shape[0] // PARTS
+        return ref.at[pl.ds(part * span, span)]
+    return ref
+
+
+def streamed(setup, kinds_in, kinds_out, *refs):
+    ins, outs = refs[: len(kinds_in)], refs[len(kinds_in) : len(kinds_in) + len(kinds_out)]
+    rest = list(refs[len(kinds_in) + len(kinds_out) :])
+    sems, scratch = rest[0], rest[1:]
+    moved = [k for k in kinds_in if k not in HELD]
+    in_bufs = scratch[: len(moved)]
+    out_bufs = scratch[len(moved) : len(moved) + len(kinds_out)]
+    extra = scratch[len(moved) + len(kinds_out) :]
+    sources = [r for r, k in zip(ins, kinds_in) if k not in HELD]
+
+    def fetch(n, part):
+        src, dst = window(sources[n], moved[n], part), window(in_bufs[n], moved[n], part)
+        return pltpu.make_async_copy(src, dst, sems.at[n, part])
+
+    def store(n, part):
+        src, dst = window(out_bufs[n], kinds_out[n], part), window(outs[n], kinds_out[n], part)
+        return pltpu.make_async_copy(src, dst, sems.at[len(moved) + n, part])
+
+    for n, kind in enumerate(moved):
+        if kind == "whole":
+            fetch(n, 0).start()
+
+    def begin(part, carry):
+        for n, kind in enumerate(moved):
+            if kind != "whole":
+                fetch(n, part).start()
+        return carry
+
+    lax.fori_loop(0, PARTS, begin, 0)
+    for n, kind in enumerate(moved):
+        if kind == "whole":
+            fetch(n, 0).wait()
+    buffers = iter(in_bufs)
+    views = [r if k in HELD else next(buffers) for r, k in zip(ins, kinds_in)]
+    body, last = setup(*[v for v, k in zip(views, kinds_in) if k != "order"], *out_bufs, *extra)
+    per_part = GROUPS_HERE // PARTS
+
+    def step(part, carry):
+        for n, kind in enumerate(moved):
+            if kind != "whole":
+                fetch(n, part).wait()
+        for i in range(per_part):
+            gi = part * per_part + i
+            body(gi, pl.ds(pl.multiple_of(gi * GS, GS), GS))
+        for n, kind in enumerate(kinds_out):
+            if kind != "whole":
+                store(n, part).start()
+        return carry
+
+    lax.fori_loop(0, PARTS, step, 0)
+    if last is not None:
+        last()
+    for n, kind in enumerate(kinds_out):
+        if kind == "whole":
+            store(n, 0).start()
+
+    def end(part, carry):
+        for n, kind in enumerate(kinds_out):
+            if kind != "whole":
+                store(n, part).wait()
+        return carry
+
+    lax.fori_loop(0, PARTS, end, 0)
+    for n, kind in enumerate(kinds_out):
+        if kind == "whole":
+            store(n, 0).wait()
 
 
 def params(mib):
@@ -97,8 +178,7 @@
 
 
 def ends_kernel(by_pole, feat, halo, taps, k_o, v_o, e_o, edge_o, ext):
-    for gi in range(GB):
-        cs = slice(gi * GS, (gi + 1) * GS)
+    def body(gi, cs):
         key = filtered(1, taps, feat, halo, cs, ext)
         value = filtered(2, taps, feat, halo, cs, ext)
         k_o[:, cs] = key
@@ -107,18 +187,18 @@
         edge_o[1, :, cs] = value[0:PAD, :]
         e_o[gi] = weighted_rows(jnp.exp(-by_pole[gi] * (L - 1.0 - lane_place())), key * value)
 
+    return body, None
+
 
 def states_kernel(rate, feat, halo, taps, k, v, weight, skip, q_o, bl_o, s_o, ext):
-    first = pl.program_id(0) * GB
     tri = ones_tri(True)
     place = iota((L, GS), 0).astype(F32)
-    for gi in range(GB):
-        cs = slice(gi * GS, (gi + 1) * GS)
+    def body(gi, cs):
         q_o[:, cs] = filtered(0, taps, feat, halo, cs, ext)
         prod = k[:, cs] * v[:, cs]
         modal = skip[0:1, cs] * prod
         for p in range(0, POLES, 2):
-            rates = [rate[p + i, first + gi] for i in range(2)]
+            rates = [rate[p + i, gi] for i in range(2)]
             both = tri_dot(tri, [jnp.exp(place * r) * prod for r in rates])
             for i, r in enumerate(rates):
                 state = jnp.exp(place * (-r)) * both[:, i * GS : (i + 1) * GS]
@@ -126,10 +206,11 @@
                 modal = modal + weight[p + i : p + i + 1, cs] * state
         bl_o[:, cs] = modal
 
+    return body, None
+
 
 def coefs_kernel(by_pole, k, v, feat, halo, c_o, ext):
-    for gi in range(GB):
-        cs = slice(gi * GS, (gi + 1) * GS)
+    def body(gi, cs):
         fill_ext(ext, feat, halo, cs)
         table = two_parts(jnp.exp(-by_pole[gi] * (L - 1.0 - lane_place())))
         for j, other in ((1, v[:, cs]), (2, k[:, cs])):
@@ -140,8 +221,10 @@
                 at = POLES * (TAPS * (j - 1) + t)
                 c_o[gi, at : at + POLES, :] = both[:, t * GS : (t + 1) * GS]
 
-
-def scan_kernel(back, rate, where, rows, out):
+    return body, None
+
+
+def scan_kernel(back, rate, where, rows, *refs):
     me = where[0]
     group = me // 4
     pole = 2 * (me % 4)
@@ -151,31 +234,27 @@
     keep = (lag >= 0) & (row % 2 == col % 2)
     own = jnp.where(row % 2 == 0, low, high)
     decay = jnp.where(keep, jnp.exp(-(own * L) * jnp.maximum(lag, 0).astype(F32)), 0.0)
-    out[...] = jnp.dot(decay, rows[...], precision=HIGHEST, preferred_element_type=F32)
+    refs[-1][...] = jnp.dot(decay, rows[...], precision=HIGHEST, preferred_element_type=F32)
 
 
 def branch_kernel(q, bl, cot, gain, state_in, by_lane, weight, br_o, stats_o, acc):
-    step = pl.program_id(0)
-
-    @pl.when(step == 0)
-    def _():
-        acc[...] = jnp.zeros_like(acc)
-
-    for gi in range(GB):
-        cs = slice(gi * GS, (gi + 1) * GS)
+    acc[...] = jnp.zeros_like(acc)
+
+    def body(gi, cs):
         branch = bl[:, cs] + spread_poles(by_lane[gi], 1, weight[:, cs] * state_in[gi])
         br_o[:, cs] = branch
         gated = q[:, cs] * branch
         acc[0] += gated * gated
         acc[1] += (gain[0:1, cs] * cot[:, cs].astype(F32)) * gated
 
-    @pl.when(step == pl.num_programs(0) - 1)
-    def _():
+    def last():
         row = iota((8, L), 0)
         squares = rowsum(acc[0].T)
         slopes = rowsum(acc[1].T)
         stats_o[...] = jnp.where(row == 0, squares, jnp.where(row == 1, slopes, 0.0))
 
+    return body, last
+
 
 def down(row):
     return jnp.broadcast_to(row, (L, L)).T
@@ -185,8 +264,7 @@
     inv_row = lax.rsqrt(stats[0:1, :] / D + EPSILON)
     inv = down(inv_row)
     pull = down(stats[1:2, :] * inv_row * inv_row * inv_row / D)
-    for gi in range(GB):
-        cs = slice(gi * GS, (gi + 1) * GS)
+    def body(gi, cs):
         query, branch = q[:, cs], br[:, cs]
         dgated = (gain[0:1, cs] * cot[:, cs].astype(F32)) * inv - (query * branch) * pull
         dbranch = dgated * query
@@ -196,18 +274,18 @@
         edge_o[0, :, cs] = dgated[0:PAD, :] * branch[0:PAD, :]
         edge_o[1, :, cs] = back
 
+    return body, None
+
 
 def adjoint_kernel(
     rate, by_pole, g, k, v, states, weight, skip, state_in, back, edge,
     dpl_o, res_o, loc_o, mix_o, edge_o,
 ):
-    first = pl.program_id(0) * GB
     tri = ones_tri(False)
     place = iota((L, GS), 0).astype(F32)
     centre = place - (L - 1) / 2
     lane = lane_place()
-    for gi in range(GB):
-        cs = slice(gi * GS, (gi + 1) * GS)
+    def body(gi, cs):
         dbranch = g[:, cs]
         prod = k[:, cs] * v[:, cs]
         total = skip[0:1, cs] * dbranch
@@ -222,7 +300,7 @@
         mix_o[gi] = once * (deep + L * jnp.exp(-(L - 1) * own_rate) * own_in)
         loc = once * own_in * heavy
         for p in range(0, POLES, 2):
-            rates = [rate[p + i, first + gi] for i in range(2)]
+            rates = [rate[p + i, gi] for i in range(2)]
             both = tri_dot(tri, [jnp.exp(place * (-r)) * dbranch for r in rates])
             for i, r in enumerate(rates):
                 at = slice(p + i, p + i + 1)
@@ -235,6 +313,8 @@
         edge_o[1, :, cs] = total[0:PAD, :]
         edge_o[2, :, cs] = edge[1, :, cs]
 
+    return body, None
+
 
 def outs_kernel(
     stats, q, br, cot, gain, k, v, g, dpl, res, feat, halo, out_o, dq_o, pack_o, ext,
@@ -242,8 +322,7 @@
     inv_row = lax.rsqrt(stats[0:1, :] / D + EPSILON)
     inv = down(inv_row)
     pull = down(stats[1:2, :] * inv_row * inv_row * inv_row / D)
-    for gi in range(GB):
-        cs = slice(gi * GS, (gi + 1) * GS)
+    def body(gi, cs):
         fill_ext(ext, feat, halo, cs)
         query, branch, key, value = q[:, cs], br[:, cs], k[:, cs], v[:, cs]
         grad = cot[:, cs].astype(F32)
@@ -262,11 +341,12 @@
         pack_o[gi, 30:31, :] = rowsum(grad * normed)
         pack_o[gi, 31:32, :] = jnp.zeros((1, GS), F32)
 
+    return body, None
+
 
 def sums_kernel(later, by_pole, weight, loc, mix, coefs, pack, pack_o):
     lane, sub = iota((POLES, GS), 1), iota((POLES, GS), 0)
-    for gi in range(GB):
-        cs = slice(gi * GS, (gi + 1) * GS)
+    def body(gi, cs):
         coming = later[gi]
         scaled = weight[:, cs] * coming
         pack_o[gi] = pack[gi]
@@ -277,12 +357,12 @@
         inner = jnp.sum(weight[:, cs] * (loc[gi] + coming * mix[gi]), axis=1, keepdims=True)
         pack_o[gi, 31:32, :] = rowsum(jnp.where(lane == sub, -by_pole[gi] * inner, 0.0))
 
+    return body, None
+
 
 def finish_kernel(rate, later, by_lane, dpl, dq, k, v, weight, rim, near, taps, grad_o, dext):
-    first = pl.program_id(0) * GB
     ahead = (iota((PAD, GS), 0) + 1).astype(F32)
-    for gi in range(GB):
-        cs = slice(gi * GS, (gi + 1) * GS)
+    def body(gi, cs):
         coming = later[gi]
         dprod = dpl[:, cs] + spread_poles(by_lane[gi], -1, weight[:, cs] * coming)
         dext[0, 0:L, :] = dq[:, cs]
@@ -291,7 +371,7 @@
         beyond = weight[:, cs] * (coming - rim[2, :, cs])
         next_prod = rim[1, :, cs]
         for p in range(POLES):
-            next_prod = next_prod + jnp.exp(ahead * rate[p, first + gi]) * beyond[p : p + 1, :]
+            next_prod = next_prod + jnp.exp(ahead * rate[p, gi]) * beyond[p : p + 1, :]
         dext[0, L : L + PAD, :] = rim[0, :, cs]
         dext[1, L : L + PAD, :] = next_prod * near[1, :, cs]
         dext[2, L : L + PAD, :] = next_prod * near[0, :, cs]
@@ -300,6 +380,8 @@
             for t in range(1, TAPS):
                 acc = acc + taps[j, t : t + 1, cs] * dext[j, pl.ds(t, L), :]
             grad_o[j, :, cs] = acc.astype(BF16)
+
+    return body, None
 
 
 def unpack_kernel(pack, conv_o, rate_o, res_o, skip_o, gain_o):
@@ -318,16 +400,23 @@
     return pl.BlockSpec(memory_space=pltpu.SMEM)
 
 
-def cols(*lead):
-    return pl.BlockSpec((*lead, GB * GS), lambda i: (0,) * len(lead) + (i,))
-
-
-def groups_of(rows):
-    return pl.BlockSpec((GB, rows, GS), lambda i: (i, 0, 0))
+def vmem():
+    return pl.BlockSpec(memory_space=pltpu.VMEM)
 
 
 def shape(*dims, dtype=F32):
     return jax.ShapeDtypeStruct(dims, dtype)
+
+
+ends_kernel.kinds = ((W, C, V, C,), (C, C, G, C,))
+states_kernel.kinds = ((S, C, V, C, C, C, C, C,), (C, C, C,))
+coefs_kernel.kinds = ((W, C, C, C, V,), (G,))
+branch_kernel.kinds = ((C, C, C, C, G, W, C,), (C, W,))
+gate_kernel.kinds = ((W, C, C, C, C, W,), (C, G, C,))
+adjoint_kernel.kinds = ((S, W, C, C, C, C, C, C, G, G, C,), (C, G, G, G, C,))
+outs_kernel.kinds = ((W, C, C, C, C, C, C, C, C, G, C, V,), (C, C, G,))
+sums_kernel.kinds = ((G, W, C, G, G, G, G, O,), (G,))
+finish_kernel.kinds = ((S, G, W, C, C, C, C, C, C, C, C,), (C,))
 
 
 def shifted(value, step):
@@ -346,106 +435,99 @@
     gain = norm_gain[None]
     where = lax.axis_index(CTX).astype(jnp.int32)[None]
 
-    def call(kernel, ins, outs, args, scratch=(), flops=0, moved=0, special=0):
+    def call(setup, outs, args, extra=(), flops=0, moved=0, special=0):
+        kinds_in, kinds_out = setup.kinds
+        fetched = [a for a, k in zip(args, kinds_in) if k not in HELD]
+        space = {"smem": pltpu.SMEM, "vmem": pltpu.VMEM}
         return pl.pallas_call(
-            kernel,
-            grid=(groups // GB,),
-            in_specs=ins,
-            out_specs=[o[0] for o in outs],
-            out_shape=[o[1] for o in outs],
-            scratch_shapes=[pltpu.VMEM(d, F32) for d in scratch],
+            functools.partial(streamed, setup, kinds_in, kinds_out),
+            in_specs=[pl.BlockSpec(memory_space=space.get(k, pl.ANY)) for k in kinds_in],
+            out_specs=[pl.BlockSpec(memory_space=pl.ANY) for _ in outs],
+            out_shape=outs,
+            scratch_shapes=[pltpu.SemaphoreType.DMA((len(fetched) + len(outs), PARTS))]
+            + [pltpu.VMEM(a.shape, a.dtype) for a in [*fetched, *outs]]
+            + [pltpu.VMEM(d, F32) for d in extra],
             compiler_params=params(VMEM_MIB),
             cost_estimate=pl.CostEstimate(flops=flops, bytes_accessed=moved, transcendentals=special),
-            name=kernel.__name__,
+            name=setup.__name__,
         )(*args)
 
-    wide = (cols(L), shape(L, channels))
-    per_pole = (groups_of(POLES), shape(groups, POLES, GS))
+    wide = shape(L, channels)
+    per_pole = shape(groups, POLES, GS)
+    edges = shape(2, PAD, channels)
     ext3 = (3, PAD + L, GS)
 
     halo = shifted(feat[:, L - PAD :], 1)
     rate = jnp.exp(log_rate)
     by_pole = jnp.broadcast_to(rate.T[:, :, None], (groups, POLES, GS))
     by_lane = jnp.tile(rate.T, (1, GS // POLES))[:, None, :]
-    poles, lanes = groups_of(POLES), groups_of(1)
 
     key, value, ends, edge = call(
-        ends_kernel,
-        [poles, cols(3, L), cols(3, PAD), cols(3, TAPS)],
-        [wide, wide, per_pole, (cols(2, PAD), shape(2, PAD, channels))],
-        (by_pole, feat, halo, taps),
-        [ext3],
+        ends_kernel, [wide, wide, per_pole, edges], (by_pole, feat, halo, taps), [ext3]
     )
     near = shifted(edge, -1)
 
-    def carried(rows, back):
-        sent = lax.all_to_all(rows.reshape(count, 2, GS), CTX, 0, 0)
+    def owned(rows):
+        return lax.all_to_all(rows.reshape(count, 2, GS), CTX, 0, 0).reshape(L, GS)
+
+    def carried(rows, after, back):
         summed = pl.pallas_call(
             functools.partial(scan_kernel, back),
-            in_specs=[smem(), smem(), pl.BlockSpec((L, GS), lambda: (0, 0))],
-            out_specs=pl.BlockSpec((L, GS), lambda: (0, 0)),
+            in_specs=[smem(), smem(), vmem()] + [pl.BlockSpec(memory_space=pl.ANY)] * len(after),
+            out_specs=vmem(),
             out_shape=shape(L, GS),
             compiler_params=params(16),
             name="carry_back" if back else "carry_on",
-        )(rate, where, sent.reshape(L, GS))
+        )(rate, where, rows, *after)
         given = lax.all_to_all(summed.reshape(count, 2, GS), CTX, 0, 0)
         return given.reshape(groups, POLES, GS)
 
-    state_in = carried(ends, False)
+    rows_in = owned(ends)
+    coefs = call(
+        coefs_kernel,
+        [shape(groups, 2 * TAPS * POLES, GS)],
+        (by_pole, key, value, feat, halo),
+        [ext3],
+        flops=4_000_000_000,
+        moved=4_000_000,
+    )[0]
+    state_in = carried(rows_in, (coefs, near), False)
 
     query, base, states = call(
         states_kernel,
-        [smem(), cols(3, L), cols(3, PAD), cols(3, TAPS), cols(L), cols(L), cols(POLES), cols(1)],
-        [wide, wide, (cols(POLES, L), shape(POLES, L, channels))],
+        [wide, wide, shape(POLES, L, channels)],
         (rate, feat, halo, taps, key, value, residues, skip),
         [ext3],
         flops=4_000_000_000,
         moved=14_000_000,
         special=4_000_000,
     )
-    coefs = call(
-        coefs_kernel,
-        [poles, cols(L), cols(L), cols(3, L), cols(3, PAD)],
-        [(groups_of(2 * TAPS * POLES), shape(groups, 2 * TAPS * POLES, GS))],
-        (by_pole, key, value, feat, halo),
-        [ext3],
-        flops=4_000_000_000,
-        moved=4_000_000,
-    )[0]
-
     branch, stats = call(
         branch_kernel,
-        [cols(L), cols(L), cols(L), cols(1), poles, lanes, cols(POLES)],
-        [wide, (pl.BlockSpec((8, L), lambda i: (0, 0)), shape(8, L))],
+        [wide, shape(8, L)],
         (query, base, cot, gain, state_in, by_lane, residues),
         [(2, L, GS)],
     )
     stats = lax.psum(stats, "c")
-    small = pl.BlockSpec((8, L), lambda i: (0, 0))
 
     dbranch, back_in, edge = call(
-        gate_kernel,
-        [small] + [cols(L)] * 3 + [cols(1), poles],
-        [wide, per_pole, (cols(2, PAD), shape(2, PAD, channels))],
-        (stats, query, branch, cot, gain, by_pole),
-    )
-    later = carried(back_in, True)
-
+        gate_kernel, [wide, per_pole, edges], (stats, query, branch, cot, gain, by_pole)
+    )
+    rows_back = owned(back_in)
     dlocal, res_part, loc_part, mix_part, edge = call(
         adjoint_kernel,
-        [smem(), poles] + [cols(L)] * 3 + [cols(POLES, L), cols(POLES), cols(1), poles, poles, cols(2, PAD)],
-        [wide, per_pole, per_pole, per_pole, (cols(3, PAD), shape(3, PAD, channels))],
+        [wide, per_pole, per_pole, per_pole, shape(3, PAD, channels)],
         (rate, by_pole, dbranch, key, value, states, residues, skip, state_in, back_in, edge),
         flops=6_000_000_000,
         moved=16_000_000,
         special=4_000_000,
     )
+    later = carried(rows_back, (dlocal,), True)
     rim = shifted(edge, -1)
 
     block_out, dquery, pack = call(
         outs_kernel,
-        [small] + [cols(L)] * 3 + [cols(1)] + [cols(L)] * 4 + [poles, cols(3, L), cols(3, PAD)],
-        [(cols(L), shape(L, channels, dtype=BF16)), wide, (groups_of(ROWS), shape(groups, ROWS, GS))],
+        [shape(L, channels, dtype=BF16), wide, shape(groups, ROWS, GS)],
         (stats, query, branch, cot, gain, key, value, dbranch, dlocal, res_part, feat, halo),
         [ext3],
         flops=1_000_000_000,
@@ -453,23 +535,23 @@
     )
     pack = call(
         sums_kernel,
-        [poles, poles, cols(POLES), poles, poles, groups_of(2 * TAPS * POLES), groups_of(ROWS)],
-        [(groups_of(ROWS), shape(groups, ROWS, GS))],
-        (later, by_pole, residues, loc_part, mix_part, coefs, pack),
+        [shape(groups, ROWS, GS)],
+        (later, by_pole, residues, loc_part, mix_part, coefs, pack, rim),
     )[0]
     feature_grad = call(
         finish_kernel,
-        [smem(), poles, lanes] + [cols(L)] * 4 + [cols(POLES), cols(3, PAD), cols(2, PAD), cols(3, TAPS)],
-        [(cols(3, L), shape(3, L, channels, dtype=BF16))],
+        [shape(3, L, channels, dtype=BF16)],
         (rate, later, by_lane, dlocal, dquery, key, value, residues, rim, near, taps),
         [ext3],
         flops=1_000_000_000,
         moved=10_000_000,
     )[0]
 
-    parts = lax.all_to_all(pack, YX, 0, 0)
-    mine = lax.psum(jnp.sum(parts, axis=0), "z")
-    totals = lax.all_to_all(jnp.broadcast_to(mine[None], (groups, ROWS, GS)), YX, 0, 0)
+    share = groups * ROWS // count
+    parts = lax.all_to_all(pack.reshape(count, share, GS), CTX, 0, 0)
+    mine = lax.psum(jnp.sum(parts, axis=0), "y")
+    totals = lax.all_to_all(jnp.broadcast_to(mine[None], (count, share, GS)), CTX, 0, 0)
+    totals = totals.reshape(groups, ROWS, GS)
     conv, rate_grad, res, skip_grad, gain_grad = pl.pallas_call(
         unpack_kernel,
         out_shape=[shape(3, TAPS, channels), shape(groups, GS), shape(POLES, channels)] + [shape(1, channels)] * 2,

time: 238 us -> 205 us (0.86)
  Pallas kernels: 71.2 us -> 53.9 us
  blocking collectives: 58.3 us -> 45.1 us
  waiting for transfers between devices: 36.5 us -> 30.5 us
  local copies, waits for them, and re-layouts: 4.22 us -> 7.25 us
    psum x1, blocking collectives: 55.9 us -> 10.8 us  [local(): mine = lax.psum(jnp.sum(parts, axis=0), 'y')]
    all_to_all x0 -> x1, blocking collectives: none -> 31.9 us  [local(): parts = lax.all_to_all(pack.reshape(count, share, GS), CTX, 0, 0)]
    pallas_call x9, Pallas kernels: 67.6 us -> 50.2 us  [call(): pl.pallas_call(functools.partial(streamed, setup, kinds_in, kinds_out), i...]
    all_to_all x4 -> x3, starting transfers between devices: 37.4 us -> 29.6 us  [the longest x2 23 us: owned(): return lax.all_to_all(rows.reshape(count, 2, GS), CTX, 0, 0).reshape(L, GS)]
    all_to_all x2, starting transfers between devices: 15.6 us -> 22.9 us  [carried(): given = lax.all_to_all(summed.reshape(count, 2, GS), CTX, 0, 0)]
    all_to_all x4 -> x3, waiting for transfers between devices: 20.1 us -> 16 us  [the longest x1 11 us: local(): lax.all_to_all(jnp.broadcast_to(mine[None], (count, share, GS)), CTX, 0, 0)]
    ppermute x3, waiting for transfers between devices: 13.4 us -> 9.8 us  [shifted(): return lax.ppermute(value, CTX, pairs)]
    unnamed x13 -> x19, local copies, waits for them, and re-layouts: 1.62 us -> 4.73 us
  transfers between devices with their start and end apart: 9 -> 8, of which waited for: 6 -> 6; matrix products, arithmetic and copies ran while one was open for 1% -> 0% of each run, Pallas kernels for 18% -> 19%
where the time goes in v3:
time: 205 us; the launch traced here: 204 us
  starting transfers between devices  66 us (32%)
  Pallas kernels  53.9 us (26%)
  blocking collectives  45.1 us (22%)
  waiting for transfers between devices  30.5 us (15%)
  local copies, waits for them, and re-layouts  7.25 us (4%)
    pallas_call x9, Pallas kernels, call(): pl.pallas_call(functools.partial(streamed, setup, kinds_in, kinds_out), i...  50.2 us
    all_to_all x1, blocking collectives, local(): parts = lax.all_to_all(pack.reshape(count, share, GS), CTX, 0, 0)  31.9 us
    all_to_all x2, starting transfers between devices, owned(): return lax.all_to_all(rows.reshape(count, 2, GS), CTX, 0, 0).reshape(L, GS)  23 us
    all_to_all x2, starting transfers between devices, carried(): given = lax.all_to_all(summed.reshape(count, 2, GS), CTX, 0, 0)  22.9 us
    ppermute x3, starting transfers between devices, shifted(): return lax.ppermute(value, CTX, pairs)  13.6 us
    all_to_all x1, waiting for transfers between devices, local(): lax.all_to_all(jnp.broadcast_to(mine[None], (count, share, GS)), CTX, 0, 0)  11 us
    psum x1, blocking collectives, local(): mine = lax.psum(jnp.sum(parts, axis=0), 'y')  10.8 us
    ppermute x3, waiting for transfers between devices, shifted(): return lax.ppermute(value, CTX, pairs)  9.8 us
  transfers between devices with their start and end apart: 8, of which 6 were waited for; matrix products, arithmetic and copies ran while one was open for 0% of the time, Pallas kernels for 19%

profile of v3, /device:TPU:6, one launch (start us, length us, event | category | flops | bytes accessed | tf_op | source)
XLA Modules:
  0.0 203.7 jit_solution(13914230360079946381)
XLA Ops:
  0.6 0.9 slice.8
  1.5 3.8 %collective-permute-start = (bf16[3,8,2048]{2,1,0:T(8,128)(2,1)S(1)}, bf16[3,8,2048]{2,1,0:T(8,128)(2,1)S(1)}, u32[]{:S(2)}, u32[]{:S(2)}) collective-permute-start(bf16[3,8,2048]{2,1,0:T(8,128)(2,1)S(1)} %slice.8), channel_id=1, source_target_pairs={{0,2},{2,4},{4,6},{6,8},{8,10},{10,12},{12,14},{14,16},{16,18},{18... | collective-permute-start | bytes 294920 | tf_op jit(solution)/shard_map/ppermute | solution.py:424
  5.4 0.7 exponential_bitcast_fusion
  6.1 0.1 copy.17
  6.2 9.8 %collective-permute-done.refs_2_.refs_4_.refs_11_ = bf16[3,8,2048]{2,1,0:T(8,128)(2,1)S(1)} collective-permute-done((bf16[3,8,2048]{2,1,0:T(8,128)(2,1)S(1)}, bf16[3,8,2048]{2,1,0:T(8,128)(2,1)S(1)}, u32[]{:S(2)}, u32[]{:S(2)}) %collective-permute-start) | collective-permute-done | bytes 98336 | tf_op jit(solution)/shard_map/ppermute | solution.py:424
  16.0 0.1 broadcast_in_dim.27.refs_0_.refs_5_.refs_1_
  16.1 0.0 copy-start.3
  16.1 0.9 copy-done.3
  17.0 4.1 %ends_kernel.1 = (f32[128,2048]{1,0:T(8,128)}, f32[128,2048]{1,0:T(8,128)}, f32[16,8,128]{2,1,0:T(8,128)}, f32[2,8,2048]{2,1,0:T(8,128)S(1)}) custom-call(f32[16,8,128]{2,1,0:T(8,128)S(1)} %broadcast_in_dim.27.refs_0_.refs_5_.refs_1_, bf16[3,128,2048]{2,1,0:T(8,128)(2,1)} %bitcast.51, bf16[3,8,2048]{2,1,0:T(8,128)(2,1)S(1)} %collective-permute-done.refs_2_.refs_4_.refs_11_, ...), custom_call_target="tpu_custom_call" | custom-call | tf_op jit(solution)/shard_map/ends_kernel/pallas_call | solution.py:442
  21.1 12.1 %all-to-all-start = ((f32[64,2,128]{2,1,0:T(2,128)}), f32[64,2,128]{2,1,0:T(2,128)S(1)}, u32[]{:S(2)}, u32[]{:S(2)}) async-start(f32[64,2,128]{2,1,0:T(2,128)} %bitcast.9), calls=%async_computation | async-start | bytes 131072 | tf_op jit(solution)/shard_map/all_to_all | solution.py:471
  33.1 4.9 %collective-permute-start.1 = (f32[2,8,2048]{2,1,0:T(8,128)S(1)}, f32[2,8,2048]{2,1,0:T(8,128)S(1)}, u32[]{:S(2)}, u32[]{:S(2)}) collective-permute-start(f32[2,8,2048]{2,1,0:T(8,128)S(1)} %get-tuple-element.37), channel_id=1, source_target_pairs={{2,0},{4,2},{6,4},{8,6},{10,8},{12,10},{14,12},{16,14},{18,16},{20... | collective-permute-start | bytes 393224 | tf_op jit(solution)/shard_map/ppermute | solution.py:424
  38.0 0.0 copy-start.4
  38.0 0.0 copy-start.5
  38.0 0.0 copy-start.8
  38.0 5.2 %coefs_kernel.1.refs_0_.refs_5_ = f32[16,112,128]{2,1,0:T(8,128)} custom-call(f32[16,8,128]{2,1,0:T(8,128)S(1)} %broadcast_in_dim.27.refs_0_.refs_5_.refs_1_, f32[128,2048]{1,0:T(8,128)} %get-tuple-element.32.refs_4_.refs_1_.refs_3_.refs_5_, f32[128,2048]{1,0:T(8,128)} %get-tuple-element.33.refs_5_.refs_2_.refs_4_.refs_6_, bf16[3,128,2048]{2,1,0:T(8,128)(2,1)} %bitcast.52, ...), custom_call_target="tpu_custom_call" | custom-call | flops 4000000000 | bytes 4000000 | tf_op jit(solution)/shard_map/coefs_kernel/pallas_call | solution.py:442
  43.3 0.0 collective-permute-done.1.refs_1_.refs_9_
  43.3 2.8 %all-to-all-done = f32[64,2,128]{2,1,0:T(2,128)S(1)} async-done(((f32[64,2,128]{2,1,0:T(2,128)}), f32[64,2,128]{2,1,0:T(2,128)S(1)}, u32[]{:S(2)}, u32[]{:S(2)}) %all-to-all-start) | async-done | bytes 65568 | tf_op jit(solution)/shard_map/all_to_all | solution.py:471
  46.1 0.0 copy-start.2
  46.1 1.2 copy-done.2
  47.3 1.5 carry_on.1
  48.7 10.0 %all-to-all-start.1 = ((f32[64,2,128]{2,1,0:T(2,128)}), f32[64,2,128]{2,1,0:T(2,128)S(1)}, u32[]{:S(2)}, u32[]{:S(2)}) async-start(f32[64,2,128]{2,1,0:T(2,128)} %bitcast.11), calls=%async_computation.1 | async-start | bytes 131072 | tf_op jit(solution)/shard_map/all_to_all | solution.py:482
  58.7 0.0 copy-done.4
  58.7 0.0 copy-done.5
  58.7 0.0 copy-done.8
  58.7 0.0 copy-start.1
  58.7 0.0 copy-start.7
  58.7 8.6 %states_kernel.1 = (f32[128,2048]{1,0:T(8,128)}, f32[128,2048]{1,0:T(8,128)}, f32[8,128,2048]{2,1,0:T(8,128)}) custom-call(f32[8,16]{1,0:T(8,128)S(1)} %get-tuple-element.72.refs_0_.rate, bf16[3,128,2048]{2,1,0:T(8,128)(2,1)} %bitcast.53, bf16[3,8,2048]{2,1,0:T(8,128)(2,1)S(1)} %collective-permute-done.refs_2_.refs_4_.refs_11_, f32[3,7,2048]{2,1,0:T(8,128)S(1)} %bitcast.37, ...), custom_call_target="tpu_custom_call" | custom-call | flops 4000000000 | bytes 14000000 | tf_op jit(solution)/shard_map/states_kernel/pallas_call | solution.py:442
  67.4 4.2 %all-to-all-done.1 = f32[64,2,128]{2,1,0:T(2,128)S(1)} async-done(((f32[64,2,128]{2,1,0:T(2,128)}), f32[64,2,128]{2,1,0:T(2,128)S(1)}, u32[]{:S(2)}, u32[]{:S(2)}) %all-to-all-start.1) | async-done | bytes 65568 | tf_op jit(solution)/shard_map/all_to_all | solution.py:482
  71.6 0.0 copy-done.1
  71.6 0.0 copy-done.7
  71.6 3.0 %branch_kernel.1 = (f32[128,2048]{1,0:T(8,128)}, f32[8,128]{1,0:T(8,128)S(1)}) custom-call(f32[128,2048]{1,0:T(8,128)} %get-tuple-element.34.refs_0_.refs_1_, f32[128,2048]{1,0:T(8,128)} %get-tuple-element.35.refs_1_, bf16[128,2048]{1,0:T(8,128)(2,1)S(1)} %bitcast.31, f32[1,2048]{1,0:T(1,128)S(1)} %bitcast.45, f32[16,8,128]{2,1,0:T(8,128)S(1)} %bitcast.41, ...), custom_call_target="tpu_custom_call" | custom-call | tf_op jit(solution)/shard_map/branch_kernel/pallas_call | solution.py:442
  74.6 2.5 %psum.14.refs_0_ = f32[8,128]{1,0:T(8,128)S(1)} all-reduce(f32[8,128]{1,0:T(8,128)S(1)} %get-tuple-element.38), channel_id=1, replica_groups=mesh['y'=4,'x'=4,'z'=16,'c'=2] {'c'}, use_global_device_ids=true, to_apply=%region_0.0 | all-reduce | flops 1024 | bytes 8192 | tf_op jit(solution)/shard_map/psum | solution.py:511
  77.1 3.1 %gate_kernel.1 = (f32[128,2048]{1,0:T(8,128)}, f32[16,8,128]{2,1,0:T(8,128)}, f32[2,8,2048]{2,1,0:T(8,128)S(1)}) custom-call(f32[8,128]{1,0:T(8,128)S(1)} %psum.14.refs_0_, f32[128,2048]{1,0:T(8,128)} %get-tuple-element.34.refs_0_.refs_1_, f32[128,2048]{1,0:T(8,128)} %get-tuple-element.39.refs_2_, bf16[128,2048]{1,0:T(8,128)(2,1)S(1)} %bitcast.32, ...), custom_call_target="tpu_custom_call" | custom-call | tf_op jit(solution)/shard_map/gate_kernel/pallas_call | solution.py:442
  80.2 11.0 %all-to-all-start.2 = ((f32[64,2,128]{2,1,0:T(2,128)}), f32[64,2,128]{2,1,0:T(2,128)S(1)}, u32[]{:S(2)}, u32[]{:S(2)}) async-start(f32[64,2,128]{2,1,0:T(2,128)} %bitcast.15), calls=%async_computation.2 | async-start | bytes 131072 | tf_op jit(solution)/shard_map/all_to_all | solution.py:471
  91.2 11.0 %adjoint_kernel.1 = (f32[128,2048]{1,0:T(8,128)}, f32[16,8,128]{2,1,0:T(8,128)S(1)}, f32[16,8,128]{2,1,0:T(8,128)S(1)}, f32[16,8,128]{2,1,0:T(8,128)S(1)}, f32[3,8,2048]{2,1,0:T(8,128)S(1)}) custom-call(f32[8,16]{1,0:T(8,128)S(1)} %get-tuple-element.72.refs_0_.rate, f32[16,8,128]{2,1,0:T(8,128)S(1)} %broadcast_in_dim.27.refs_0_.refs_5_.refs_1_, ...), custom_call_target="tpu_custom_call" | custom-call | flops 6000000000 | bytes 16000000 | tf_op jit(solution)/shard_map/adjoint_kernel/pallas_call | solution.py:442
  102.2 2.2 %all-to-all-done.2 = f32[64,2,128]{2,1,0:T(2,128)S(1)} async-done(((f32[64,2,128]{2,1,0:T(2,128)}), f32[64,2,128]{2,1,0:T(2,128)S(1)}, u32[]{:S(2)}, u32[]{:S(2)}) %all-to-all-start.2) | async-done | bytes 65568 | tf_op jit(solution)/shard_map/all_to_all | solution.py:471
  104.4 0.0 copy-start
  104.4 1.2 copy-done
  105.7 1.5 carry_back.1
  107.1 12.9 %all-to-all-start.3 = ((f32[64,2,128]{2,1,0:T(2,128)}), f32[64,2,128]{2,1,0:T(2,128)S(1)}, u32[]{:S(2)}, u32[]{:S(2)}) async-start(f32[64,2,128]{2,1,0:T(2,128)} %bitcast.17), calls=%async_computation.3 | async-start | bytes 131072 | tf_op jit(solution)/shard_map/all_to_all | solution.py:482
  120.1 4.9 %collective-permute-start.2 = (f32[3,8,2048]{2,1,0:T(8,128)S(1)}, f32[3,8,2048]{2,1,0:T(8,128)S(1)}, u32[]{:S(2)}, u32[]{:S(2)}) collective-permute-start(f32[3,8,2048]{2,1,0:T(8,128)S(1)} %get-tuple-element.48), channel_id=1, source_target_pairs={{2,0},{4,2},{6,4},{8,6},{10,8},{12,10},{14,12},{16,14},{18,16},{20... | collective-permute-start | bytes 589832 | tf_op jit(solution)/shard_map/ppermute | solution.py:424
  124.9 6.8 %outs_kernel.1 = (bf16[128,2048]{1,0:T(8,128)(2,1)}, f32[128,2048]{1,0:T(8,128)}, f32[16,32,128]{2,1,0:T(8,128)S(1)}) custom-call(f32[8,128]{1,0:T(8,128)S(1)} %psum.14.refs_0_, f32[128,2048]{1,0:T(8,128)} %get-tuple-element.34.refs_0_.refs_1_, f32[128,2048]{1,0:T(8,128)} %get-tuple-element.39.refs_2_, bf16[128,2048]{1,0:T(8,128)(2,1)S(1)} %bitcast.33, ...), custom_call_target="tpu_custom_call" | custom-call | flops 1000000000 | bytes 10000000 | tf_op jit(solution)/shard_map/outs_kernel/pallas_call | solution.py:442
  131.8 0.0 copy-start.6
  131.8 0.7 copy-done.6
  132.5 0.0 collective-permute-done.2.refs_8_.refs_7_
  132.5 0.5 all-to-all-done.3
  133.0 2.1 %sums_kernel.1 = f32[16,32,128]{2,1,0:T(8,128)S(1)} custom-call(f32[16,8,128]{2,1,0:T(8,128)S(1)} %bitcast.39, f32[16,8,128]{2,1,0:T(8,128)S(1)} %broadcast_in_dim.27.refs_0_.refs_5_.refs_1_, f32[8,2048]{1,0:T(8,128)S(1)} %copy-done.5, f32[16,8,128]{2,1,0:T(8,128)S(1)} %get-tuple-element.49.refs_3_, f32[16,8,128]{2,1,0:T(8,128)S(1)} %get-tuple-element.50.refs_4_, ...), custom_call_target="tpu_custom_call" | custom-call | tf_op jit(solution)/shard_map/sums_kernel/pallas_call | solution.py:442
  135.1 31.9 %all_to_all.30 = f32[64,8,128]{2,1,0:T(8,128)S(1)} all-to-all(f32[64,8,128]{2,1,0:T(8,128)S(1)} %bitcast.34), channel_id=1, replica_groups=mesh['y'=4,'x'=4,'z'=16,'c'=2] {'x','z'}, dimensions={0} | all-to-all | bytes 524288 | tf_op jit(solution)/shard_map/all_to_all | solution.py:551
  167.0 0.1 reduce_sum.9
  167.0 10.8 %psum.15 = f32[8,128]{1,0:T(8,128)S(1)} all-reduce(f32[8,128]{1,0:T(8,128)S(1)} %reduce_sum.9), channel_id=1, replica_groups=mesh['y'=4,'x'=4,'z'=16,'c'=2] {'y'}, use_global_device_ids=true, to_apply=%region_2.0 | all-reduce | flops 1024 | bytes 8192 | tf_op jit(solution)/shard_map/psum | solution.py:552
  177.8 0.7 broadcast_in_dim.33
  178.5 6.5 %all-to-all-start.5 = ((f32[64,8,128]{2,1,0:T(8,128)}), f32[64,8,128]{2,1,0:T(8,128)S(1)}, u32[]{:S(2)}, u32[]{:S(2)}) async-start(f32[64,8,128]{2,1,0:T(8,128)} %broadcast_in_dim.33), calls=%async_computation.5 | async-start | bytes 524288 | tf_op jit(solution)/shard_map/all_to_all | solution.py:553
  185.1 6.2 %finish_kernel.1 = bf16[3,128,2048]{2,1,0:T(8,128)(2,1)} custom-call(f32[8,16]{1,0:T(8,128)S(1)} %get-tuple-element.72.refs_0_.rate, f32[16,8,128]{2,1,0:T(8,128)S(1)} %bitcast.40, f32[16,1,128]{2,1,0:T(1,128)S(1)} %copy.18.refs_5_.refs_2_, f32[128,2048]{1,0:T(8,128)} %get-tuple-element.44.refs_8_.refs_0_.refs_3_, f32[128,2048]{1,0:T(8,128)} %get-tuple-element.47.refs_4_, ...), custom_call_target="tpu_custom_call" | custom-call | flops 1000000000 | bytes 10000000 | tf_op jit(solution)/shard_map/finish_kernel/pallas_call | solution.py:442
  191.3 11.0 %all-to-all-done.5 = f32[64,8,128]{2,1,0:T(8,128)S(1)} async-done(((f32[64,8,128]{2,1,0:T(8,128)}), f32[64,8,128]{2,1,0:T(8,128)S(1)}, u32[]{:S(2)}, u32[]{:S(2)}) %all-to-all-start.5) | async-done | bytes 262176 | tf_op jit(solution)/shard_map/all_to_all | solution.py:553
  202.3 0.7 unpack.1
  203.1 0.7 copy.20
  (3 shorter events, 0.1 us)
Async XLA Ops:
  1.5 14.4 %collective-permute-start = (bf16[3,8,2048]{2,1,0:T(8,128)(2,1)S(1)}, bf16[3,8,2048]{2,1,0:T(8,128)(2,1)S(1)}, u32[]{:S(2)}, u32[]{:S(2)}) collective-permute-start(bf16[3,8,2048]{2,1,0:T(8,128)(2,1)S(1)} %slice.8), channel_id=1, source_target_pairs={{0,2},{2,4},{4,6},{6,8},{8,10},{10,12},{12,14},{14,16},{16,18},{18... | collective-permute-start | bytes 294920 | tf_op jit(solution)/shard_map/ppermute | solution.py:424
  16.1 0.9 copy-start.3
  21.1 25.0 %all-to-all-start = ((f32[64,2,128]{2,1,0:T(2,128)}), f32[64,2,128]{2,1,0:T(2,128)S(1)}, u32[]{:S(2)}, u32[]{:S(2)}) async-start(f32[64,2,128]{2,1,0:T(2,128)} %bitcast.9), calls=%async_computation | async-start | bytes 131072 | tf_op jit(solution)/shard_map/all_to_all | solution.py:471
  33.1 10.2 %collective-permute-start.1 = (f32[2,8,2048]{2,1,0:T(8,128)S(1)}, f32[2,8,2048]{2,1,0:T(8,128)S(1)}, u32[]{:S(2)}, u32[]{:S(2)}) collective-permute-start(f32[2,8,2048]{2,1,0:T(8,128)S(1)} %get-tuple-element.37), channel_id=1, source_target_pairs={{2,0},{4,2},{6,4},{8,6},{10,8},{12,10},{14,12},{16,14},{18,16},{20... | collective-permute-start | bytes 393224 | tf_op jit(solution)/shard_map/ppermute | solution.py:424
  38.0 20.7 %copy-start.4 = (f32[7,3,2048]{2,0,1:T(8,128)S(1)}, f32[7,3,2048]{2,0,1:T(8,128)}, u32[]{:S(2)}) copy-start(f32[7,3,2048]{2,0,1:T(8,128)} %param.8) | copy-start | bytes 516100
  38.0 20.7 %copy-start.5 = (f32[8,2048]{1,0:T(8,128)S(1)}, f32[8,2048]{1,0:T(8,128)}, u32[]{:S(2)}) copy-start(f32[8,2048]{1,0:T(8,128)} %refs_2_.1) | copy-start | bytes 196612
  38.0 20.7 %copy-start.8 = (f32[2048]{0:T(1024)S(1)}, f32[2048]{0:T(1024)}, u32[]{:S(2)}) copy-start(f32[2048]{0:T(1024)} %param.11) | copy-start | bytes 24580
  46.1 1.2 copy-start.2
  48.7 22.9 %all-to-all-start.1 = ((f32[64,2,128]{2,1,0:T(2,128)}), f32[64,2,128]{2,1,0:T(2,128)S(1)}, u32[]{:S(2)}, u32[]{:S(2)}) async-start(f32[64,2,128]{2,1,0:T(2,128)} %bitcast.11), calls=%async_computation.1 | async-start | bytes 131072 | tf_op jit(solution)/shard_map/all_to_all | solution.py:482
  58.7 12.9 %copy-start.1 = (bf16[1,128,2048]{2,1,0:T(8,128)(2,1)S(1)}, bf16[1,128,2048]{2,1,0:T(8,128)(2,1)}, u32[]{:S(2)}) copy-start(bf16[1,128,2048]{2,1,0:T(8,128)(2,1)} %param.13) | copy-start | bytes 1572868
  58.7 12.9 %copy-start.7 = (f32[2048]{0:T(1024)S(1)}, f32[2048]{0:T(1024)}, u32[]{:S(2)}) copy-start(f32[2048]{0:T(1024)} %param.12) | copy-start | bytes 24580
  80.2 24.2 %all-to-all-start.2 = ((f32[64,2,128]{2,1,0:T(2,128)}), f32[64,2,128]{2,1,0:T(2,128)S(1)}, u32[]{:S(2)}, u32[]{:S(2)}) async-start(f32[64,2,128]{2,1,0:T(2,128)} %bitcast.15), calls=%async_computation.2 | async-start | bytes 131072 | tf_op jit(solution)/shard_map/all_to_all | solution.py:471
  104.4 1.2 copy-start
  107.1 25.9 %all-to-all-start.3 = ((f32[64,2,128]{2,1,0:T(2,128)}), f32[64,2,128]{2,1,0:T(2,128)S(1)}, u32[]{:S(2)}, u32[]{:S(2)}) async-start(f32[64,2,128]{2,1,0:T(2,128)} %bitcast.17), calls=%async_computation.3 | async-start | bytes 131072 | tf_op jit(solution)/shard_map/all_to_all | solution.py:482
  120.1 12.4 %collective-permute-start.2 = (f32[3,8,2048]{2,1,0:T(8,128)S(1)}, f32[3,8,2048]{2,1,0:T(8,128)S(1)}, u32[]{:S(2)}, u32[]{:S(2)}) collective-permute-start(f32[3,8,2048]{2,1,0:T(8,128)S(1)} %get-tuple-element.48), channel_id=1, source_target_pairs={{2,0},{4,2},{6,4},{8,6},{10,8},{12,10},{14,12},{16,14},{18,16},{20... | collective-permute-start | bytes 589832 | tf_op jit(solution)/shard_map/ppermute | solution.py:424
  131.8 0.7 copy-start.6
  178.5 23.8 %all-to-all-start.5 = ((f32[64,8,128]{2,1,0:T(8,128)}), f32[64,8,128]{2,1,0:T(8,128)S(1)}, u32[]{:S(2)}, u32[]{:S(2)}) async-start(f32[64,8,128]{2,1,0:T(8,128)} %broadcast_in_dim.33), calls=%async_computation.5 | async-start | bytes 524288 | tf_op jit(solution)/shard_map/all_to_all | solution.py:553

commit v4 on v3

--- a/solution.py
+++ b/solution.py
@@ -23,7 +23,9 @@
 C, G, W, S, V, O = "cols", "groups", "whole", "smem", "vmem", "order"
 ROWS = 32
 VMEM_MIB = 53
+ENDS_MIB = 53.6
 CTX = ("x", "z")
+YX = ("y", "x")
 
 
 def window(ref, kind, part):
@@ -106,7 +108,7 @@
 
 
 def params(mib):
-    return pltpu.CompilerParams(vmem_limit_bytes=mib * 1024 * 1024)
+    return pltpu.CompilerParams(vmem_limit_bytes=int(mib * 1024 * 1024))
 
 
 def iota(shape, dim):
@@ -118,6 +120,18 @@
     col = iota((L, 2 * L), 1) % L
     keep = col <= row if lower else col >= row
     return jnp.where(keep, 1.0, 0.0).astype(BF16)
+
+
+def powers(rate, sign):
+    column = iota((PAD, GS), 0).astype(F32)
+    table = jnp.exp((sign * rate) * column)
+    rows = PAD
+    while rows < L:
+        factor = jnp.exp(jnp.full((PAD, GS), sign * rows, F32) * rate)
+        more = jnp.concatenate([factor] * (rows // PAD), axis=0)
+        table = jnp.concatenate([table, table * more], axis=0)
+        rows *= 2
+    return table
 
 
 def split(x):
@@ -192,16 +206,15 @@
 
 def states_kernel(rate, feat, halo, taps, k, v, weight, skip, q_o, bl_o, s_o, ext):
     tri = ones_tri(True)
-    place = iota((L, GS), 0).astype(F32)
     def body(gi, cs):
         q_o[:, cs] = filtered(0, taps, feat, halo, cs, ext)
         prod = k[:, cs] * v[:, cs]
         modal = skip[0:1, cs] * prod
         for p in range(0, POLES, 2):
             rates = [rate[p + i, gi] for i in range(2)]
-            both = tri_dot(tri, [jnp.exp(place * r) * prod for r in rates])
+            both = tri_dot(tri, [powers(r, 1.0) * prod for r in rates])
             for i, r in enumerate(rates):
-                state = jnp.exp(place * (-r)) * both[:, i * GS : (i + 1) * GS]
+                state = powers(r, -1.0) * both[:, i * GS : (i + 1) * GS]
                 s_o[p + i, :, cs] = state
                 modal = modal + weight[p + i : p + i + 1, cs] * state
         bl_o[:, cs] = modal
@@ -301,10 +314,10 @@
         loc = once * own_in * heavy
         for p in range(0, POLES, 2):
             rates = [rate[p + i, gi] for i in range(2)]
-            both = tri_dot(tri, [jnp.exp(place * (-r)) * dbranch for r in rates])
+            both = tri_dot(tri, [powers(r, -1.0) * dbranch for r in rates])
             for i, r in enumerate(rates):
                 at = slice(p + i, p + i + 1)
-                adjoint = jnp.exp(place * r) * both[:, i * GS : (i + 1) * GS]
+                adjoint = powers(r, 1.0) * both[:, i * GS : (i + 1) * GS]
                 total = total + weight[at, cs] * adjoint
                 res_o[gi, at, :] = residue[at, :] + rowsum(prod * adjoint)
                 loc_o[gi, at, :] = loc[at, :] + rowsum(far_grad * states[p + i, :, cs] - far_prod * adjoint)
@@ -384,6 +397,10 @@
     return body, None
 
 
+def relay_kernel(parts, _, out):
+    out[...] = jnp.broadcast_to(jnp.sum(parts[...], axis=0, keepdims=True), out.shape)
+
+
 def unpack_kernel(pack, conv_o, rate_o, res_o, skip_o, gain_o):
     groups = pack.shape[0]
     for gi in range(groups):
@@ -447,7 +464,7 @@
             scratch_shapes=[pltpu.SemaphoreType.DMA((len(fetched) + len(outs), PARTS))]
             + [pltpu.VMEM(a.shape, a.dtype) for a in [*fetched, *outs]]
             + [pltpu.VMEM(d, F32) for d in extra],
-            compiler_params=params(VMEM_MIB),
+            compiler_params=params(ENDS_MIB if setup is ends_kernel else VMEM_MIB),
             cost_estimate=pl.CostEstimate(flops=flops, bytes_accessed=moved, transcendentals=special),
             name=setup.__name__,
         )(*args)
@@ -476,7 +493,7 @@
             in_specs=[smem(), smem(), vmem()] + [pl.BlockSpec(memory_space=pl.ANY)] * len(after),
             out_specs=vmem(),
             out_shape=shape(L, GS),
-            compiler_params=params(16),
+            compiler_params=params(VMEM_MIB),
             name="carry_back" if back else "carry_on",
         )(rate, where, rows, *after)
         given = lax.all_to_all(summed.reshape(count, 2, GS), CTX, 0, 0)
@@ -522,7 +539,7 @@
         moved=16_000_000,
         special=4_000_000,
     )
-    later = carried(rows_back, (dlocal,), True)
+    later = carried(rows_back, (loc_part,), True)
     rim = shifted(edge, -1)
 
     block_out, dquery, pack = call(
@@ -547,11 +564,19 @@
         moved=10_000_000,
     )[0]
 
-    share = groups * ROWS // count
-    parts = lax.all_to_all(pack.reshape(count, share, GS), CTX, 0, 0)
-    mine = lax.psum(jnp.sum(parts, axis=0), "y")
-    totals = lax.all_to_all(jnp.broadcast_to(mine[None], (count, share, GS)), CTX, 0, 0)
-    totals = totals.reshape(groups, ROWS, GS)
+    owned_rows = jnp.sum(lax.all_to_all(pack, YX, 0, 0), axis=0)
+    depth = lax.axis_size("z")
+    slices = owned_rows.reshape(depth, ROWS // depth, GS)
+    copies = pl.pallas_call(
+        relay_kernel,
+        in_specs=[vmem(), pl.BlockSpec(memory_space=pl.ANY)],
+        out_specs=vmem(),
+        out_shape=shape(*slices.shape),
+        compiler_params=params(VMEM_MIB),
+        name="relay",
+    )(lax.all_to_all(slices, "z", 0, 0), feature_grad)
+    whole = lax.all_to_all(copies, "z", 0, 0).reshape(ROWS, GS)
+    totals = lax.all_to_all(jnp.broadcast_to(whole[None], pack.shape), YX, 0, 0)
     conv, rate_grad, res, skip_grad, gain_grad = pl.pallas_call(
         unpack_kernel,
         out_shape=[shape(3, TAPS, channels), shape(groups, GS), shape(POLES, channels)] + [shape(1, channels)] * 2,

time: 205 us -> 199 us (0.971)
  local copies, waits for them, and re-layouts: 7.25 us -> 3.21 us
  waiting for transfers between devices: 30.5 us -> 26.7 us
    all_to_all x1 -> x3, blocking collectives: 31.9 us -> 43.4 us  [the longest x1 18.1 us: local(): whole = lax.all_to_all(copies, 'z', 0, 0).reshape(ROWS, GS)]
    psum x1 -> x0, blocking collectives: 10.8 us -> none  [local(): mine = lax.psum(jnp.sum(parts, axis=0), 'y')]
    all_to_all x1, waiting for transfers between devices: 11 us -> 6.3 us  [local(): lax.all_to_all(slices, 'z', 0, 0)]
    unnamed x19 -> x13, local copies, waits for them, and re-layouts: 4.73 us -> 1.39 us
where the time goes in v4:
time: 199 us; the launch traced here: 197 us
  starting transfers between devices  67.1 us (34%)
  Pallas kernels  53 us (27%)
  blocking collectives  45.9 us (23%)
  waiting for transfers between devices  26.7 us (13%)
  local copies, waits for them, and re-layouts  3.21 us (2%)
    pallas_call x9, Pallas kernels, call(): pl.pallas_call(functools.partial(streamed, setup, kinds_in, kinds_out), i...  49.4 us
    all_to_all x2, starting transfers between devices, owned(): return lax.all_to_all(rows.reshape(count, 2, GS), CTX, 0, 0).reshape(L, GS)  22.7 us
    all_to_all x2, starting transfers between devices, carried(): given = lax.all_to_all(summed.reshape(count, 2, GS), CTX, 0, 0)  22.4 us
    all_to_all x1, blocking collectives, local(): whole = lax.all_to_all(copies, 'z', 0, 0).reshape(ROWS, GS)  18.1 us
    all_to_all x1, blocking collectives, local(): owned_rows = jnp.sum(lax.all_to_all(pack, YX, 0, 0), axis=0)  13.7 us
    ppermute x3, starting transfers between devices, shifted(): return lax.ppermute(value, CTX, pairs)  13.6 us
    all_to_all x1, blocking collectives, local(): totals = lax.all_to_all(jnp.broadcast_to(whole[None], pack.shape), YX, 0, 0)  11.6 us
    ppermute x3, waiting for transfers between devices, shifted(): return lax.ppermute(value, CTX, pairs)  9.8 us
  transfers between devices with their start and end apart: 8, of which 6 were waited for; matrix products, arithmetic and copies ran while one was open for 0% of the time, Pallas kernels for 19%

profile of v4, /device:TPU:6, one launch (start us, length us, event | category | flops | bytes accessed | tf_op | source)
XLA Modules:
  0.0 197.4 jit_solution(1281421482104637642)
XLA Ops:
  0.6 0.9 slice.8
  1.5 3.8 %collective-permute-start = (bf16[3,8,2048]{2,1,0:T(8,128)(2,1)S(1)}, bf16[3,8,2048]{2,1,0:T(8,128)(2,1)S(1)}, u32[]{:S(2)}, u32[]{:S(2)}) collective-permute-start(bf16[3,8,2048]{2,1,0:T(8,128)(2,1)S(1)} %slice.8), channel_id=1, source_target_pairs={{0,2},{2,4},{4,6},{6,8},{8,10},{10,12},{12,14},{14,16},{16,18},{18... | collective-permute-start | bytes 294920 | tf_op jit(solution)/shard_map/ppermute | solution.py:441
  5.4 0.7 exponential_bitcast_fusion
  6.1 0.1 copy.17
  6.2 9.8 %collective-permute-done.refs_2_.refs_4_.refs_11_ = bf16[3,8,2048]{2,1,0:T(8,128)(2,1)S(1)} collective-permute-done((bf16[3,8,2048]{2,1,0:T(8,128)(2,1)S(1)}, bf16[3,8,2048]{2,1,0:T(8,128)(2,1)S(1)}, u32[]{:S(2)}, u32[]{:S(2)}) %collective-permute-start) | collective-permute-done | bytes 98336 | tf_op jit(solution)/shard_map/ppermute | solution.py:441
  16.0 0.1 broadcast_in_dim.28.refs_0_.refs_5_.refs_1_
  16.1 4.1 %ends_kernel.1 = (f32[128,2048]{1,0:T(8,128)}, f32[128,2048]{1,0:T(8,128)}, f32[16,8,128]{2,1,0:T(8,128)}, f32[2,8,2048]{2,1,0:T(8,128)}) custom-call(f32[16,8,128]{2,1,0:T(8,128)S(1)} %broadcast_in_dim.28.refs_0_.refs_5_.refs_1_, bf16[3,128,2048]{2,1,0:T(8,128)(2,1)} %bitcast.49, bf16[3,8,2048]{2,1,0:T(8,128)(2,1)S(1)} %collective-permute-done.refs_2_.refs_4_.refs_11_, ...), custom_call_target="tpu_custom_call" | custom-call | tf_op jit(solution)/shard_map/ends_kernel/pallas_call | solution.py:459
  20.1 12.1 %all-to-all-start = ((f32[64,2,128]{2,1,0:T(2,128)}), f32[64,2,128]{2,1,0:T(2,128)S(1)}, u32[]{:S(2)}, u32[]{:S(2)}) async-start(f32[64,2,128]{2,1,0:T(2,128)} %bitcast.9), calls=%async_computation | async-start | bytes 131072 | tf_op jit(solution)/shard_map/all_to_all | solution.py:488
  32.2 4.9 %collective-permute-start.1 = (f32[2,8,2048]{2,1,0:T(8,128)}, f32[2,8,2048]{2,1,0:T(8,128)S(1)}, u32[]{:S(2)}, u32[]{:S(2)}) collective-permute-start(f32[2,8,2048]{2,1,0:T(8,128)} %get-tuple-element.37), channel_id=1, source_target_pairs={{2,0},{4,2},{6,4},{8,6},{10,8},{12,10},{14,12},{16,14},{18,16},{20... | collective-permute-start | bytes 393224 | tf_op jit(solution)/shard_map/ppermute | solution.py:441
  37.1 0.0 copy-start.1
  37.1 0.0 copy-start.2
  37.1 0.0 copy-start.5
  37.1 5.2 %coefs_kernel.1.refs_0_.refs_5_ = f32[16,112,128]{2,1,0:T(8,128)} custom-call(f32[16,8,128]{2,1,0:T(8,128)S(1)} %broadcast_in_dim.28.refs_0_.refs_5_.refs_1_, f32[128,2048]{1,0:T(8,128)} %get-tuple-element.32.refs_4_.refs_1_.refs_3_.refs_5_, f32[128,2048]{1,0:T(8,128)} %get-tuple-element.33.refs_5_.refs_2_.refs_4_.refs_6_, bf16[3,128,2048]{2,1,0:T(8,128)(2,1)} %bitcast.50, ...), custom_call_target="tpu_custom_call" | custom-call | flops 4000000000 | bytes 4000000 | tf_op jit(solution)/shard_map/coefs_kernel/pallas_call | solution.py:459
  42.4 0.0 collective-permute-done.1.refs_1_.refs_9_
  42.4 2.8 %all-to-all-done = f32[64,2,128]{2,1,0:T(2,128)S(1)} async-done(((f32[64,2,128]{2,1,0:T(2,128)}), f32[64,2,128]{2,1,0:T(2,128)S(1)}, u32[]{:S(2)}, u32[]{:S(2)}) %all-to-all-start) | async-done | bytes 65568 | tf_op jit(solution)/shard_map/all_to_all | solution.py:488
  45.1 1.5 carry_on.1
  46.6 10.0 %all-to-all-start.1 = ((f32[64,2,128]{2,1,0:T(2,128)}), f32[64,2,128]{2,1,0:T(2,128)S(1)}, u32[]{:S(2)}, u32[]{:S(2)}) async-start(f32[64,2,128]{2,1,0:T(2,128)} %bitcast.11), calls=%async_computation.1 | async-start | bytes 131072 | tf_op jit(solution)/shard_map/all_to_all | solution.py:499
  56.6 0.0 copy-done.1
  56.6 0.0 copy-done.2
  56.6 0.0 copy-done.5
  56.6 0.0 copy-start
  56.6 0.0 copy-start.4
  56.6 8.2 %states_kernel.1 = (f32[128,2048]{1,0:T(8,128)}, f32[128,2048]{1,0:T(8,128)}, f32[8,128,2048]{2,1,0:T(8,128)}) custom-call(f32[8,16]{1,0:T(8,128)S(1)} %get-tuple-element.72.refs_0_.rate, bf16[3,128,2048]{2,1,0:T(8,128)(2,1)} %bitcast.51, bf16[3,8,2048]{2,1,0:T(8,128)(2,1)S(1)} %collective-permute-done.refs_2_.refs_4_.refs_11_, f32[3,7,2048]{2,1,0:T(8,128)S(1)} %bitcast.35, ...), custom_call_target="tpu_custom_call" | custom-call | flops 4000000000 | bytes 14000000 | tf_op jit(solution)/shard_map/states_kernel/pallas_call | solution.py:459
  64.9 4.6 %all-to-all-done.1 = f32[64,2,128]{2,1,0:T(2,128)S(1)} async-done(((f32[64,2,128]{2,1,0:T(2,128)}), f32[64,2,128]{2,1,0:T(2,128)S(1)}, u32[]{:S(2)}, u32[]{:S(2)}) %all-to-all-start.1) | async-done | bytes 65568 | tf_op jit(solution)/shard_map/all_to_all | solution.py:499
  69.5 0.0 copy-done
  69.5 0.0 copy-done.4
  69.5 3.0 %branch_kernel.1 = (f32[128,2048]{1,0:T(8,128)}, f32[8,128]{1,0:T(8,128)S(1)}) custom-call(f32[128,2048]{1,0:T(8,128)} %get-tuple-element.34.refs_0_.refs_1_, f32[128,2048]{1,0:T(8,128)} %get-tuple-element.35.refs_1_, bf16[128,2048]{1,0:T(8,128)(2,1)S(1)} %bitcast.31, f32[1,2048]{1,0:T(1,128)S(1)} %bitcast.43, f32[16,8,128]{2,1,0:T(8,128)S(1)} %bitcast.39, ...), custom_call_target="tpu_custom_call" | custom-call | tf_op jit(solution)/shard_map/branch_kernel/pallas_call | solution.py:459
  72.5 2.5 %psum.7.refs_0_ = f32[8,128]{1,0:T(8,128)S(1)} all-reduce(f32[8,128]{1,0:T(8,128)S(1)} %get-tuple-element.38), channel_id=1, replica_groups=mesh['y'=4,'x'=4,'z'=16,'c'=2] {'c'}, use_global_device_ids=true, to_apply=%region_0.0 | all-reduce | flops 1024 | bytes 8192 | tf_op jit(solution)/shard_map/psum | solution.py:528
  75.0 3.1 %gate_kernel.1 = (f32[128,2048]{1,0:T(8,128)}, f32[16,8,128]{2,1,0:T(8,128)}, f32[2,8,2048]{2,1,0:T(8,128)S(1)}) custom-call(f32[8,128]{1,0:T(8,128)S(1)} %psum.7.refs_0_, f32[128,2048]{1,0:T(8,128)} %get-tuple-element.34.refs_0_.refs_1_, f32[128,2048]{1,0:T(8,128)} %get-tuple-element.39.refs_2_, bf16[128,2048]{1,0:T(8,128)(2,1)S(1)} %bitcast.32, ...), custom_call_target="tpu_custom_call" | custom-call | tf_op jit(solution)/shard_map/gate_kernel/pallas_call | solution.py:459
  78.1 10.6 %all-to-all-start.2 = ((f32[64,2,128]{2,1,0:T(2,128)}), f32[64,2,128]{2,1,0:T(2,128)S(1)}, u32[]{:S(2)}, u32[]{:S(2)}) async-start(f32[64,2,128]{2,1,0:T(2,128)} %bitcast.15), calls=%async_computation.2 | async-start | bytes 131072 | tf_op jit(solution)/shard_map/all_to_all | solution.py:488
  88.7 10.5 %adjoint_kernel.1 = (f32[128,2048]{1,0:T(8,128)}, f32[16,8,128]{2,1,0:T(8,128)S(1)}, f32[16,8,128]{2,1,0:T(8,128)S(1)}, f32[16,8,128]{2,1,0:T(8,128)S(1)}, f32[3,8,2048]{2,1,0:T(8,128)S(1)}) custom-call(f32[8,16]{1,0:T(8,128)S(1)} %get-tuple-element.72.refs_0_.rate, f32[16,8,128]{2,1,0:T(8,128)S(1)} %broadcast_in_dim.28.refs_0_.refs_5_.refs_1_, ...), custom_call_target="tpu_custom_call" | custom-call | flops 6000000000 | bytes 16000000 | tf_op jit(solution)/shard_map/adjoint_kernel/pallas_call | solution.py:459
  99.2 2.7 %all-to-all-done.2 = f32[64,2,128]{2,1,0:T(2,128)S(1)} async-done(((f32[64,2,128]{2,1,0:T(2,128)}), f32[64,2,128]{2,1,0:T(2,128)S(1)}, u32[]{:S(2)}, u32[]{:S(2)}) %all-to-all-start.2) | async-done | bytes 65568 | tf_op jit(solution)/shard_map/all_to_all | solution.py:488
  102.0 1.5 carry_back.1
  103.4 12.4 %all-to-all-start.3 = ((f32[64,2,128]{2,1,0:T(2,128)}), f32[64,2,128]{2,1,0:T(2,128)S(1)}, u32[]{:S(2)}, u32[]{:S(2)}) async-start(f32[64,2,128]{2,1,0:T(2,128)} %bitcast.17), calls=%async_computation.3 | async-start | bytes 131072 | tf_op jit(solution)/shard_map/all_to_all | solution.py:499
  115.9 4.9 %collective-permute-start.2 = (f32[3,8,2048]{2,1,0:T(8,128)S(1)}, f32[3,8,2048]{2,1,0:T(8,128)S(1)}, u32[]{:S(2)}, u32[]{:S(2)}) collective-permute-start(f32[3,8,2048]{2,1,0:T(8,128)S(1)} %get-tuple-element.49), channel_id=1, source_target_pairs={{2,0},{4,2},{6,4},{8,6},{10,8},{12,10},{14,12},{16,14},{18,16},{20... | collective-permute-start | bytes 589832 | tf_op jit(solution)/shard_map/ppermute | solution.py:441
  120.7 6.8 %outs_kernel.1 = (bf16[128,2048]{1,0:T(8,128)(2,1)}, f32[128,2048]{1,0:T(8,128)}, f32[16,32,128]{2,1,0:T(8,128)S(1)}) custom-call(f32[8,128]{1,0:T(8,128)S(1)} %psum.7.refs_0_, f32[128,2048]{1,0:T(8,128)} %get-tuple-element.34.refs_0_.refs_1_, f32[128,2048]{1,0:T(8,128)} %get-tuple-element.39.refs_2_, bf16[128,2048]{1,0:T(8,128)(2,1)S(1)} %bitcast.33, ...), custom_call_target="tpu_custom_call" | custom-call | flops 1000000000 | bytes 10000000 | tf_op jit(solution)/shard_map/outs_kernel/pallas_call | solution.py:459
  127.6 0.0 copy-start.3
  127.6 0.7 copy-done.3
  128.3 0.0 collective-permute-done.2.refs_8_.refs_7_
  128.3 0.5 all-to-all-done.3
  128.8 2.1 %sums_kernel.1 = f32[16,32,128]{2,1,0:T(8,128)S(1)} custom-call(f32[16,8,128]{2,1,0:T(8,128)S(1)} %bitcast.37, f32[16,8,128]{2,1,0:T(8,128)S(1)} %broadcast_in_dim.28.refs_0_.refs_5_.refs_1_, f32[8,2048]{1,0:T(8,128)S(1)} %copy-done.2, f32[16,8,128]{2,1,0:T(8,128)S(1)} %get-tuple-element.47.refs_0_.refs_3_, f32[16,8,128]{2,1,0:T(8,128)S(1)} %get-tuple-element.50.refs_4_, ...), custom_call_target="tpu_custom_call" | custom-call | tf_op jit(solution)/shard_map/sums_kernel/pallas_call | solution.py:459
  130.9 13.7 %all_to_all.40 = f32[16,32,128]{2,1,0:T(8,128)S(1)} all-to-all(f32[16,32,128]{2,1,0:T(8,128)S(1)} %sums_kernel.1), channel_id=1, replica_groups=mesh['y'=4,'x'=4,'z'=16,'c'=2] {'y','x'}, dimensions={0} | all-to-all | bytes 524288 | tf_op jit(solution)/shard_map/all_to_all | solution.py:567
  144.6 0.6 reduce_sum.9
  145.2 8.5 %all-to-all-start.5 = ((f32[16,2,128]{2,1,0:T(2,128)}), f32[16,2,128]{2,1,0:T(2,128)S(1)}, u32[]{:S(2)}, u32[]{:S(2)}) async-start(f32[16,2,128]{2,1,0:T(2,128)} %bitcast.21), calls=%async_computation.5 | async-start | bytes 32768 | tf_op jit(solution)/shard_map/all_to_all | solution.py:577
  153.7 6.2 %finish_kernel.1._ = bf16[3,128,2048]{2,1,0:T(8,128)(2,1)} custom-call(f32[8,16]{1,0:T(8,128)S(1)} %get-tuple-element.72.refs_0_.rate, f32[16,8,128]{2,1,0:T(8,128)S(1)} %bitcast.38, f32[16,1,128]{2,1,0:T(1,128)S(1)} %copy.18.refs_5_.refs_2_, f32[128,2048]{1,0:T(8,128)} %get-tuple-element.44.refs_8_.refs_3_, f32[128,2048]{1,0:T(8,128)} %get-tuple-element.48.refs_4_, ...), custom_call_target="tpu_custom_call" | custom-call | flops 1000000000 | bytes 10000000 | tf_op jit(solution)/shard_map/finish_kernel/pallas_call | solution.py:459
  159.9 6.3 %all-to-all-done.5.parts = f32[16,2,128]{2,1,0:T(2,128)S(1)} async-done(((f32[16,2,128]{2,1,0:T(2,128)}), f32[16,2,128]{2,1,0:T(2,128)S(1)}, u32[]{:S(2)}, u32[]{:S(2)}) %all-to-all-start.5) | async-done | bytes 16416 | tf_op jit(solution)/shard_map/all_to_all | solution.py:577
  166.3 18.1 %all_to_all.41 = f32[16,2,128]{2,1,0:T(2,128)S(1)} all-to-all(f32[16,2,128]{2,1,0:T(2,128)S(1)} %relay.1), channel_id=1, replica_groups=mesh['y'=4,'x'=4,'z'=16,'c'=2] {'z'}, dimensions={0} | all-to-all | bytes 32768 | tf_op jit(solution)/shard_map/all_to_all | solution.py:578
  184.4 11.6 %all_to_all.42.pack = f32[16,32,128]{2,1,0:T(8,128)S(1)} all-to-all(f32[16,32,128]{2,1,0:T(8,128)S(1)} %broadcast_in_dim.35), channel_id=1, replica_groups=mesh['y'=4,'x'=4,'z'=16,'c'=2] {'y','x'}, dimensions={0} | all-to-all | bytes 524288 | tf_op jit(solution)/shard_map/all_to_all | solution.py:579
  196.0 0.7 unpack.1
  196.7 0.7 copy.20
  (5 shorter events, 0.1 us)
Async XLA Ops:
  1.5 14.4 %collective-permute-start = (bf16[3,8,2048]{2,1,0:T(8,128)(2,1)S(1)}, bf16[3,8,2048]{2,1,0:T(8,128)(2,1)S(1)}, u32[]{:S(2)}, u32[]{:S(2)}) collective-permute-start(bf16[3,8,2048]{2,1,0:T(8,128)(2,1)S(1)} %slice.8), channel_id=1, source_target_pairs={{0,2},{2,4},{4,6},{6,8},{8,10},{10,12},{12,14},{14,16},{16,18},{18... | collective-permute-start | bytes 294920 | tf_op jit(solution)/shard_map/ppermute | solution.py:441
  20.1 25.0 %all-to-all-start = ((f32[64,2,128]{2,1,0:T(2,128)}), f32[64,2,128]{2,1,0:T(2,128)S(1)}, u32[]{:S(2)}, u32[]{:S(2)}) async-start(f32[64,2,128]{2,1,0:T(2,128)} %bitcast.9), calls=%async_computation | async-start | bytes 131072 | tf_op jit(solution)/shard_map/all_to_all | solution.py:488
  32.2 10.2 %collective-permute-start.1 = (f32[2,8,2048]{2,1,0:T(8,128)}, f32[2,8,2048]{2,1,0:T(8,128)S(1)}, u32[]{:S(2)}, u32[]{:S(2)}) collective-permute-start(f32[2,8,2048]{2,1,0:T(8,128)} %get-tuple-element.37), channel_id=1, source_target_pairs={{2,0},{4,2},{6,4},{8,6},{10,8},{12,10},{14,12},{16,14},{18,16},{20... | collective-permute-start | bytes 393224 | tf_op jit(solution)/shard_map/ppermute | solution.py:441
  37.1 19.5 %copy-start.1 = (f32[7,3,2048]{2,0,1:T(8,128)S(1)}, f32[7,3,2048]{2,0,1:T(8,128)}, u32[]{:S(2)}) copy-start(f32[7,3,2048]{2,0,1:T(8,128)} %param.8) | copy-start | bytes 516100
  37.1 19.5 %copy-start.2 = (f32[8,2048]{1,0:T(8,128)S(1)}, f32[8,2048]{1,0:T(8,128)}, u32[]{:S(2)}) copy-start(f32[8,2048]{1,0:T(8,128)} %refs_2_.1) | copy-start | bytes 196612
  37.1 19.5 %copy-start.5 = (f32[2048]{0:T(1024)S(1)}, f32[2048]{0:T(1024)}, u32[]{:S(2)}) copy-start(f32[2048]{0:T(1024)} %param.11) | copy-start | bytes 24580
  46.6 22.9 %all-to-all-start.1 = ((f32[64,2,128]{2,1,0:T(2,128)}), f32[64,2,128]{2,1,0:T(2,128)S(1)}, u32[]{:S(2)}, u32[]{:S(2)}) async-start(f32[64,2,128]{2,1,0:T(2,128)} %bitcast.11), calls=%async_computation.1 | async-start | bytes 131072 | tf_op jit(solution)/shard_map/all_to_all | solution.py:499
  56.6 12.9 %copy-start = (bf16[1,128,2048]{2,1,0:T(8,128)(2,1)S(1)}, bf16[1,128,2048]{2,1,0:T(8,128)(2,1)}, u32[]{:S(2)}) copy-start(bf16[1,128,2048]{2,1,0:T(8,128)(2,1)} %param.13) | copy-start | bytes 1572868
  56.6 12.9 %copy-start.4 = (f32[2048]{0:T(1024)S(1)}, f32[2048]{0:T(1024)}, u32[]{:S(2)}) copy-start(f32[2048]{0:T(1024)} %param.12) | copy-start | bytes 24580
  78.1 23.9 %all-to-all-start.2 = ((f32[64,2,128]{2,1,0:T(2,128)}), f32[64,2,128]{2,1,0:T(2,128)S(1)}, u32[]{:S(2)}, u32[]{:S(2)}) async-start(f32[64,2,128]{2,1,0:T(2,128)} %bitcast.15), calls=%async_computation.2 | async-start | bytes 131072 | tf_op jit(solution)/shard_map/all_to_all | solution.py:488
  103.4 25.4 %all-to-all-start.3 = ((f32[64,2,128]{2,1,0:T(2,128)}), f32[64,2,128]{2,1,0:T(2,128)S(1)}, u32[]{:S(2)}, u32[]{:S(2)}) async-start(f32[64,2,128]{2,1,0:T(2,128)} %bitcast.17), calls=%async_computation.3 | async-start | bytes 131072 | tf_op jit(solution)/shard_map/all_to_all | solution.py:499
  115.9 12.4 %collective-permute-start.2 = (f32[3,8,2048]{2,1,0:T(8,128)S(1)}, f32[3,8,2048]{2,1,0:T(8,128)S(1)}, u32[]{:S(2)}, u32[]{:S(2)}) collective-permute-start(f32[3,8,2048]{2,1,0:T(8,128)S(1)} %get-tuple-element.49), channel_id=1, source_target_pairs={{2,0},{4,2},{6,4},{8,6},{10,8},{12,10},{14,12},{16,14},{18,16},{20... | collective-permute-start | bytes 589832 | tf_op jit(solution)/shard_map/ppermute | solution.py:441
  127.6 0.7 copy-start.3
  145.2 21.0 %all-to-all-start.5 = ((f32[16,2,128]{2,1,0:T(2,128)}), f32[16,2,128]{2,1,0:T(2,128)S(1)}, u32[]{:S(2)}, u32[]{:S(2)}) async-start(f32[16,2,128]{2,1,0:T(2,128)} %bitcast.21), calls=%async_computation.5 | async-start | bytes 32768 | tf_op jit(solution)/shard_map/all_to_all | solution.py:577

commit v5 on v4

--- a/solution.py
+++ b/solution.py
@@ -397,7 +397,8 @@
     return body, None
 
 
-def relay_kernel(parts, _, out):
+def relay_kernel(parts, *refs):
+    out = refs[-1]
     out[...] = jnp.broadcast_to(jnp.sum(parts[...], axis=0, keepdims=True), out.shape)
 
 
@@ -410,7 +411,8 @@
         res_o[:, cs] = pack[gi, 21:29, :]
         skip_o[0:1, cs] = pack[gi, 29:30, :]
         gain_o[0:1, cs] = pack[gi, 30:31, :]
-        rate_o[gi : gi + 1, :] = pack[gi, 31:32, :]
+    rates = jnp.concatenate([pack[gi, 31:32, :] for gi in range(groups)], axis=0)
+    rate_o[...] = rates.T[0:POLES, :]
 
 
 def smem():
@@ -564,22 +566,22 @@
         moved=10_000_000,
     )[0]
 
-    owned_rows = jnp.sum(lax.all_to_all(pack, YX, 0, 0), axis=0)
-    depth = lax.axis_size("z")
-    slices = owned_rows.reshape(depth, ROWS // depth, GS)
-    copies = pl.pallas_call(
-        relay_kernel,
-        in_specs=[vmem(), pl.BlockSpec(memory_space=pl.ANY)],
-        out_specs=vmem(),
-        out_shape=shape(*slices.shape),
-        compiler_params=params(VMEM_MIB),
-        name="relay",
-    )(lax.all_to_all(slices, "z", 0, 0), feature_grad)
-    whole = lax.all_to_all(copies, "z", 0, 0).reshape(ROWS, GS)
-    totals = lax.all_to_all(jnp.broadcast_to(whole[None], pack.shape), YX, 0, 0)
+    def summed_copies(parts, after, name):
+        return pl.pallas_call(
+            relay_kernel,
+            in_specs=[vmem()] + [pl.BlockSpec(memory_space=pl.ANY)] * len(after),
+            out_specs=vmem(),
+            out_shape=shape(*parts.shape),
+            compiler_params=params(VMEM_MIB),
+            name=name,
+        )(parts, *after)
+
+    owned_rows = summed_copies(lax.all_to_all(pack, YX, 0, 0), (), "add_over_yx")
+    everyone = lax.all_to_all(owned_rows, "z", 0, 0)
+    totals = lax.all_to_all(summed_copies(everyone, (feature_grad,), "add_over_z"), YX, 0, 0)
     conv, rate_grad, res, skip_grad, gain_grad = pl.pallas_call(
         unpack_kernel,
-        out_shape=[shape(3, TAPS, channels), shape(groups, GS), shape(POLES, channels)] + [shape(1, channels)] * 2,
+        out_shape=[shape(3, TAPS, channels), shape(POLES, groups), shape(POLES, channels)] + [shape(1, channels)] * 2,
         compiler_params=params(16),
         name="unpack",
     )(totals)
@@ -587,7 +589,7 @@
         block_out[None],
         feature_grad.transpose(1, 0, 2)[None],
         conv.transpose(1, 0, 2),
-        rate_grad[:, :POLES].T,
+        rate_grad,
         res,
         skip_grad[0],
         gain_grad[0],

time: 199 us -> 186 us (0.935)
  blocking collectives: 45.9 us -> 27.9 us
  waiting for transfers between devices: 26.7 us -> 30.2 us
    all_to_all x3 -> x2, blocking collectives: 43.4 us -> 25.4 us  [the longest x1 13.7 us: local(): lax.all_to_all(pack, YX, 0, 0)]
    all_to_all x1, waiting for transfers between devices: 6.3 us -> 9.89 us  [local(): everyone = lax.all_to_all(owned_rows, 'z', 0, 0)]
  transfers between devices with their start and end apart: 8 -> 8, of which waited for: 6 -> 6; matrix products, arithmetic and copies ran while one was open for 0% -> 0% of each run, Pallas kernels for 19% -> 20%
where the time goes in v5:
time: 186 us; the launch traced here: 182 us
  starting transfers between devices  67.1 us (36%)
  Pallas kernels  53.9 us (29%)
  waiting for transfers between devices  30.2 us (16%)
  blocking collectives  27.9 us (15%)
  local copies, waits for them, and re-layouts  2.53 us (1%)
    pallas_call x9, Pallas kernels, call(): pl.pallas_call(functools.partial(streamed, setup, kinds_in, kinds_out), i...  49.4 us
    all_to_all x2, starting transfers between devices, owned(): return lax.all_to_all(rows.reshape(count, 2, GS), CTX, 0, 0).reshape(L, GS)  22.7 us
    all_to_all x2, starting transfers between devices, carried(): given = lax.all_to_all(summed.reshape(count, 2, GS), CTX, 0, 0)  22.4 us
    all_to_all x1, blocking collectives, local(): lax.all_to_all(pack, YX, 0, 0)  13.7 us
    ppermute x3, starting transfers between devices, shifted(): return lax.ppermute(value, CTX, pairs)  13.6 us
    all_to_all x1, blocking collectives, local(): lax.all_to_all(summed_copies(everyone, (feature_grad,), 'add_over_z'), YX...  11.7 us
    all_to_all x1, waiting for transfers between devices, local(): everyone = lax.all_to_all(owned_rows, 'z', 0, 0)  9.89 us
    ppermute x3, waiting for transfers between devices, shifted(): return lax.ppermute(value, CTX, pairs)  9.8 us
  transfers between devices with their start and end apart: 8, of which 6 were waited for; matrix products, arithmetic and copies ran while one was open for 0% of the time, Pallas kernels for 20%

profile of v5, /device:TPU:6, one launch (start us, length us, event | category | flops | bytes accessed | tf_op | source)
XLA Modules:
  0.0 182.5 jit_solution(3921243602594987389)
XLA Ops:
  0.6 0.9 slice.4
  1.5 3.8 %collective-permute-start = (bf16[3,8,2048]{2,1,0:T(8,128)(2,1)S(1)}, bf16[3,8,2048]{2,1,0:T(8,128)(2,1)S(1)}, u32[]{:S(2)}, u32[]{:S(2)}) collective-permute-start(bf16[3,8,2048]{2,1,0:T(8,128)(2,1)S(1)} %slice.4), channel_id=1, source_target_pairs={{0,2},{2,4},{4,6},{6,8},{8,10},{10,12},{12,14},{14,16},{16,18},{18... | collective-permute-start | bytes 294920 | tf_op jit(solution)/shard_map/ppermute | solution.py:443
  5.4 0.7 exponential_bitcast_fusion
  6.1 0.1 copy.16
  6.2 9.8 %collective-permute-done.refs_2_.refs_4_.refs_11_ = bf16[3,8,2048]{2,1,0:T(8,128)(2,1)S(1)} collective-permute-done((bf16[3,8,2048]{2,1,0:T(8,128)(2,1)S(1)}, bf16[3,8,2048]{2,1,0:T(8,128)(2,1)S(1)}, u32[]{:S(2)}, u32[]{:S(2)}) %collective-permute-start) | collective-permute-done | bytes 98336 | tf_op jit(solution)/shard_map/ppermute | solution.py:443
  16.0 0.1 broadcast_in_dim.21.refs_0_.refs_5_.refs_1_
  16.1 4.1 %ends_kernel.1 = (f32[128,2048]{1,0:T(8,128)}, f32[128,2048]{1,0:T(8,128)}, f32[16,8,128]{2,1,0:T(8,128)}, f32[2,8,2048]{2,1,0:T(8,128)}) custom-call(f32[16,8,128]{2,1,0:T(8,128)S(1)} %broadcast_in_dim.21.refs_0_.refs_5_.refs_1_, bf16[3,128,2048]{2,1,0:T(8,128)(2,1)} %bitcast.45, bf16[3,8,2048]{2,1,0:T(8,128)(2,1)S(1)} %collective-permute-done.refs_2_.refs_4_.refs_11_, ...), custom_call_target="tpu_custom_call" | custom-call | tf_op jit(solution)/shard_map/ends_kernel/pallas_call | solution.py:461
  20.1 12.1 %all-to-all-start = ((f32[64,2,128]{2,1,0:T(2,128)}), f32[64,2,128]{2,1,0:T(2,128)S(1)}, u32[]{:S(2)}, u32[]{:S(2)}) async-start(f32[64,2,128]{2,1,0:T(2,128)} %bitcast.9), calls=%async_computation | async-start | bytes 131072 | tf_op jit(solution)/shard_map/all_to_all | solution.py:490
  32.2 4.9 %collective-permute-start.1 = (f32[2,8,2048]{2,1,0:T(8,128)}, f32[2,8,2048]{2,1,0:T(8,128)S(1)}, u32[]{:S(2)}, u32[]{:S(2)}) collective-permute-start(f32[2,8,2048]{2,1,0:T(8,128)} %get-tuple-element.37), channel_id=1, source_target_pairs={{2,0},{4,2},{6,4},{8,6},{10,8},{12,10},{14,12},{16,14},{18,16},{20... | collective-permute-start | bytes 393224 | tf_op jit(solution)/shard_map/ppermute | solution.py:443
  37.1 0.0 copy-start.1
  37.1 0.0 copy-start.2
  37.1 0.0 copy-start.5
  37.1 5.2 %coefs_kernel.1.refs_0_.refs_5_ = f32[16,112,128]{2,1,0:T(8,128)} custom-call(f32[16,8,128]{2,1,0:T(8,128)S(1)} %broadcast_in_dim.21.refs_0_.refs_5_.refs_1_, f32[128,2048]{1,0:T(8,128)} %get-tuple-element.32.refs_4_.refs_1_.refs_3_.refs_5_, f32[128,2048]{1,0:T(8,128)} %get-tuple-element.33.refs_5_.refs_2_.refs_4_.refs_6_, bf16[3,128,2048]{2,1,0:T(8,128)(2,1)} %bitcast.46, ...), custom_call_target="tpu_custom_call" | custom-call | flops 4000000000 | bytes 4000000 | tf_op jit(solution)/shard_map/coefs_kernel/pallas_call | solution.py:461
  42.4 0.0 collective-permute-done.1.refs_1_.refs_9_
  42.4 2.8 %all-to-all-done = f32[64,2,128]{2,1,0:T(2,128)S(1)} async-done(((f32[64,2,128]{2,1,0:T(2,128)}), f32[64,2,128]{2,1,0:T(2,128)S(1)}, u32[]{:S(2)}, u32[]{:S(2)}) %all-to-all-start) | async-done | bytes 65568 | tf_op jit(solution)/shard_map/all_to_all | solution.py:490
  45.2 1.5 carry_on.1
  46.6 10.0 %all-to-all-start.1 = ((f32[64,2,128]{2,1,0:T(2,128)}), f32[64,2,128]{2,1,0:T(2,128)S(1)}, u32[]{:S(2)}, u32[]{:S(2)}) async-start(f32[64,2,128]{2,1,0:T(2,128)} %bitcast.11), calls=%async_computation.1 | async-start | bytes 131072 | tf_op jit(solution)/shard_map/all_to_all | solution.py:501
  56.6 0.0 copy-done.1
  56.6 0.0 copy-done.2
  56.6 0.0 copy-done.5
  56.6 0.0 copy-start
  56.6 0.0 copy-start.4
  56.7 8.3 %states_kernel.1 = (f32[128,2048]{1,0:T(8,128)}, f32[128,2048]{1,0:T(8,128)}, f32[8,128,2048]{2,1,0:T(8,128)}) custom-call(f32[8,16]{1,0:T(8,128)S(1)} %get-tuple-element.58.refs_0_.rate, bf16[3,128,2048]{2,1,0:T(8,128)(2,1)} %bitcast.47, bf16[3,8,2048]{2,1,0:T(8,128)(2,1)S(1)} %collective-permute-done.refs_2_.refs_4_.refs_11_, f32[3,7,2048]{2,1,0:T(8,128)S(1)} %bitcast.31, ...), custom_call_target="tpu_custom_call" | custom-call | flops 4000000000 | bytes 14000000 | tf_op jit(solution)/shard_map/states_kernel/pallas_call | solution.py:461
  64.9 4.6 %all-to-all-done.1 = f32[64,2,128]{2,1,0:T(2,128)S(1)} async-done(((f32[64,2,128]{2,1,0:T(2,128)}), f32[64,2,128]{2,1,0:T(2,128)S(1)}, u32[]{:S(2)}, u32[]{:S(2)}) %all-to-all-start.1) | async-done | bytes 65568 | tf_op jit(solution)/shard_map/all_to_all | solution.py:501
  69.5 0.0 copy-done
  69.5 0.0 copy-done.4
  69.5 3.0 %branch_kernel.1 = (f32[128,2048]{1,0:T(8,128)}, f32[8,128]{1,0:T(8,128)S(1)}) custom-call(f32[128,2048]{1,0:T(8,128)} %get-tuple-element.34.refs_0_.refs_1_, f32[128,2048]{1,0:T(8,128)} %get-tuple-element.35.refs_1_, bf16[128,2048]{1,0:T(8,128)(2,1)S(1)} %bitcast.27, f32[1,2048]{1,0:T(1,128)S(1)} %bitcast.39, f32[16,8,128]{2,1,0:T(8,128)S(1)} %bitcast.35, ...), custom_call_target="tpu_custom_call" | custom-call | tf_op jit(solution)/shard_map/branch_kernel/pallas_call | solution.py:461
  72.5 2.5 %psum.7.refs_0_ = f32[8,128]{1,0:T(8,128)S(1)} all-reduce(f32[8,128]{1,0:T(8,128)S(1)} %get-tuple-element.38), channel_id=1, replica_groups=mesh['y'=4,'x'=4,'z'=16,'c'=2] {'c'}, use_global_device_ids=true, to_apply=%region_0.0 | all-reduce | flops 1024 | bytes 8192 | tf_op jit(solution)/shard_map/psum | solution.py:530
  75.0 3.1 %gate_kernel.1 = (f32[128,2048]{1,0:T(8,128)}, f32[16,8,128]{2,1,0:T(8,128)}, f32[2,8,2048]{2,1,0:T(8,128)S(1)}) custom-call(f32[8,128]{1,0:T(8,128)S(1)} %psum.7.refs_0_, f32[128,2048]{1,0:T(8,128)} %get-tuple-element.34.refs_0_.refs_1_, f32[128,2048]{1,0:T(8,128)} %get-tuple-element.39.refs_2_, bf16[128,2048]{1,0:T(8,128)(2,1)S(1)} %bitcast.28, ...), custom_call_target="tpu_custom_call" | custom-call | tf_op jit(solution)/shard_map/gate_kernel/pallas_call | solution.py:461
  78.1 10.6 %all-to-all-start.2 = ((f32[64,2,128]{2,1,0:T(2,128)}), f32[64,2,128]{2,1,0:T(2,128)S(1)}, u32[]{:S(2)}, u32[]{:S(2)}) async-start(f32[64,2,128]{2,1,0:T(2,128)} %bitcast.15), calls=%async_computation.2 | async-start | bytes 131072 | tf_op jit(solution)/shard_map/all_to_all | solution.py:490
  88.8 10.5 %adjoint_kernel.1 = (f32[128,2048]{1,0:T(8,128)}, f32[16,8,128]{2,1,0:T(8,128)S(1)}, f32[16,8,128]{2,1,0:T(8,128)S(1)}, f32[16,8,128]{2,1,0:T(8,128)S(1)}, f32[3,8,2048]{2,1,0:T(8,128)S(1)}) custom-call(f32[8,16]{1,0:T(8,128)S(1)} %get-tuple-element.58.refs_0_.rate, f32[16,8,128]{2,1,0:T(8,128)S(1)} %broadcast_in_dim.21.refs_0_.refs_5_.refs_1_, ...), custom_call_target="tpu_custom_call" | custom-call | flops 6000000000 | bytes 16000000 | tf_op jit(solution)/shard_map/adjoint_kernel/pallas_call | solution.py:461
  99.3 2.7 %all-to-all-done.2 = f32[64,2,128]{2,1,0:T(2,128)S(1)} async-done(((f32[64,2,128]{2,1,0:T(2,128)}), f32[64,2,128]{2,1,0:T(2,128)S(1)}, u32[]{:S(2)}, u32[]{:S(2)}) %all-to-all-start.2) | async-done | bytes 65568 | tf_op jit(solution)/shard_map/all_to_all | solution.py:490
  102.0 1.5 carry_back.1
  103.5 12.4 %all-to-all-start.3 = ((f32[64,2,128]{2,1,0:T(2,128)}), f32[64,2,128]{2,1,0:T(2,128)S(1)}, u32[]{:S(2)}, u32[]{:S(2)}) async-start(f32[64,2,128]{2,1,0:T(2,128)} %bitcast.17), calls=%async_computation.3 | async-start | bytes 131072 | tf_op jit(solution)/shard_map/all_to_all | solution.py:501
  115.9 4.9 %collective-permute-start.2 = (f32[3,8,2048]{2,1,0:T(8,128)S(1)}, f32[3,8,2048]{2,1,0:T(8,128)S(1)}, u32[]{:S(2)}, u32[]{:S(2)}) collective-permute-start(f32[3,8,2048]{2,1,0:T(8,128)S(1)} %get-tuple-element.49), channel_id=1, source_target_pairs={{2,0},{4,2},{6,4},{8,6},{10,8},{12,10},{14,12},{16,14},{18,16},{20... | collective-permute-start | bytes 589832 | tf_op jit(solution)/shard_map/ppermute | solution.py:443
  120.8 6.9 %outs_kernel.1 = (bf16[128,2048]{1,0:T(8,128)(2,1)}, f32[128,2048]{1,0:T(8,128)}, f32[16,32,128]{2,1,0:T(8,128)S(1)}) custom-call(f32[8,128]{1,0:T(8,128)S(1)} %psum.7.refs_0_, f32[128,2048]{1,0:T(8,128)} %get-tuple-element.34.refs_0_.refs_1_, f32[128,2048]{1,0:T(8,128)} %get-tuple-element.39.refs_2_, bf16[128,2048]{1,0:T(8,128)(2,1)S(1)} %bitcast.29, ...), custom_call_target="tpu_custom_call" | custom-call | flops 1000000000 | bytes 10000000 | tf_op jit(solution)/shard_map/outs_kernel/pallas_call | solution.py:461
  127.6 0.0 copy-start.3
  127.7 0.7 copy-done.3
  128.4 0.0 collective-permute-done.2.refs_8_.refs_7_
  128.4 0.5 all-to-all-done.3
  128.8 2.1 %sums_kernel.1 = f32[16,32,128]{2,1,0:T(8,128)S(1)} custom-call(f32[16,8,128]{2,1,0:T(8,128)S(1)} %bitcast.33, f32[16,8,128]{2,1,0:T(8,128)S(1)} %broadcast_in_dim.21.refs_0_.refs_5_.refs_1_, f32[8,2048]{1,0:T(8,128)S(1)} %copy-done.2, f32[16,8,128]{2,1,0:T(8,128)S(1)} %get-tuple-element.47.refs_0_.refs_3_, f32[16,8,128]{2,1,0:T(8,128)S(1)} %get-tuple-element.50.refs_4_, ...), custom_call_target="tpu_custom_call" | custom-call | tf_op jit(solution)/shard_map/sums_kernel/pallas_call | solution.py:461
  130.9 13.7 %all_to_all.35.parts = f32[16,32,128]{2,1,0:T(8,128)S(1)} all-to-all(f32[16,32,128]{2,1,0:T(8,128)S(1)} %sums_kernel.1), channel_id=1, replica_groups=mesh['y'=4,'x'=4,'z'=16,'c'=2] {'y','x'}, dimensions={0} | all-to-all | bytes 524288 | tf_op jit(solution)/shard_map/all_to_all | solution.py:579
  144.7 0.7 add_over_yx.1
  145.4 8.5 %all-to-all-start.5 = ((f32[16,32,128]{2,1,0:T(8,128)}), f32[16,32,128]{2,1,0:T(8,128)S(1)}, u32[]{:S(2)}, u32[]{:S(2)}) async-start(f32[16,32,128]{2,1,0:T(8,128)} %add_over_yx.1), calls=%async_computation.5 | async-start | bytes 524288 | tf_op jit(solution)/shard_map/all_to_all | solution.py:580
  153.9 6.2 %finish_kernel.1.refs_0_ = bf16[3,128,2048]{2,1,0:T(8,128)(2,1)} custom-call(f32[8,16]{1,0:T(8,128)S(1)} %get-tuple-element.58.refs_0_.rate, f32[16,8,128]{2,1,0:T(8,128)S(1)} %bitcast.34, f32[16,1,128]{2,1,0:T(1,128)S(1)} %copy.17.refs_5_.refs_2_, f32[128,2048]{1,0:T(8,128)} %get-tuple-element.44.refs_8_.refs_3_, f32[128,2048]{1,0:T(8,128)} %get-tuple-element.48.refs_4_, ...), custom_call_target="tpu_custom_call" | custom-call | flops 1000000000 | bytes 10000000 | tf_op jit(solution)/shard_map/finish_kernel/pallas_call | solution.py:461
  160.1 9.9 %all-to-all-done.5.parts = f32[16,32,128]{2,1,0:T(8,128)S(1)} async-done(((f32[16,32,128]{2,1,0:T(8,128)}), f32[16,32,128]{2,1,0:T(8,128)S(1)}, u32[]{:S(2)}, u32[]{:S(2)}) %all-to-all-start.5) | async-done | bytes 262176 | tf_op jit(solution)/shard_map/all_to_all | solution.py:580
  170.1 11.7 %all_to_all.36.pack = f32[16,32,128]{2,1,0:T(8,128)S(1)} all-to-all(f32[16,32,128]{2,1,0:T(8,128)S(1)} %add_over_z.1), channel_id=1, replica_groups=mesh['y'=4,'x'=4,'z'=16,'c'=2] {'y','x'}, dimensions={0} | all-to-all | bytes 524288 | tf_op jit(solution)/shard_map/all_to_all | solution.py:581
  181.8 0.7 unpack.1
  (3 shorter events, 0.1 us)
Async XLA Ops:
  1.5 14.4 %collective-permute-start = (bf16[3,8,2048]{2,1,0:T(8,128)(2,1)S(1)}, bf16[3,8,2048]{2,1,0:T(8,128)(2,1)S(1)}, u32[]{:S(2)}, u32[]{:S(2)}) collective-permute-start(bf16[3,8,2048]{2,1,0:T(8,128)(2,1)S(1)} %slice.4), channel_id=1, source_target_pairs={{0,2},{2,4},{4,6},{6,8},{8,10},{10,12},{12,14},{14,16},{16,18},{18... | collective-permute-start | bytes 294920 | tf_op jit(solution)/shard_map/ppermute | solution.py:443
  20.1 25.0 %all-to-all-start = ((f32[64,2,128]{2,1,0:T(2,128)}), f32[64,2,128]{2,1,0:T(2,128)S(1)}, u32[]{:S(2)}, u32[]{:S(2)}) async-start(f32[64,2,128]{2,1,0:T(2,128)} %bitcast.9), calls=%async_computation | async-start | bytes 131072 | tf_op jit(solution)/shard_map/all_to_all | solution.py:490
  32.2 10.2 %collective-permute-start.1 = (f32[2,8,2048]{2,1,0:T(8,128)}, f32[2,8,2048]{2,1,0:T(8,128)S(1)}, u32[]{:S(2)}, u32[]{:S(2)}) collective-permute-start(f32[2,8,2048]{2,1,0:T(8,128)} %get-tuple-element.37), channel_id=1, source_target_pairs={{2,0},{4,2},{6,4},{8,6},{10,8},{12,10},{14,12},{16,14},{18,16},{20... | collective-permute-start | bytes 393224 | tf_op jit(solution)/shard_map/ppermute | solution.py:443
  37.1 19.5 %copy-start.1 = (f32[7,3,2048]{2,0,1:T(8,128)S(1)}, f32[7,3,2048]{2,0,1:T(8,128)}, u32[]{:S(2)}) copy-start(f32[7,3,2048]{2,0,1:T(8,128)} %param.8) | copy-start | bytes 516100
  37.1 19.5 %copy-start.2 = (f32[8,2048]{1,0:T(8,128)S(1)}, f32[8,2048]{1,0:T(8,128)}, u32[]{:S(2)}) copy-start(f32[8,2048]{1,0:T(8,128)} %refs_2_.1) | copy-start | bytes 196612
  37.1 19.5 %copy-start.5 = (f32[2048]{0:T(1024)S(1)}, f32[2048]{0:T(1024)}, u32[]{:S(2)}) copy-start(f32[2048]{0:T(1024)} %param.11) | copy-start | bytes 24580
  46.6 22.9 %all-to-all-start.1 = ((f32[64,2,128]{2,1,0:T(2,128)}), f32[64,2,128]{2,1,0:T(2,128)S(1)}, u32[]{:S(2)}, u32[]{:S(2)}) async-start(f32[64,2,128]{2,1,0:T(2,128)} %bitcast.11), calls=%async_computation.1 | async-start | bytes 131072 | tf_op jit(solution)/shard_map/all_to_all | solution.py:501
  56.6 12.9 %copy-start = (bf16[1,128,2048]{2,1,0:T(8,128)(2,1)S(1)}, bf16[1,128,2048]{2,1,0:T(8,128)(2,1)}, u32[]{:S(2)}) copy-start(bf16[1,128,2048]{2,1,0:T(8,128)(2,1)} %param.13) | copy-start | bytes 1572868
  56.6 12.9 %copy-start.4 = (f32[2048]{0:T(1024)S(1)}, f32[2048]{0:T(1024)}, u32[]{:S(2)}) copy-start(f32[2048]{0:T(1024)} %param.12) | copy-start | bytes 24580
  78.1 23.9 %all-to-all-start.2 = ((f32[64,2,128]{2,1,0:T(2,128)}), f32[64,2,128]{2,1,0:T(2,128)S(1)}, u32[]{:S(2)}, u32[]{:S(2)}) async-start(f32[64,2,128]{2,1,0:T(2,128)} %bitcast.15), calls=%async_computation.2 | async-start | bytes 131072 | tf_op jit(solution)/shard_map/all_to_all | solution.py:490
  103.5 25.4 %all-to-all-start.3 = ((f32[64,2,128]{2,1,0:T(2,128)}), f32[64,2,128]{2,1,0:T(2,128)S(1)}, u32[]{:S(2)}, u32[]{:S(2)}) async-start(f32[64,2,128]{2,1,0:T(2,128)} %bitcast.17), calls=%async_computation.3 | async-start | bytes 131072 | tf_op jit(solution)/shard_map/all_to_all | solution.py:501
  115.9 12.5 %collective-permute-start.2 = (f32[3,8,2048]{2,1,0:T(8,128)S(1)}, f32[3,8,2048]{2,1,0:T(8,128)S(1)}, u32[]{:S(2)}, u32[]{:S(2)}) collective-permute-start(f32[3,8,2048]{2,1,0:T(8,128)S(1)} %get-tuple-element.49), channel_id=1, source_target_pairs={{2,0},{4,2},{6,4},{8,6},{10,8},{12,10},{14,12},{16,14},{18,16},{20... | collective-permute-start | bytes 589832 | tf_op jit(solution)/shard_map/ppermute | solution.py:443
  127.6 0.7 copy-start.3
  145.4 24.6 %all-to-all-start.5 = ((f32[16,32,128]{2,1,0:T(8,128)}), f32[16,32,128]{2,1,0:T(8,128)S(1)}, u32[]{:S(2)}, u32[]{:S(2)}) async-start(f32[16,32,128]{2,1,0:T(8,128)} %add_over_yx.1), calls=%async_computation.5 | async-start | bytes 524288 | tf_op jit(solution)/shard_map/all_to_all | solution.py:580

commit v6 on v5

--- a/solution.py
+++ b/solution.py
@@ -20,10 +20,13 @@
 GROUPS_HERE = 16
 PARTS = 4
 HELD = ("smem", "vmem", "order")
+STREAMS = {"first": slice(0, 1), "last": slice(1, 3)}
+F0, F12 = "first", "last"
 C, G, W, S, V, O = "cols", "groups", "whole", "smem", "vmem", "order"
 ROWS = 32
 VMEM_MIB = 53
 ENDS_MIB = 53.6
+OUTS_MIB = 53
 CTX = ("x", "z")
 YX = ("y", "x")
 
@@ -33,6 +36,9 @@
         span = ref.shape[-1] // PARTS
         at = pl.ds(pl.multiple_of(part * span, span), span)
         return ref.at[(slice(None),) * (len(ref.shape) - 1) + (at,)]
+    if kind in STREAMS:
+        span = ref.shape[-1] // PARTS
+        return ref.at[STREAMS[kind], :, pl.ds(pl.multiple_of(part * span, span), span)]
     if kind == "groups":
         span = ref.shape[0] // PARTS
         return ref.at[pl.ds(part * span, span)]
@@ -115,23 +121,30 @@
     return lax.broadcasted_iota(jnp.int32, shape, dim)
 
 
-def ones_tri(lower):
+def ones_tri():
     row = iota((L, 2 * L), 0)
     col = iota((L, 2 * L), 1) % L
-    keep = col <= row if lower else col >= row
-    return jnp.where(keep, 1.0, 0.0).astype(BF16)
-
-
-def powers(rate, sign):
+    return jnp.where(col <= row, 1.0, 0.0).astype(BF16)
+
+
+def ones_and_lags():
+    row = iota((L, 2 * L), 0)
+    col = iota((L, 2 * L), 1) % L
+    ones = jnp.where(col >= row, 1.0, 0.0)
+    return jnp.concatenate([ones, jnp.maximum(col - row, 0).astype(F32)], axis=0).astype(BF16)
+
+
+def powers(rates, sign):
     column = iota((PAD, GS), 0).astype(F32)
-    table = jnp.exp((sign * rate) * column)
-    rows = PAD
-    while rows < L:
-        factor = jnp.exp(jnp.full((PAD, GS), sign * rows, F32) * rate)
-        more = jnp.concatenate([factor] * (rows // PAD), axis=0)
-        table = jnp.concatenate([table, table * more], axis=0)
-        rows *= 2
-    return table
+    spans = [PAD * 2**n for n in range(4)]
+    factors = [jnp.exp((sign * span) * rates) for span in spans]
+    tables = []
+    for p in range(POLES):
+        table = jnp.exp((sign * column) * rates[p : p + 1, :])
+        for factor in factors:
+            table = jnp.concatenate([table, table * factor[p : p + 1, :]], axis=0)
+        tables.append(table)
+    return tables
 
 
 def split(x):
@@ -148,15 +161,13 @@
     return jnp.sum(x, axis=0, keepdims=True)
 
 
-def fill_ext(ext, feat, halo, cs):
-    for j in range(3):
-        ext[j, 0:PAD, :] = halo[j, :, cs].astype(F32)
-        ext[j, PAD : PAD + L, :] = feat[j, :, cs].astype(F32)
-
-
-def filtered(j, taps, feat, halo, cs, ext):
+def extend(j, feat, halo, cs, ext):
     ext[j, 0:PAD, :] = halo[j, :, cs].astype(F32)
     ext[j, PAD : PAD + L, :] = feat[j, :, cs].astype(F32)
+
+
+def filtered(j, taps, feat, halo, cs, ext):
+    extend(j, feat, halo, cs, ext)
     acc = taps[j, 0:1, cs] * ext[j, PAD : PAD + L, :]
     for k in range(1, TAPS):
         acc = acc + taps[j, k : k + 1, cs] * ext[j, pl.ds(PAD - k, L), :]
@@ -191,48 +202,40 @@
     return jnp.dot(left, right, preferred_element_type=F32)
 
 
-def ends_kernel(by_pole, feat, halo, taps, k_o, v_o, e_o, edge_o, ext):
+def ends_kernel(by_pole, feat, halo, taps, k_o, v_o, e_o, ext):
     def body(gi, cs):
         key = filtered(1, taps, feat, halo, cs, ext)
         value = filtered(2, taps, feat, halo, cs, ext)
         k_o[:, cs] = key
         v_o[:, cs] = value
-        edge_o[0, :, cs] = key[0:PAD, :]
-        edge_o[1, :, cs] = value[0:PAD, :]
         e_o[gi] = weighted_rows(jnp.exp(-by_pole[gi] * (L - 1.0 - lane_place())), key * value)
 
     return body, None
 
 
-def states_kernel(rate, feat, halo, taps, k, v, weight, skip, q_o, bl_o, s_o, ext):
-    tri = ones_tri(True)
+def query_kernel(by_pole, k, v, feat, halo, taps, q_o, deep_o, ext):
     def body(gi, cs):
         q_o[:, cs] = filtered(0, taps, feat, halo, cs, ext)
+        lane = lane_place()
+        table = (L - 1.0 - lane) * jnp.exp(-by_pole[gi] * (L - 2.0 - lane))
+        deep_o[gi] = weighted_rows(table, k[:, cs] * v[:, cs])
+
+    return body, None
+
+
+def states_kernel(by_pole, k, v, weight, skip, bl_o):
+    tri = ones_tri()
+
+    def body(gi, cs):
         prod = k[:, cs] * v[:, cs]
         modal = skip[0:1, cs] * prod
+        grow, decay = powers(by_pole[gi], 1.0), powers(by_pole[gi], -1.0)
         for p in range(0, POLES, 2):
-            rates = [rate[p + i, gi] for i in range(2)]
-            both = tri_dot(tri, [powers(r, 1.0) * prod for r in rates])
-            for i, r in enumerate(rates):
-                state = powers(r, -1.0) * both[:, i * GS : (i + 1) * GS]
-                s_o[p + i, :, cs] = state
+            both = tri_dot(tri, [grow[p] * prod, grow[p + 1] * prod])
+            for i in range(2):
+                state = decay[p + i] * both[:, i * GS : (i + 1) * GS]
                 modal = modal + weight[p + i : p + i + 1, cs] * state
         bl_o[:, cs] = modal
-
-    return body, None
-
-
-def coefs_kernel(by_pole, k, v, feat, halo, c_o, ext):
-    def body(gi, cs):
-        fill_ext(ext, feat, halo, cs)
-        table = two_parts(jnp.exp(-by_pole[gi] * (L - 1.0 - lane_place())))
-        for j, other in ((1, v[:, cs]), (2, k[:, cs])):
-            xs = [split(other * ext[j, pl.ds(PAD - t, L), :]) for t in range(TAPS)]
-            both = jnp.dot(table, jnp.concatenate(xs, axis=1), preferred_element_type=F32)
-            both = both[0:POLES, :] + both[POLES : 2 * POLES, :]
-            for t in range(TAPS):
-                at = POLES * (TAPS * (j - 1) + t)
-                c_o[gi, at : at + POLES, :] = both[:, t * GS : (t + 1) * GS]
 
     return body, None
 
@@ -274,9 +277,7 @@
 
 
 def gate_kernel(stats, q, br, cot, gain, by_pole, g_o, back_o, edge_o):
-    inv_row = lax.rsqrt(stats[0:1, :] / D + EPSILON)
-    inv = down(inv_row)
-    pull = down(stats[1:2, :] * inv_row * inv_row * inv_row / D)
+    inv, pull = row_scales(stats)
     def body(gi, cs):
         query, branch = q[:, cs], br[:, cs]
         dgated = (gain[0:1, cs] * cot[:, cs].astype(F32)) * inv - (query * branch) * pull
@@ -291,94 +292,104 @@
 
 
 def adjoint_kernel(
-    rate, by_pole, g, k, v, states, weight, skip, state_in, back, edge,
-    dpl_o, res_o, loc_o, mix_o, edge_o,
+    by_pole, g, k, v, weight, skip, state_in, back, deep, edge,
+    dpl_o, res_o, loc_o, mix_o, skip_o, edge_o,
 ):
-    tri = ones_tri(False)
-    place = iota((L, GS), 0).astype(F32)
-    centre = place - (L - 1) / 2
+    tri = ones_and_lags()
     lane = lane_place()
+
     def body(gi, cs):
         dbranch = g[:, cs]
-        prod = k[:, cs] * v[:, cs]
+        key, value = k[:, cs], v[:, cs]
+        prod = key * value
         total = skip[0:1, cs] * dbranch
-        far_grad = centre * dbranch
-        far_prod = centre * prod
+        skip_o[0:1, cs] = rowsum(dbranch * prod)
         own_in = state_in[gi]
         own_rate = by_pole[gi]
         once = jnp.exp(-own_rate)
         residue = own_in * back[gi]
         heavy = weighted_rows((lane + 1.0) * jnp.exp(-own_rate * lane), dbranch)
-        deep = weighted_rows((L - 1.0 - lane) * jnp.exp(-own_rate * (L - 2.0 - lane)), prod)
-        mix_o[gi] = once * (deep + L * jnp.exp(-(L - 1) * own_rate) * own_in)
+        mix_o[gi] = once * (deep[gi] + L * jnp.exp(-(L - 1) * own_rate) * own_in)
         loc = once * own_in * heavy
+        grow, decay = powers(own_rate, 1.0), powers(own_rate, -1.0)
         for p in range(0, POLES, 2):
-            rates = [rate[p + i, gi] for i in range(2)]
-            both = tri_dot(tri, [powers(r, -1.0) * dbranch for r in rates])
-            for i, r in enumerate(rates):
+            both = tri_dot(tri, [decay[p] * dbranch, decay[p + 1] * dbranch])
+            for i in range(2):
                 at = slice(p + i, p + i + 1)
-                adjoint = powers(r, 1.0) * both[:, i * GS : (i + 1) * GS]
+                lanes = slice(i * GS, (i + 1) * GS)
+                adjoint = grow[p + i] * both[0:L, lanes]
                 total = total + weight[at, cs] * adjoint
                 res_o[gi, at, :] = residue[at, :] + rowsum(prod * adjoint)
-                loc_o[gi, at, :] = loc[at, :] + rowsum(far_grad * states[p + i, :, cs] - far_prod * adjoint)
+                loc_o[gi, at, :] = loc[at, :] + rowsum((prod * grow[p + i]) * both[L : 2 * L, lanes])
         dpl_o[:, cs] = total
         edge_o[0, :, cs] = edge[0, :, cs]
         edge_o[1, :, cs] = total[0:PAD, :]
         edge_o[2, :, cs] = edge[1, :, cs]
-
-    return body, None
-
-
-def outs_kernel(
-    stats, q, br, cot, gain, k, v, g, dpl, res, feat, halo, out_o, dq_o, pack_o, ext,
-):
+        edge_o[3, :, cs] = key[0:PAD, :]
+        edge_o[4, :, cs] = value[0:PAD, :]
+
+    return body, None
+
+
+def tap_sums(pack_o, gi, j, own, ext):
+    for t in range(TAPS):
+        at = TAPS * j + t
+        pack_o[gi, at : at + 1, :] = rowsum(own * ext[j, pl.ds(PAD - t, L), :])
+
+
+def row_scales(stats):
     inv_row = lax.rsqrt(stats[0:1, :] / D + EPSILON)
-    inv = down(inv_row)
-    pull = down(stats[1:2, :] * inv_row * inv_row * inv_row / D)
-    def body(gi, cs):
-        fill_ext(ext, feat, halo, cs)
-        query, branch, key, value = q[:, cs], br[:, cs], k[:, cs], v[:, cs]
+    return down(inv_row), down(stats[1:2, :] * inv_row * inv_row * inv_row / D)
+
+
+def outs_kernel(stats, br, cot, gain, res, skips, feat, halo, taps, pack_o, ext):
+    inv, pull = row_scales(stats)
+
+    def body(gi, cs):
+        branch = br[:, cs]
         grad = cot[:, cs].astype(F32)
-        gated = query * branch
-        normed = gated * inv
-        out_o[:, cs] = (gain[0:1, cs] * normed).astype(BF16)
+        gated = filtered(0, taps, feat, halo, cs, ext) * branch
         dquery = ((gain[0:1, cs] * grad) * inv - gated * pull) * branch
-        dq_o[:, cs] = dquery
-        local_prod = dpl[:, cs]
-        for j, own in enumerate((dquery, local_prod * value, local_prod * key)):
-            for t in range(TAPS):
-                at = TAPS * j + t
-                pack_o[gi, at : at + 1, :] = rowsum(own * ext[j, pl.ds(PAD - t, L), :])
+        tap_sums(pack_o, gi, 0, dquery, ext)
+        pack_o[gi, 7:21, :] = jnp.zeros((2 * TAPS, GS), F32)
         pack_o[gi, 21:29, :] = res[gi]
-        pack_o[gi, 29:30, :] = rowsum(g[:, cs] * (key * value))
-        pack_o[gi, 30:31, :] = rowsum(grad * normed)
+        pack_o[gi, 29:30, :] = skips[0:1, cs]
+        pack_o[gi, 30:31, :] = rowsum(grad * (gated * inv))
         pack_o[gi, 31:32, :] = jnp.zeros((1, GS), F32)
 
     return body, None
 
 
-def sums_kernel(later, by_pole, weight, loc, mix, coefs, pack, pack_o):
+def sums_kernel(later, by_pole, by_lane, weight, loc, mix, dpl, k, v, feat, halo, pack, pack_o, ext):
     lane, sub = iota((POLES, GS), 1), iota((POLES, GS), 0)
+
     def body(gi, cs):
         coming = later[gi]
         scaled = weight[:, cs] * coming
+        dprod = dpl[:, cs] + spread_poles(by_lane[gi], -1, scaled)
         pack_o[gi] = pack[gi]
-        for i in range(2 * TAPS):
-            at = TAPS + i
-            more = rowsum(scaled * coefs[gi, POLES * i : POLES * (i + 1), :])
-            pack_o[gi, at : at + 1, :] = pack[gi, at : at + 1, :] + more
-        inner = jnp.sum(weight[:, cs] * (loc[gi] + coming * mix[gi]), axis=1, keepdims=True)
+        for j, other in ((1, v), (2, k)):
+            extend(j, feat, halo, cs, ext)
+            tap_sums(pack_o, gi, j, dprod * other[:, cs], ext)
+        inner = jnp.sum(weight[:, cs] * loc[gi] + scaled * mix[gi], axis=1, keepdims=True)
         pack_o[gi, 31:32, :] = rowsum(jnp.where(lane == sub, -by_pole[gi] * inner, 0.0))
 
     return body, None
 
 
-def finish_kernel(rate, later, by_lane, dpl, dq, k, v, weight, rim, near, taps, grad_o, dext):
+def finish_kernel(
+    rate, later, by_lane, dpl, q, k, v, br, cot, weight, rim, taps, stats, gain, grad_o, out_o, dext
+):
     ahead = (iota((PAD, GS), 0) + 1).astype(F32)
+    inv, pull = row_scales(stats)
+
     def body(gi, cs):
         coming = later[gi]
+        branch = br[:, cs]
+        gated = q[:, cs] * branch
+        out_o[:, cs] = (gain[0:1, cs] * (gated * inv)).astype(BF16)
         dprod = dpl[:, cs] + spread_poles(by_lane[gi], -1, weight[:, cs] * coming)
-        dext[0, 0:L, :] = dq[:, cs]
+        dext[0, 0:L, :] = ((gain[0:1, cs] * cot[:, cs].astype(F32)) * inv - gated * pull) * branch
         dext[1, 0:L, :] = dprod * v[:, cs]
         dext[2, 0:L, :] = dprod * k[:, cs]
         beyond = weight[:, cs] * (coming - rim[2, :, cs])
@@ -386,8 +397,8 @@
         for p in range(POLES):
             next_prod = next_prod + jnp.exp(ahead * rate[p, gi]) * beyond[p : p + 1, :]
         dext[0, L : L + PAD, :] = rim[0, :, cs]
-        dext[1, L : L + PAD, :] = next_prod * near[1, :, cs]
-        dext[2, L : L + PAD, :] = next_prod * near[0, :, cs]
+        dext[1, L : L + PAD, :] = next_prod * rim[4, :, cs]
+        dext[2, L : L + PAD, :] = next_prod * rim[3, :, cs]
         for j in range(3):
             acc = taps[j, 0:1, cs] * dext[j, 0:L, :]
             for t in range(1, TAPS):
@@ -427,15 +438,15 @@
     return jax.ShapeDtypeStruct(dims, dtype)
 
 
-ends_kernel.kinds = ((W, C, V, C,), (C, C, G, C,))
-states_kernel.kinds = ((S, C, V, C, C, C, C, C,), (C, C, C,))
-coefs_kernel.kinds = ((W, C, C, C, V,), (G,))
+ends_kernel.kinds = ((W, F12, V, C,), (C, C, G,))
+query_kernel.kinds = ((W, C, C, F0, V, C,), (C, G,))
+states_kernel.kinds = ((W, C, C, C, C,), (C,))
 branch_kernel.kinds = ((C, C, C, C, G, W, C,), (C, W,))
 gate_kernel.kinds = ((W, C, C, C, C, W,), (C, G, C,))
-adjoint_kernel.kinds = ((S, W, C, C, C, C, C, C, G, G, C,), (C, G, G, G, C,))
-outs_kernel.kinds = ((W, C, C, C, C, C, C, C, C, G, C, V,), (C, C, G,))
-sums_kernel.kinds = ((G, W, C, G, G, G, G, O,), (G,))
-finish_kernel.kinds = ((S, G, W, C, C, C, C, C, C, C, C,), (C,))
+adjoint_kernel.kinds = ((W, C, C, C, C, C, G, G, G, C,), (C, G, G, G, C, C,))
+outs_kernel.kinds = ((W, C, C, C, G, C, F0, V, C,), (G,))
+sums_kernel.kinds = ((G, W, W, C, G, G, C, C, C, F12, V, G,), (G,))
+finish_kernel.kinds = ((S, G, W, C, C, C, C, C, C, C, C, C, W, C,), (C, C,))
 
 
 def shifted(value, step):
@@ -466,7 +477,7 @@
             scratch_shapes=[pltpu.SemaphoreType.DMA((len(fetched) + len(outs), PARTS))]
             + [pltpu.VMEM(a.shape, a.dtype) for a in [*fetched, *outs]]
             + [pltpu.VMEM(d, F32) for d in extra],
-            compiler_params=params(ENDS_MIB if setup is ends_kernel else VMEM_MIB),
+            compiler_params=params({ends_kernel: ENDS_MIB, outs_kernel: OUTS_MIB}.get(setup, VMEM_MIB)),
             cost_estimate=pl.CostEstimate(flops=flops, bytes_accessed=moved, transcendentals=special),
             name=setup.__name__,
         )(*args)
@@ -481,10 +492,9 @@
     by_pole = jnp.broadcast_to(rate.T[:, :, None], (groups, POLES, GS))
     by_lane = jnp.tile(rate.T, (1, GS // POLES))[:, None, :]
 
-    key, value, ends, edge = call(
-        ends_kernel, [wide, wide, per_pole, edges], (by_pole, feat, halo, taps), [ext3]
-    )
-    near = shifted(edge, -1)
+    key, value, ends = call(
+        ends_kernel, [wide, wide, per_pole], (by_pole, feat, halo, taps), [ext3]
+    )
 
     def owned(rows):
         return lax.all_to_all(rows.reshape(count, 2, GS), CTX, 0, 0).reshape(L, GS)
@@ -502,25 +512,24 @@
         return given.reshape(groups, POLES, GS)
 
     rows_in = owned(ends)
-    coefs = call(
-        coefs_kernel,
-        [shape(groups, 2 * TAPS * POLES, GS)],
-        (by_pole, key, value, feat, halo),
+    query, deep = call(
+        query_kernel,
+        [wide, per_pole],
+        (by_pole, key, value, feat, halo, taps),
         [ext3],
+        flops=1_000_000_000,
+        moved=6_000_000,
+    )
+    state_in = carried(rows_in, (deep,), False)
+
+    base = call(
+        states_kernel,
+        [wide],
+        (by_pole, key, value, residues, skip),
         flops=4_000_000_000,
         moved=4_000_000,
+        special=4_000_000,
     )[0]
-    state_in = carried(rows_in, (coefs, near), False)
-
-    query, base, states = call(
-        states_kernel,
-        [wide, wide, shape(POLES, L, channels)],
-        (rate, feat, halo, taps, key, value, residues, skip),
-        [ext3],
-        flops=4_000_000_000,
-        moved=14_000_000,
-        special=4_000_000,
-    )
     branch, stats = call(
         branch_kernel,
         [wide, shape(8, L)],
@@ -533,10 +542,10 @@
         gate_kernel, [wide, per_pole, edges], (stats, query, branch, cot, gain, by_pole)
     )
     rows_back = owned(back_in)
-    dlocal, res_part, loc_part, mix_part, edge = call(
+    dlocal, res_part, loc_part, mix_part, skip_part, edge = call(
         adjoint_kernel,
-        [wide, per_pole, per_pole, per_pole, shape(3, PAD, channels)],
-        (rate, by_pole, dbranch, key, value, states, residues, skip, state_in, back_in, edge),
+        [wide, per_pole, per_pole, per_pole, shape(1, channels), shape(5, PAD, channels)],
+        (by_pole, dbranch, key, value, residues, skip, state_in, back_in, deep, edge),
         flops=6_000_000_000,
         moved=16_000_000,
         special=4_000_000,
@@ -544,27 +553,28 @@
     later = carried(rows_back, (loc_part,), True)
     rim = shifted(edge, -1)
 
-    block_out, dquery, pack = call(
+    pack = call(
         outs_kernel,
-        [shape(L, channels, dtype=BF16), wide, shape(groups, ROWS, GS)],
-        (stats, query, branch, cot, gain, key, value, dbranch, dlocal, res_part, feat, halo),
+        [shape(groups, ROWS, GS)],
+        (stats, branch, cot, gain, res_part, skip_part, feat, halo, taps),
         [ext3],
         flops=1_000_000_000,
-        moved=10_000_000,
-    )
+        moved=4_000_000,
+    )[0]
     pack = call(
         sums_kernel,
         [shape(groups, ROWS, GS)],
-        (later, by_pole, residues, loc_part, mix_part, coefs, pack, rim),
+        (later, by_pole, by_lane, residues, loc_part, mix_part, dlocal, key, value, feat, halo, pack),
+        [ext3],
     )[0]
-    feature_grad = call(
+    feature_grad, block_out = call(
         finish_kernel,
-        [shape(3, L, channels, dtype=BF16)],
-        (rate, later, by_lane, dlocal, dquery, key, value, residues, rim, near, taps),
+        [shape(3, L, channels, dtype=BF16), shape(L, channels, dtype=BF16)],
+        (rate, later, by_lane, dlocal, query, key, value, branch, cot, residues, rim, taps, stats, gain),
         [ext3],
         flops=1_000_000_000,
-        moved=10_000_000,
-    )[0]
+        moved=12_000_000,
+    )
 
     def summed_copies(parts, after, name):
         return pl.pallas_call(
@@ -576,7 +586,7 @@
             name=name,
         )(parts, *after)
 
-    owned_rows = summed_copies(lax.all_to_all(pack, YX, 0, 0), (), "add_over_yx")
+    owned_rows = summed_copies(lax.all_to_all(pack, YX, 0, 0), (rim,), "add_over_yx")
     everyone = lax.all_to_all(owned_rows, "z", 0, 0)
     totals = lax.all_to_all(summed_copies(everyone, (feature_grad,), "add_over_z"), YX, 0, 0)
     conv, rate_grad, res, skip_grad, gain_grad = pl.pallas_call(

time: 186 us -> 177 us (0.952)
  waiting for transfers between devices: 30.2 us -> 51.3 us
  blocking collectives: 27.9 us -> 14 us
  starting transfers between devices: 67.1 us -> 57.6 us
  Pallas kernels: 53.9 us -> 47.9 us
    all_to_all x1 -> x0, blocking collectives: 13.7 us -> none  [local(): lax.all_to_all(pack, YX, 0, 0)]
    all_to_all x2, waiting for transfers between devices: 5.5 us -> 14.3 us  [owned(): return lax.all_to_all(rows.reshape(count, 2, GS), CTX, 0, 0).reshape(L, GS)]
    all_to_all x0 -> x1, starting transfers between devices: none -> 7.67 us  [local(): lax.all_to_all(pack, YX, 0, 0)]
    all_to_all x2, waiting for transfers between devices: 5.04 us -> 11.6 us  [carried(): given = lax.all_to_all(summed.reshape(count, 2, GS), CTX, 0, 0)]
    all_to_all x0 -> x1, waiting for transfers between devices: none -> 6.31 us  [local(): lax.all_to_all(pack, YX, 0, 0)]
    pallas_call x9, Pallas kernels: 49.4 us -> 43.5 us  [call(): pl.pallas_call(functools.partial(streamed, setup, kinds_in, kinds_out), i...]
    all_to_all x2, starting transfers between devices: 22.4 us -> 16.6 us  [carried(): given = lax.all_to_all(summed.reshape(count, 2, GS), CTX, 0, 0)]
    ppermute x3 -> x2, starting transfers between devices: 13.6 us -> 8.68 us  [shifted(): return lax.ppermute(value, CTX, pairs)]
  transfers between devices with their start and end apart: 8 -> 8, of which waited for: 6 -> 7; matrix products, arithmetic and copies ran while one was open for 0% -> 0% of each run, Pallas kernels for 20% -> 19%
where the time goes in v6:
time: 177 us; the launch traced here: 174 us
  starting transfers between devices  57.6 us (33%)
  waiting for transfers between devices  51.3 us (29%)
  Pallas kernels  47.9 us (27%)
  blocking collectives  14 us (8%)
  local copies, waits for them, and re-layouts  1.87 us (1%)
    pallas_call x9, Pallas kernels, call(): pl.pallas_call(functools.partial(streamed, setup, kinds_in, kinds_out), i...  43.5 us
    all_to_all x2, starting transfers between devices, owned(): return lax.all_to_all(rows.reshape(count, 2, GS), CTX, 0, 0).reshape(L, GS)  20.1 us
    all_to_all x2, starting transfers between devices, carried(): given = lax.all_to_all(summed.reshape(count, 2, GS), CTX, 0, 0)  16.6 us
    all_to_all x2, waiting for transfers between devices, owned(): return lax.all_to_all(rows.reshape(count, 2, GS), CTX, 0, 0).reshape(L, GS)  14.3 us
    all_to_all x2, waiting for transfers between devices, carried(): given = lax.all_to_all(summed.reshape(count, 2, GS), CTX, 0, 0)  11.6 us
    all_to_all x1, blocking collectives, local(): lax.all_to_all(summed_copies(everyone, (feature_grad,), 'add_over_z'), YX...  11.5 us
    ppermute x2, waiting for transfers between devices, shifted(): return lax.ppermute(value, CTX, pairs)  9.85 us
    all_to_all x1, waiting for transfers between devices, local(): everyone = lax.all_to_all(owned_rows, 'z', 0, 0)  9.27 us
  transfers between devices with their start and end apart: 8, of which 7 were waited for; matrix products, arithmetic and copies ran while one was open for 0% of the time, Pallas kernels for 19%

profile of v6, /device:TPU:6, one launch (start us, length us, event | category | flops | bytes accessed | tf_op | source)
XLA Modules:
  0.0 173.5 jit_solution(7270822805618200171)
XLA Ops:
  0.6 0.0 copy-start.1
  0.6 0.9 slice.4
  1.6 3.8 %collective-permute-start = (bf16[3,8,2048]{2,1,0:T(8,128)(2,1)S(1)}, bf16[3,8,2048]{2,1,0:T(8,128)(2,1)S(1)}, u32[]{:S(2)}, u32[]{:S(2)}) collective-permute-start(bf16[3,8,2048]{2,1,0:T(8,128)(2,1)S(1)} %slice.4), channel_id=1, source_target_pairs={{0,2},{2,4},{4,6},{6,8},{8,10},{10,12},{12,14},{14,16},{16,18},{18... | collective-permute-start | bytes 294920 | tf_op jit(solution)/shard_map/ppermute | solution.py:454
  5.4 0.7 exponential_bitcast_fusion
  6.1 0.1 copy.16
  6.2 9.9 %collective-permute-done.refs_2_.refs_4_.refs_7_.refs_10_ = bf16[3,8,2048]{2,1,0:T(8,128)(2,1)S(1)} collective-permute-done((bf16[3,8,2048]{2,1,0:T(8,128)(2,1)S(1)}, bf16[3,8,2048]{2,1,0:T(8,128)(2,1)S(1)}, u32[]{:S(2)}, u32[]{:S(2)}) %collective-permute-start) | collective-permute-done | bytes 98336 | tf_op jit(solution)/shard_map/ppermute | solution.py:454
  16.0 0.1 broadcast_in_dim.22.refs_0_.refs_5_.refs_1_
  16.1 4.0 %ends_kernel.1 = (f32[128,2048]{1,0:T(8,128)}, f32[128,2048]{1,0:T(8,128)}, f32[16,8,128]{2,1,0:T(8,128)}) custom-call(f32[16,8,128]{2,1,0:T(8,128)S(1)} %broadcast_in_dim.22.refs_0_.refs_5_.refs_1_, bf16[3,128,2048]{2,1,0:T(8,128)(2,1)} %bitcast.48, bf16[3,8,2048]{2,1,0:T(8,128)(2,1)S(1)} %collective-permute-done.refs_2_.refs_4_.refs_7_.refs_10_, ...), custom_call_target="tpu_custom_call" | custom-call | tf_op jit(solution)/shard_map/ends_kernel/pallas_call | solution.py:472
  20.1 12.1 %all-to-all-start = ((f32[64,2,128]{2,1,0:T(2,128)}), f32[64,2,128]{2,1,0:T(2,128)S(1)}, u32[]{:S(2)}, u32[]{:S(2)}) async-start(f32[64,2,128]{2,1,0:T(2,128)} %bitcast.9), calls=%async_computation | async-start | bytes 131072 | tf_op jit(solution)/shard_map/all_to_all | solution.py:500
  32.2 0.1 copy.17.refs_5_.refs_2_
  32.2 0.0 copy-done.1
  32.2 0.0 copy-start.2
  32.2 0.0 copy-start.4
  32.2 3.4 %query_kernel.1 = (f32[128,2048]{1,0:T(8,128)}, f32[16,8,128]{2,1,0:T(8,128)S(1)}) custom-call(f32[16,8,128]{2,1,0:T(8,128)S(1)} %broadcast_in_dim.22.refs_0_.refs_5_.refs_1_, f32[128,2048]{1,0:T(8,128)} %get-tuple-element.30.refs_1_.refs_2_.refs_5_.refs_7_, f32[128,2048]{1,0:T(8,128)} %get-tuple-element.31.refs_2_.refs_3_.refs_6_.refs_8_, ...), custom_call_target="tpu_custom_call" | custom-call | flops 1000000000 | bytes 6000000 | tf_op jit(solution)/shard_map/query_kernel/pallas_call | solution.py:472
  35.7 9.4 %all-to-all-done = f32[64,2,128]{2,1,0:T(2,128)S(1)} async-done(((f32[64,2,128]{2,1,0:T(2,128)}), f32[64,2,128]{2,1,0:T(2,128)S(1)}, u32[]{:S(2)}, u32[]{:S(2)}) %all-to-all-start) | async-done | bytes 65568 | tf_op jit(solution)/shard_map/all_to_all | solution.py:500
  45.1 1.5 carry_on.1
  46.6 6.4 %all-to-all-start.1 = ((f32[64,2,128]{2,1,0:T(2,128)}), f32[64,2,128]{2,1,0:T(2,128)S(1)}, u32[]{:S(2)}, u32[]{:S(2)}) async-start(f32[64,2,128]{2,1,0:T(2,128)} %bitcast.11), calls=%async_computation.1 | async-start | bytes 131072 | tf_op jit(solution)/shard_map/all_to_all | solution.py:511
  52.9 0.0 copy-done.2
  52.9 0.0 copy-done.4
  52.9 0.0 copy-start
  53.0 0.0 copy-start.3
  53.0 5.7 %states_kernel.1.refs_1_ = f32[128,2048]{1,0:T(8,128)} custom-call(f32[16,8,128]{2,1,0:T(8,128)S(1)} %broadcast_in_dim.22.refs_0_.refs_5_.refs_1_, f32[128,2048]{1,0:T(8,128)} %get-tuple-element.30.refs_1_.refs_2_.refs_5_.refs_7_, f32[128,2048]{1,0:T(8,128)} %get-tuple-element.31.refs_2_.refs_3_.refs_6_.refs_8_, f32[8,2048]{1,0:T(8,128)S(1)} %copy-done.2, ...), custom_call_target="tpu_custom_call" | custom-call | flops 4000000000 | bytes 4000000 | tf_op jit(solution)/shard_map/states_kernel/pallas_call | solution.py:472
  58.7 7.1 %all-to-all-done.1 = f32[64,2,128]{2,1,0:T(2,128)S(1)} async-done(((f32[64,2,128]{2,1,0:T(2,128)}), f32[64,2,128]{2,1,0:T(2,128)S(1)}, u32[]{:S(2)}, u32[]{:S(2)}) %all-to-all-start.1) | async-done | bytes 65568 | tf_op jit(solution)/shard_map/all_to_all | solution.py:511
  65.9 0.0 copy-done
  65.9 0.0 copy-done.3
  65.9 3.0 %branch_kernel.1 = (f32[128,2048]{1,0:T(8,128)}, f32[8,128]{1,0:T(8,128)S(1)}) custom-call(f32[128,2048]{1,0:T(8,128)} %get-tuple-element.32.refs_0_.refs_1_.refs_4_, f32[128,2048]{1,0:T(8,128)} %states_kernel.1.refs_1_, bf16[128,2048]{1,0:T(8,128)(2,1)S(1)} %bitcast.29, f32[1,2048]{1,0:T(1,128)S(1)} %bitcast.41, f32[16,8,128]{2,1,0:T(8,128)S(1)} %bitcast.37, ...), custom_call_target="tpu_custom_call" | custom-call | tf_op jit(solution)/shard_map/branch_kernel/pallas_call | solution.py:472
  68.9 2.5 %psum.7.refs_0_.refs_12_ = f32[8,128]{1,0:T(8,128)S(1)} all-reduce(f32[8,128]{1,0:T(8,128)S(1)} %get-tuple-element.35), channel_id=1, replica_groups=mesh['y'=4,'x'=4,'z'=16,'c'=2] {'c'}, use_global_device_ids=true, to_apply=%region_0.0 | all-reduce | flops 1024 | bytes 8192 | tf_op jit(solution)/shard_map/psum | solution.py:539
  71.4 3.1 %gate_kernel.1 = (f32[128,2048]{1,0:T(8,128)}, f32[16,8,128]{2,1,0:T(8,128)}, f32[2,8,2048]{2,1,0:T(8,128)S(1)}) custom-call(f32[8,128]{1,0:T(8,128)S(1)} %psum.7.refs_0_.refs_12_, f32[128,2048]{1,0:T(8,128)} %get-tuple-element.32.refs_0_.refs_1_.refs_4_, f32[128,2048]{1,0:T(8,128)} %get-tuple-element.36.refs_2_.refs_7_.refs_1_, ...), custom_call_target="tpu_custom_call" | custom-call | tf_op jit(solution)/shard_map/gate_kernel/pallas_call | solution.py:472
  74.5 8.0 %all-to-all-start.2 = ((f32[64,2,128]{2,1,0:T(2,128)}), f32[64,2,128]{2,1,0:T(2,128)S(1)}, u32[]{:S(2)}, u32[]{:S(2)}) async-start(f32[64,2,128]{2,1,0:T(2,128)} %bitcast.14), calls=%async_computation.2 | async-start | bytes 131072 | tf_op jit(solution)/shard_map/all_to_all | solution.py:500
  82.6 8.3 %adjoint_kernel.1 = (f32[128,2048]{1,0:T(8,128)}, f32[16,8,128]{2,1,0:T(8,128)S(1)}, f32[16,8,128]{2,1,0:T(8,128)S(1)}, f32[16,8,128]{2,1,0:T(8,128)S(1)}, f32[1,2048]{1,0:T(1,128)S(1)}, /*index=5*/f32[5,8,2048]{2,1,0:T(8,128)}) custom-call(f32[16,8,128]{2,1,0:T(8,128)S(1)} %broadcast_in_dim.22.refs_0_.refs_5_.refs_1_, ...), custom_call_target="tpu_custom_call" | custom-call | flops 6000000000 | bytes 16000000 | tf_op jit(solution)/shard_map/adjoint_kernel/pallas_call | solution.py:472
  90.9 4.9 %all-to-all-done.2 = f32[64,2,128]{2,1,0:T(2,128)S(1)} async-done(((f32[64,2,128]{2,1,0:T(2,128)}), f32[64,2,128]{2,1,0:T(2,128)S(1)}, u32[]{:S(2)}, u32[]{:S(2)}) %all-to-all-start.2) | async-done | bytes 65568 | tf_op jit(solution)/shard_map/all_to_all | solution.py:500
  95.8 1.5 carry_back.1
  97.3 10.2 %all-to-all-start.3 = ((f32[64,2,128]{2,1,0:T(2,128)}), f32[64,2,128]{2,1,0:T(2,128)S(1)}, u32[]{:S(2)}, u32[]{:S(2)}) async-start(f32[64,2,128]{2,1,0:T(2,128)} %bitcast.16), calls=%async_computation.3 | async-start | bytes 131072 | tf_op jit(solution)/shard_map/all_to_all | solution.py:511
  107.5 4.9 %collective-permute-start.1 = (f32[5,8,2048]{2,1,0:T(8,128)}, f32[5,8,2048]{2,1,0:T(8,128)S(1)}, u32[]{:S(2)}, u32[]{:S(2)}) collective-permute-start(f32[5,8,2048]{2,1,0:T(8,128)} %get-tuple-element.42), channel_id=1, source_target_pairs={{2,0},{4,2},{6,4},{8,6},{10,8},{12,10},{14,12},{16,14},{18,16},{20... | collective-permute-start | bytes 983048 | tf_op jit(solution)/shard_map/ppermute | solution.py:454
  112.4 3.6 %outs_kernel.1.refs_11_ = f32[16,32,128]{2,1,0:T(8,128)S(1)} custom-call(f32[8,128]{1,0:T(8,128)S(1)} %psum.7.refs_0_.refs_12_, f32[128,2048]{1,0:T(8,128)} %get-tuple-element.36.refs_2_.refs_7_.refs_1_, bf16[128,2048]{1,0:T(8,128)(2,1)} %bitcast.27, f32[1,2048]{1,0:T(1,128)S(1)} %bitcast.43, f32[16,8,128]{2,1,0:T(8,128)S(1)} %get-tuple-element.46.refs_4_, ...), custom_call_target="tpu_custom_call" | custom-call | flops 1000000000 | bytes 4000000 | tf_op jit(solution)/shard_map/outs_kernel/pallas_call | solution.py:472
  116.0 4.4 %all-to-all-done.3 = f32[64,2,128]{2,1,0:T(2,128)S(1)} async-done(((f32[64,2,128]{2,1,0:T(2,128)}), f32[64,2,128]{2,1,0:T(2,128)S(1)}, u32[]{:S(2)}, u32[]{:S(2)}) %all-to-all-start.3) | async-done | bytes 65568 | tf_op jit(solution)/shard_map/all_to_all | solution.py:511
  120.5 5.2 %sums_kernel.1 = f32[16,32,128]{2,1,0:T(8,128)} custom-call(f32[16,8,128]{2,1,0:T(8,128)S(1)} %bitcast.35, f32[16,8,128]{2,1,0:T(8,128)S(1)} %broadcast_in_dim.22.refs_0_.refs_5_.refs_1_, f32[16,1,128]{2,1,0:T(1,128)S(1)} %copy.17.refs_5_.refs_2_, f32[8,2048]{1,0:T(8,128)S(1)} %copy-done.2, f32[16,8,128]{2,1,0:T(8,128)S(1)} %get-tuple-element.40.refs_0_.refs_4_, ...), custom_call_target="tpu_custom_call" | custom-call | tf_op jit(solution)/shard_map/sums_kernel/pallas_call | solution.py:472
  125.7 7.7 %all-to-all-start.4 = ((f32[16,32,128]{2,1,0:T(8,128)}), f32[16,32,128]{2,1,0:T(8,128)S(1)}, u32[]{:S(2)}, u32[]{:S(2)}) async-start(f32[16,32,128]{2,1,0:T(8,128)} %sums_kernel.1), calls=%async_computation.4 | async-start | bytes 524288 | tf_op jit(solution)/shard_map/all_to_all | solution.py:589
  133.4 0.0 collective-permute-done.1.refs_10_.refs_0_
  133.4 6.3 %all-to-all-done.4.parts = f32[16,32,128]{2,1,0:T(8,128)S(1)} async-done(((f32[16,32,128]{2,1,0:T(8,128)}), f32[16,32,128]{2,1,0:T(8,128)S(1)}, u32[]{:S(2)}, u32[]{:S(2)}) %all-to-all-start.4) | async-done | bytes 262176 | tf_op jit(solution)/shard_map/all_to_all | solution.py:589
  139.7 0.7 add_over_yx.1
  140.4 4.5 %all-to-all-start.5 = ((f32[16,32,128]{2,1,0:T(8,128)}), f32[16,32,128]{2,1,0:T(8,128)S(1)}, u32[]{:S(2)}, u32[]{:S(2)}) async-start(f32[16,32,128]{2,1,0:T(8,128)} %add_over_yx.1), calls=%async_computation.5 | async-start | bytes 524288 | tf_op jit(solution)/shard_map/all_to_all | solution.py:590
  145.0 7.0 %finish_kernel.1 = (bf16[3,128,2048]{2,1,0:T(8,128)(2,1)}, bf16[128,2048]{1,0:T(8,128)(2,1)}) custom-call(f32[8,16]{1,0:T(8,128)S(1)} %get-tuple-element.54.rate.refs_0_, f32[16,8,128]{2,1,0:T(8,128)S(1)} %bitcast.36, f32[16,1,128]{2,1,0:T(1,128)S(1)} %copy.17.refs_5_.refs_2_, f32[128,2048]{1,0:T(8,128)} %get-tuple-element.41.refs_3_.refs_6_, ...), custom_call_target="tpu_custom_call" | custom-call | flops 1000000000 | bytes 12000000 | tf_op jit(solution)/shard_map/finish_kernel/pallas_call | solution.py:472
  151.9 9.3 %all-to-all-done.5.parts = f32[16,32,128]{2,1,0:T(8,128)S(1)} async-done(((f32[16,32,128]{2,1,0:T(8,128)}), f32[16,32,128]{2,1,0:T(8,128)S(1)}, u32[]{:S(2)}, u32[]{:S(2)}) %all-to-all-start.5) | async-done | bytes 262176 | tf_op jit(solution)/shard_map/all_to_all | solution.py:590
  161.2 11.5 %all_to_all.35.pack = f32[16,32,128]{2,1,0:T(8,128)S(1)} all-to-all(f32[16,32,128]{2,1,0:T(8,128)S(1)} %add_over_z.1), channel_id=1, replica_groups=mesh['y'=4,'x'=4,'z'=16,'c'=2] {'y','x'}, dimensions={0} | all-to-all | bytes 524288 | tf_op jit(solution)/shard_map/all_to_all | solution.py:591
  172.8 0.7 unpack.1
  (2 shorter events, 0.0 us)
Async XLA Ops:
  0.6 31.6 %copy-start.1 = (f32[7,3,2048]{2,0,1:T(8,128)S(1)}, f32[7,3,2048]{2,0,1:T(8,128)}, u32[]{:S(2)}) copy-start(f32[7,3,2048]{2,0,1:T(8,128)} %param.8) | copy-start | bytes 516100
  1.6 14.4 %collective-permute-start = (bf16[3,8,2048]{2,1,0:T(8,128)(2,1)S(1)}, bf16[3,8,2048]{2,1,0:T(8,128)(2,1)S(1)}, u32[]{:S(2)}, u32[]{:S(2)}) collective-permute-start(bf16[3,8,2048]{2,1,0:T(8,128)(2,1)S(1)} %slice.4), channel_id=1, source_target_pairs={{0,2},{2,4},{4,6},{6,8},{8,10},{10,12},{12,14},{14,16},{16,18},{18... | collective-permute-start | bytes 294920 | tf_op jit(solution)/shard_map/ppermute | solution.py:454
  20.1 25.0 %all-to-all-start = ((f32[64,2,128]{2,1,0:T(2,128)}), f32[64,2,128]{2,1,0:T(2,128)S(1)}, u32[]{:S(2)}, u32[]{:S(2)}) async-start(f32[64,2,128]{2,1,0:T(2,128)} %bitcast.9), calls=%async_computation | async-start | bytes 131072 | tf_op jit(solution)/shard_map/all_to_all | solution.py:500
  32.2 20.7 %copy-start.2 = (f32[8,2048]{1,0:T(8,128)S(1)}, f32[8,2048]{1,0:T(8,128)}, u32[]{:S(2)}) copy-start(f32[8,2048]{1,0:T(8,128)} %refs_3_.3) | copy-start | bytes 196612
  32.2 20.7 %copy-start.4 = (f32[2048]{0:T(1024)S(1)}, f32[2048]{0:T(1024)}, u32[]{:S(2)}) copy-start(f32[2048]{0:T(1024)} %param.11) | copy-start | bytes 24580
  46.6 19.3 %all-to-all-start.1 = ((f32[64,2,128]{2,1,0:T(2,128)}), f32[64,2,128]{2,1,0:T(2,128)S(1)}, u32[]{:S(2)}, u32[]{:S(2)}) async-start(f32[64,2,128]{2,1,0:T(2,128)} %bitcast.11), calls=%async_computation.1 | async-start | bytes 131072 | tf_op jit(solution)/shard_map/all_to_all | solution.py:511
  52.9 12.9 %copy-start = (bf16[1,128,2048]{2,1,0:T(8,128)(2,1)S(1)}, bf16[1,128,2048]{2,1,0:T(8,128)(2,1)}, u32[]{:S(2)}) copy-start(bf16[1,128,2048]{2,1,0:T(8,128)(2,1)} %param.13) | copy-start | bytes 1572868
  53.0 12.9 %copy-start.3 = (f32[2048]{0:T(1024)S(1)}, f32[2048]{0:T(1024)}, u32[]{:S(2)}) copy-start(f32[2048]{0:T(1024)} %param.12) | copy-start | bytes 24580
  74.5 21.3 %all-to-all-start.2 = ((f32[64,2,128]{2,1,0:T(2,128)}), f32[64,2,128]{2,1,0:T(2,128)S(1)}, u32[]{:S(2)}, u32[]{:S(2)}) async-start(f32[64,2,128]{2,1,0:T(2,128)} %bitcast.14), calls=%async_computation.2 | async-start | bytes 131072 | tf_op jit(solution)/shard_map/all_to_all | solution.py:500
  97.3 23.2 %all-to-all-start.3 = ((f32[64,2,128]{2,1,0:T(2,128)}), f32[64,2,128]{2,1,0:T(2,128)S(1)}, u32[]{:S(2)}, u32[]{:S(2)}) async-start(f32[64,2,128]{2,1,0:T(2,128)} %bitcast.16), calls=%async_computation.3 | async-start | bytes 131072 | tf_op jit(solution)/shard_map/all_to_all | solution.py:511
  107.5 25.8 %collective-permute-start.1 = (f32[5,8,2048]{2,1,0:T(8,128)}, f32[5,8,2048]{2,1,0:T(8,128)S(1)}, u32[]{:S(2)}, u32[]{:S(2)}) collective-permute-start(f32[5,8,2048]{2,1,0:T(8,128)} %get-tuple-element.42), channel_id=1, source_target_pairs={{2,0},{4,2},{6,4},{8,6},{10,8},{12,10},{14,12},{16,14},{18,16},{20... | collective-permute-start | bytes 983048 | tf_op jit(solution)/shard_map/ppermute | solution.py:454
  125.7 14.0 %all-to-all-start.4 = ((f32[16,32,128]{2,1,0:T(8,128)}), f32[16,32,128]{2,1,0:T(8,128)S(1)}, u32[]{:S(2)}, u32[]{:S(2)}) async-start(f32[16,32,128]{2,1,0:T(8,128)} %sums_kernel.1), calls=%async_computation.4 | async-start | bytes 524288 | tf_op jit(solution)/shard_map/all_to_all | solution.py:589
  140.4 20.8 %all-to-all-start.5 = ((f32[16,32,128]{2,1,0:T(8,128)}), f32[16,32,128]{2,1,0:T(8,128)S(1)}, u32[]{:S(2)}, u32[]{:S(2)}) async-start(f32[16,32,128]{2,1,0:T(8,128)} %add_over_yx.1), calls=%async_computation.5 | async-start | bytes 524288 | tf_op jit(solution)/shard_map/all_to_all | solution.py:590

commit v7 on v6

--- a/solution.py
+++ b/solution.py
@@ -250,7 +250,12 @@
     keep = (lag >= 0) & (row % 2 == col % 2)
     own = jnp.where(row % 2 == 0, low, high)
     decay = jnp.where(keep, jnp.exp(-(own * L) * jnp.maximum(lag, 0).astype(F32)), 0.0)
-    refs[-1][...] = jnp.dot(decay, rows[...], precision=HIGHEST, preferred_element_type=F32)
+    high = decay.astype(BF16)
+    low = (decay - high.astype(F32)).astype(BF16)
+    both = split(rows[...])
+    left = jnp.concatenate([high, high, low], axis=1)
+    right = jnp.concatenate([both, both[0:L, :]], axis=0)
+    refs[-1][...] = jnp.dot(left, right, preferred_element_type=F32)
 
 
 def branch_kernel(q, bl, cot, gain, state_in, by_lane, weight, br_o, stats_o, acc):

time: 177 us -> 177 us (level)
  no operation moved by 1% of the time
where the time goes in v7:
time: 177 us; the launch traced here: 173 us
  starting transfers between devices  57.6 us (33%)
  waiting for transfers between devices  51.3 us (29%)
  Pallas kernels  47.8 us (27%)
  blocking collectives  14.1 us (8%)
  local copies, waits for them, and re-layouts  1.87 us (1%)
    pallas_call x9, Pallas kernels, call(): pl.pallas_call(functools.partial(streamed, setup, kinds_in, kinds_out), i...  43.5 us
    all_to_all x2, starting transfers between devices, owned(): return lax.all_to_all(rows.reshape(count, 2, GS), CTX, 0, 0).reshape(L, GS)  20.1 us
    all_to_all x2, starting transfers between devices, carried(): given = lax.all_to_all(summed.reshape(count, 2, GS), CTX, 0, 0)  16.6 us
    all_to_all x2, waiting for transfers between devices, owned(): return lax.all_to_all(rows.reshape(count, 2, GS), CTX, 0, 0).reshape(L, GS)  14.3 us
    all_to_all x1, blocking collectives, local(): lax.all_to_all(summed_copies(everyone, (feature_grad,), 'add_over_z'), YX...  11.6 us
    all_to_all x2, waiting for transfers between devices, carried(): given = lax.all_to_all(summed.reshape(count, 2, GS), CTX, 0, 0)  11.6 us
    ppermute x2, waiting for transfers between devices, shifted(): return lax.ppermute(value, CTX, pairs)  9.85 us
    all_to_all x1, waiting for transfers between devices, local(): everyone = lax.all_to_all(owned_rows, 'z', 0, 0)  9.21 us
  transfers between devices with their start and end apart: 8, of which 7 were waited for; matrix products, arithmetic and copies ran while one was open for 0% of the time, Pallas kernels for 19%

profile of v7, /device:TPU:6, one launch (start us, length us, event | category | flops | bytes accessed | tf_op | source)
XLA Modules:
  0.0 173.4 jit_solution(9486070898847657751)
XLA Ops:
  0.6 0.0 copy-start.1
  0.6 0.9 slice.4
  1.6 3.8 %collective-permute-start = (bf16[3,8,2048]{2,1,0:T(8,128)(2,1)S(1)}, bf16[3,8,2048]{2,1,0:T(8,128)(2,1)S(1)}, u32[]{:S(2)}, u32[]{:S(2)}) collective-permute-start(bf16[3,8,2048]{2,1,0:T(8,128)(2,1)S(1)} %slice.4), channel_id=1, source_target_pairs={{0,2},{2,4},{4,6},{6,8},{8,10},{10,12},{12,14},{14,16},{16,18},{18... | collective-permute-start | bytes 294920 | tf_op jit(solution)/shard_map/ppermute | solution.py:459
  5.4 0.7 exponential_bitcast_fusion
  6.1 0.1 copy.16
  6.2 9.9 %collective-permute-done.refs_2_.refs_4_.refs_7_.refs_10_ = bf16[3,8,2048]{2,1,0:T(8,128)(2,1)S(1)} collective-permute-done((bf16[3,8,2048]{2,1,0:T(8,128)(2,1)S(1)}, bf16[3,8,2048]{2,1,0:T(8,128)(2,1)S(1)}, u32[]{:S(2)}, u32[]{:S(2)}) %collective-permute-start) | collective-permute-done | bytes 98336 | tf_op jit(solution)/shard_map/ppermute | solution.py:459
  16.0 0.1 broadcast_in_dim.22.refs_0_.refs_5_.refs_1_
  16.1 4.0 %ends_kernel.1 = (f32[128,2048]{1,0:T(8,128)}, f32[128,2048]{1,0:T(8,128)}, f32[16,8,128]{2,1,0:T(8,128)}) custom-call(f32[16,8,128]{2,1,0:T(8,128)S(1)} %broadcast_in_dim.22.refs_0_.refs_5_.refs_1_, bf16[3,128,2048]{2,1,0:T(8,128)(2,1)} %bitcast.48, bf16[3,8,2048]{2,1,0:T(8,128)(2,1)S(1)} %collective-permute-done.refs_2_.refs_4_.refs_7_.refs_10_, ...), custom_call_target="tpu_custom_call" | custom-call | tf_op jit(solution)/shard_map/ends_kernel/pallas_call | solution.py:477
  20.1 12.1 %all-to-all-start = ((f32[64,2,128]{2,1,0:T(2,128)}), f32[64,2,128]{2,1,0:T(2,128)S(1)}, u32[]{:S(2)}, u32[]{:S(2)}) async-start(f32[64,2,128]{2,1,0:T(2,128)} %bitcast.9), calls=%async_computation | async-start | bytes 131072 | tf_op jit(solution)/shard_map/all_to_all | solution.py:505
  32.2 0.1 copy.17.refs_5_.refs_2_
  32.2 0.0 copy-done.1
  32.2 0.0 copy-start.2
  32.2 0.0 copy-start.4
  32.2 3.4 %query_kernel.1 = (f32[128,2048]{1,0:T(8,128)}, f32[16,8,128]{2,1,0:T(8,128)S(1)}) custom-call(f32[16,8,128]{2,1,0:T(8,128)S(1)} %broadcast_in_dim.22.refs_0_.refs_5_.refs_1_, f32[128,2048]{1,0:T(8,128)} %get-tuple-element.30.refs_1_.refs_2_.refs_5_.refs_7_, f32[128,2048]{1,0:T(8,128)} %get-tuple-element.31.refs_2_.refs_3_.refs_6_.refs_8_, ...), custom_call_target="tpu_custom_call" | custom-call | flops 1000000000 | bytes 6000000 | tf_op jit(solution)/shard_map/query_kernel/pallas_call | solution.py:477
  35.7 9.4 %all-to-all-done = f32[64,2,128]{2,1,0:T(2,128)S(1)} async-done(((f32[64,2,128]{2,1,0:T(2,128)}), f32[64,2,128]{2,1,0:T(2,128)S(1)}, u32[]{:S(2)}, u32[]{:S(2)}) %all-to-all-start) | async-done | bytes 65568 | tf_op jit(solution)/shard_map/all_to_all | solution.py:505
  45.1 1.4 carry_on.1
  46.5 6.4 %all-to-all-start.1 = ((f32[64,2,128]{2,1,0:T(2,128)}), f32[64,2,128]{2,1,0:T(2,128)S(1)}, u32[]{:S(2)}, u32[]{:S(2)}) async-start(f32[64,2,128]{2,1,0:T(2,128)} %bitcast.11), calls=%async_computation.1 | async-start | bytes 131072 | tf_op jit(solution)/shard_map/all_to_all | solution.py:516
  52.9 0.0 copy-done.2
  52.9 0.0 copy-done.4
  52.9 0.0 copy-start
  52.9 0.0 copy-start.3
  52.9 5.7 %states_kernel.1.refs_1_ = f32[128,2048]{1,0:T(8,128)} custom-call(f32[16,8,128]{2,1,0:T(8,128)S(1)} %broadcast_in_dim.22.refs_0_.refs_5_.refs_1_, f32[128,2048]{1,0:T(8,128)} %get-tuple-element.30.refs_1_.refs_2_.refs_5_.refs_7_, f32[128,2048]{1,0:T(8,128)} %get-tuple-element.31.refs_2_.refs_3_.refs_6_.refs_8_, f32[8,2048]{1,0:T(8,128)S(1)} %copy-done.2, ...), custom_call_target="tpu_custom_call" | custom-call | flops 4000000000 | bytes 4000000 | tf_op jit(solution)/shard_map/states_kernel/pallas_call | solution.py:477
  58.7 7.1 %all-to-all-done.1 = f32[64,2,128]{2,1,0:T(2,128)S(1)} async-done(((f32[64,2,128]{2,1,0:T(2,128)}), f32[64,2,128]{2,1,0:T(2,128)S(1)}, u32[]{:S(2)}, u32[]{:S(2)}) %all-to-all-start.1) | async-done | bytes 65568 | tf_op jit(solution)/shard_map/all_to_all | solution.py:516
  65.8 0.0 copy-done
  65.8 0.0 copy-done.3
  65.8 3.0 %branch_kernel.1 = (f32[128,2048]{1,0:T(8,128)}, f32[8,128]{1,0:T(8,128)S(1)}) custom-call(f32[128,2048]{1,0:T(8,128)} %get-tuple-element.32.refs_0_.refs_1_.refs_4_, f32[128,2048]{1,0:T(8,128)} %states_kernel.1.refs_1_, bf16[128,2048]{1,0:T(8,128)(2,1)S(1)} %bitcast.29, f32[1,2048]{1,0:T(1,128)S(1)} %bitcast.41, f32[16,8,128]{2,1,0:T(8,128)S(1)} %bitcast.37, ...), custom_call_target="tpu_custom_call" | custom-call | tf_op jit(solution)/shard_map/branch_kernel/pallas_call | solution.py:477
  68.9 2.5 %psum.7.refs_0_.refs_12_ = f32[8,128]{1,0:T(8,128)S(1)} all-reduce(f32[8,128]{1,0:T(8,128)S(1)} %get-tuple-element.35), channel_id=1, replica_groups=mesh['y'=4,'x'=4,'z'=16,'c'=2] {'c'}, use_global_device_ids=true, to_apply=%region_0.0 | all-reduce | flops 1024 | bytes 8192 | tf_op jit(solution)/shard_map/psum | solution.py:544
  71.3 3.1 %gate_kernel.1 = (f32[128,2048]{1,0:T(8,128)}, f32[16,8,128]{2,1,0:T(8,128)}, f32[2,8,2048]{2,1,0:T(8,128)S(1)}) custom-call(f32[8,128]{1,0:T(8,128)S(1)} %psum.7.refs_0_.refs_12_, f32[128,2048]{1,0:T(8,128)} %get-tuple-element.32.refs_0_.refs_1_.refs_4_, f32[128,2048]{1,0:T(8,128)} %get-tuple-element.36.refs_2_.refs_7_.refs_1_, ...), custom_call_target="tpu_custom_call" | custom-call | tf_op jit(solution)/shard_map/gate_kernel/pallas_call | solution.py:477
  74.5 8.0 %all-to-all-start.2 = ((f32[64,2,128]{2,1,0:T(2,128)}), f32[64,2,128]{2,1,0:T(2,128)S(1)}, u32[]{:S(2)}, u32[]{:S(2)}) async-start(f32[64,2,128]{2,1,0:T(2,128)} %bitcast.14), calls=%async_computation.2 | async-start | bytes 131072 | tf_op jit(solution)/shard_map/all_to_all | solution.py:505
  82.5 8.3 %adjoint_kernel.1 = (f32[128,2048]{1,0:T(8,128)}, f32[16,8,128]{2,1,0:T(8,128)S(1)}, f32[16,8,128]{2,1,0:T(8,128)S(1)}, f32[16,8,128]{2,1,0:T(8,128)S(1)}, f32[1,2048]{1,0:T(1,128)S(1)}, /*index=5*/f32[5,8,2048]{2,1,0:T(8,128)}) custom-call(f32[16,8,128]{2,1,0:T(8,128)S(1)} %broadcast_in_dim.22.refs_0_.refs_5_.refs_1_, ...), custom_call_target="tpu_custom_call" | custom-call | flops 6000000000 | bytes 16000000 | tf_op jit(solution)/shard_map/adjoint_kernel/pallas_call | solution.py:477
  90.9 4.9 %all-to-all-done.2 = f32[64,2,128]{2,1,0:T(2,128)S(1)} async-done(((f32[64,2,128]{2,1,0:T(2,128)}), f32[64,2,128]{2,1,0:T(2,128)S(1)}, u32[]{:S(2)}, u32[]{:S(2)}) %all-to-all-start.2) | async-done | bytes 65568 | tf_op jit(solution)/shard_map/all_to_all | solution.py:505
  95.8 1.4 carry_back.1
  97.2 10.2 %all-to-all-start.3 = ((f32[64,2,128]{2,1,0:T(2,128)}), f32[64,2,128]{2,1,0:T(2,128)S(1)}, u32[]{:S(2)}, u32[]{:S(2)}) async-start(f32[64,2,128]{2,1,0:T(2,128)} %bitcast.16), calls=%async_computation.3 | async-start | bytes 131072 | tf_op jit(solution)/shard_map/all_to_all | solution.py:516
  107.4 4.9 %collective-permute-start.1 = (f32[5,8,2048]{2,1,0:T(8,128)}, f32[5,8,2048]{2,1,0:T(8,128)S(1)}, u32[]{:S(2)}, u32[]{:S(2)}) collective-permute-start(f32[5,8,2048]{2,1,0:T(8,128)} %get-tuple-element.42), channel_id=1, source_target_pairs={{2,0},{4,2},{6,4},{8,6},{10,8},{12,10},{14,12},{16,14},{18,16},{20... | collective-permute-start | bytes 983048 | tf_op jit(solution)/shard_map/ppermute | solution.py:459
  112.3 3.6 %outs_kernel.1.refs_11_ = f32[16,32,128]{2,1,0:T(8,128)S(1)} custom-call(f32[8,128]{1,0:T(8,128)S(1)} %psum.7.refs_0_.refs_12_, f32[128,2048]{1,0:T(8,128)} %get-tuple-element.36.refs_2_.refs_7_.refs_1_, bf16[128,2048]{1,0:T(8,128)(2,1)} %bitcast.27, f32[1,2048]{1,0:T(1,128)S(1)} %bitcast.43, f32[16,8,128]{2,1,0:T(8,128)S(1)} %get-tuple-element.46.refs_4_, ...), custom_call_target="tpu_custom_call" | custom-call | flops 1000000000 | bytes 4000000 | tf_op jit(solution)/shard_map/outs_kernel/pallas_call | solution.py:477
  116.0 4.4 %all-to-all-done.3 = f32[64,2,128]{2,1,0:T(2,128)S(1)} async-done(((f32[64,2,128]{2,1,0:T(2,128)}), f32[64,2,128]{2,1,0:T(2,128)S(1)}, u32[]{:S(2)}, u32[]{:S(2)}) %all-to-all-start.3) | async-done | bytes 65568 | tf_op jit(solution)/shard_map/all_to_all | solution.py:516
  120.4 5.2 %sums_kernel.1 = f32[16,32,128]{2,1,0:T(8,128)} custom-call(f32[16,8,128]{2,1,0:T(8,128)S(1)} %bitcast.35, f32[16,8,128]{2,1,0:T(8,128)S(1)} %broadcast_in_dim.22.refs_0_.refs_5_.refs_1_, f32[16,1,128]{2,1,0:T(1,128)S(1)} %copy.17.refs_5_.refs_2_, f32[8,2048]{1,0:T(8,128)S(1)} %copy-done.2, f32[16,8,128]{2,1,0:T(8,128)S(1)} %get-tuple-element.40.refs_0_.refs_4_, ...), custom_call_target="tpu_custom_call" | custom-call | tf_op jit(solution)/shard_map/sums_kernel/pallas_call | solution.py:477
  125.6 7.6 %all-to-all-start.4 = ((f32[16,32,128]{2,1,0:T(8,128)}), f32[16,32,128]{2,1,0:T(8,128)S(1)}, u32[]{:S(2)}, u32[]{:S(2)}) async-start(f32[16,32,128]{2,1,0:T(8,128)} %sums_kernel.1), calls=%async_computation.4 | async-start | bytes 524288 | tf_op jit(solution)/shard_map/all_to_all | solution.py:594
  133.3 0.0 collective-permute-done.1.refs_10_.refs_0_
  133.3 6.3 %all-to-all-done.4.parts = f32[16,32,128]{2,1,0:T(8,128)S(1)} async-done(((f32[16,32,128]{2,1,0:T(8,128)}), f32[16,32,128]{2,1,0:T(8,128)S(1)}, u32[]{:S(2)}, u32[]{:S(2)}) %all-to-all-start.4) | async-done | bytes 262176 | tf_op jit(solution)/shard_map/all_to_all | solution.py:594
  139.6 0.7 add_over_yx.1
  140.3 4.5 %all-to-all-start.5 = ((f32[16,32,128]{2,1,0:T(8,128)}), f32[16,32,128]{2,1,0:T(8,128)S(1)}, u32[]{:S(2)}, u32[]{:S(2)}) async-start(f32[16,32,128]{2,1,0:T(8,128)} %add_over_yx.1), calls=%async_computation.5 | async-start | bytes 524288 | tf_op jit(solution)/shard_map/all_to_all | solution.py:595
  144.9 7.0 %finish_kernel.1 = (bf16[3,128,2048]{2,1,0:T(8,128)(2,1)}, bf16[128,2048]{1,0:T(8,128)(2,1)}) custom-call(f32[8,16]{1,0:T(8,128)S(1)} %get-tuple-element.54.rate.refs_0_, f32[16,8,128]{2,1,0:T(8,128)S(1)} %bitcast.36, f32[16,1,128]{2,1,0:T(1,128)S(1)} %copy.17.refs_5_.refs_2_, f32[128,2048]{1,0:T(8,128)} %get-tuple-element.41.refs_3_.refs_6_, ...), custom_call_target="tpu_custom_call" | custom-call | flops 1000000000 | bytes 12000000 | tf_op jit(solution)/shard_map/finish_kernel/pallas_call | solution.py:477
  151.8 9.2 %all-to-all-done.5.parts = f32[16,32,128]{2,1,0:T(8,128)S(1)} async-done(((f32[16,32,128]{2,1,0:T(8,128)}), f32[16,32,128]{2,1,0:T(8,128)S(1)}, u32[]{:S(2)}, u32[]{:S(2)}) %all-to-all-start.5) | async-done | bytes 262176 | tf_op jit(solution)/shard_map/all_to_all | solution.py:595
  161.1 11.6 %all_to_all.35.pack = f32[16,32,128]{2,1,0:T(8,128)S(1)} all-to-all(f32[16,32,128]{2,1,0:T(8,128)S(1)} %add_over_z.1), channel_id=1, replica_groups=mesh['y'=4,'x'=4,'z'=16,'c'=2] {'y','x'}, dimensions={0} | all-to-all | bytes 524288 | tf_op jit(solution)/shard_map/all_to_all | solution.py:596
  172.7 0.7 unpack.1
  (2 shorter events, 0.0 us)
Async XLA Ops:
  0.6 31.6 %copy-start.1 = (f32[7,3,2048]{2,0,1:T(8,128)S(1)}, f32[7,3,2048]{2,0,1:T(8,128)}, u32[]{:S(2)}) copy-start(f32[7,3,2048]{2,0,1:T(8,128)} %param.8) | copy-start | bytes 516100
  1.6 14.4 %collective-permute-start = (bf16[3,8,2048]{2,1,0:T(8,128)(2,1)S(1)}, bf16[3,8,2048]{2,1,0:T(8,128)(2,1)S(1)}, u32[]{:S(2)}, u32[]{:S(2)}) collective-permute-start(bf16[3,8,2048]{2,1,0:T(8,128)(2,1)S(1)} %slice.4), channel_id=1, source_target_pairs={{0,2},{2,4},{4,6},{6,8},{8,10},{10,12},{12,14},{14,16},{16,18},{18... | collective-permute-start | bytes 294920 | tf_op jit(solution)/shard_map/ppermute | solution.py:459
  20.1 25.0 %all-to-all-start = ((f32[64,2,128]{2,1,0:T(2,128)}), f32[64,2,128]{2,1,0:T(2,128)S(1)}, u32[]{:S(2)}, u32[]{:S(2)}) async-start(f32[64,2,128]{2,1,0:T(2,128)} %bitcast.9), calls=%async_computation | async-start | bytes 131072 | tf_op jit(solution)/shard_map/all_to_all | solution.py:505
  32.2 20.7 %copy-start.2 = (f32[8,2048]{1,0:T(8,128)S(1)}, f32[8,2048]{1,0:T(8,128)}, u32[]{:S(2)}) copy-start(f32[8,2048]{1,0:T(8,128)} %refs_3_.3) | copy-start | bytes 196612
  32.2 20.7 %copy-start.4 = (f32[2048]{0:T(1024)S(1)}, f32[2048]{0:T(1024)}, u32[]{:S(2)}) copy-start(f32[2048]{0:T(1024)} %param.11) | copy-start | bytes 24580
  46.5 19.3 %all-to-all-start.1 = ((f32[64,2,128]{2,1,0:T(2,128)}), f32[64,2,128]{2,1,0:T(2,128)S(1)}, u32[]{:S(2)}, u32[]{:S(2)}) async-start(f32[64,2,128]{2,1,0:T(2,128)} %bitcast.11), calls=%async_computation.1 | async-start | bytes 131072 | tf_op jit(solution)/shard_map/all_to_all | solution.py:516
  52.9 12.9 %copy-start = (bf16[1,128,2048]{2,1,0:T(8,128)(2,1)S(1)}, bf16[1,128,2048]{2,1,0:T(8,128)(2,1)}, u32[]{:S(2)}) copy-start(bf16[1,128,2048]{2,1,0:T(8,128)(2,1)} %param.13) | copy-start | bytes 1572868
  52.9 12.9 %copy-start.3 = (f32[2048]{0:T(1024)S(1)}, f32[2048]{0:T(1024)}, u32[]{:S(2)}) copy-start(f32[2048]{0:T(1024)} %param.12) | copy-start | bytes 24580
  74.5 21.3 %all-to-all-start.2 = ((f32[64,2,128]{2,1,0:T(2,128)}), f32[64,2,128]{2,1,0:T(2,128)S(1)}, u32[]{:S(2)}, u32[]{:S(2)}) async-start(f32[64,2,128]{2,1,0:T(2,128)} %bitcast.14), calls=%async_computation.2 | async-start | bytes 131072 | tf_op jit(solution)/shard_map/all_to_all | solution.py:505
  97.2 23.2 %all-to-all-start.3 = ((f32[64,2,128]{2,1,0:T(2,128)}), f32[64,2,128]{2,1,0:T(2,128)S(1)}, u32[]{:S(2)}, u32[]{:S(2)}) async-start(f32[64,2,128]{2,1,0:T(2,128)} %bitcast.16), calls=%async_computation.3 | async-start | bytes 131072 | tf_op jit(solution)/shard_map/all_to_all | solution.py:516
  107.4 25.8 %collective-permute-start.1 = (f32[5,8,2048]{2,1,0:T(8,128)}, f32[5,8,2048]{2,1,0:T(8,128)S(1)}, u32[]{:S(2)}, u32[]{:S(2)}) collective-permute-start(f32[5,8,2048]{2,1,0:T(8,128)} %get-tuple-element.42), channel_id=1, source_target_pairs={{2,0},{4,2},{6,4},{8,6},{10,8},{12,10},{14,12},{16,14},{18,16},{20... | collective-permute-start | bytes 983048 | tf_op jit(solution)/shard_map/ppermute | solution.py:459
  125.6 14.0 %all-to-all-start.4 = ((f32[16,32,128]{2,1,0:T(8,128)}), f32[16,32,128]{2,1,0:T(8,128)S(1)}, u32[]{:S(2)}, u32[]{:S(2)}) async-start(f32[16,32,128]{2,1,0:T(8,128)} %sums_kernel.1), calls=%async_computation.4 | async-start | bytes 524288 | tf_op jit(solution)/shard_map/all_to_all | solution.py:594
  140.3 20.7 %all-to-all-start.5 = ((f32[16,32,128]{2,1,0:T(8,128)}), f32[16,32,128]{2,1,0:T(8,128)S(1)}, u32[]{:S(2)}, u32[]{:S(2)}) async-start(f32[16,32,128]{2,1,0:T(8,128)} %add_over_yx.1), calls=%async_computation.5 | async-start | bytes 524288 | tf_op jit(solution)/shard_map/all_to_all | solution.py:595
